TPU v7x, 128 devices: a whole 4x4x4 slice. The times are simulated.
128 devices in a mesh: seq: 32 (over x_hi, z, y), row: 4 (over x_lo, core).
Axes of the slice: x: 4 (x_hi: 2, x_lo: 2; x = x_hi * 2 + x_lo), y: 4, z: 4, core: 2. Of those that a mesh axis runs over, the one named last changes fastest.
Arguments:
- activations: bfloat16 [256, 256, 1024], P('seq', 'row'), may hold values from -6 to 6
- noise_embed: bfloat16 [256, 1024], P('seq'), may hold values from -6 to 6
- frame_position: int32 [256], P('seq'), may hold values from 0 to 7, as said below
- cotangent: bfloat16 [256, 256, 1024], P('seq', 'row'), may hold values from -6 to 6
- ada_weight: bfloat16 [1024, 6144], P('row'), may hold values from -0.1875 to 0.1875
- ada_bias: bfloat16 [6144], P('row'), may hold values from -3 to 3
- qkv_weight: bfloat16 [1024, 3072], P('row'), may hold values from -0.1875 to 0.1875
- qkv_bias: bfloat16 [3072], P('row'), may hold values from -3 to 3
- out_weight: bfloat16 [1024, 1024], P('row'), may hold values from -0.75 to 0.75
- out_bias: bfloat16 [1024], P('row'), may hold values from -3 to 3
- up_weight: bfloat16 [1024, 4096], P('row'), may hold values from -0.1875 to 0.1875
- up_bias: bfloat16 [4096], P('row'), may hold values from -3 to 3
- down_weight: bfloat16 [4096, 1024], P('row'), may hold values from -0.09375 to 0.09375
- down_bias: bfloat16 [1024], P('row'), may hold values from -3 to 3
Outputs:
- layer_output: bfloat16 [256, 256, 1024], P('seq', 'row')
- input_grad: float32 [256, 256, 1024], P('seq', 'row')
- embed_grad: float32 [256, 1024], P('seq')
- ada_weight_grad: float32 [1024, 6144], P('row')
- ada_bias_grad: float32 [6144], P('row')
- qkv_weight_grad: float32 [1024, 3072], P('row')
- qkv_bias_grad: float32 [3072], P('row')
- out_weight_grad: float32 [1024, 1024], P('row')
- out_bias_grad: float32 [1024], P('row')
- up_weight_grad: float32 [1024, 4096], P('row')
- up_bias_grad: float32 [4096], P('row')
- down_weight_grad: float32 [4096, 1024], P('row')
- down_bias_grad: float32 [1024], P('row')
Inputs may be any that keep to these rules, and one draw needn't show every extreme that they name: frame_position[f] is the place of frame f in its clip: 0 where a clip begins, else one more than at frame f - 1; a clip holds 1 to 8 frames, and frames 0 to 7 form one clip.
All inputs are finite; a program needn't handle non-finite values.
Results may differ from a plain program's by a relative error of at most 0.028.
The roundings to bfloat16 on the way count: a program that leaves them out, or rounds other values in their place, can miss the bound.
Values may be sent and summed in bfloat16 or wider, within the bound.
No kernel may reach another device: no remote copies, remote signals or barrier semaphores. Data moves between devices by JAX's collectives and lax.ppermute only.
A program may use at most 320 MiB of HBM per device.

v0:
```python
import math

import jax
import jax.numpy as jnp
from jax import lax
from jax.experimental import pallas as pl
from jax.experimental.pallas import tpu as pltpu
from jax.sharding import Mesh, PartitionSpec as P

F32 = jnp.float32
BF16 = jnp.bfloat16
HD = 64
GRID = 16
FPD = 8
PR = 64
D = 1024
FF = 4096
HC = 256
TOK = 256
PREV = 7
AXES = ("xh", "z", "y", "xl", "c")
CORE, DIRECT, OTHER, FAR = 1, 2, 66, 64
MB = 1024 * 1024


def swap(value, mask):
    return lax.ppermute(value, AXES, [(i, i ^ mask) for i in range(128)])


def shift(value, steps):
    return lax.ppermute(value, AXES, [(i, (i + 4 * steps) % 128) for i in range(128)])


def after(value, *others):
    return lax.optimization_barrier((value,) + others)[0]


def nt(left, right):
    return lax.dot_general(left, right, (((1,), (1,)), ((), ())), preferred_element_type=F32)


def tn(left, right):
    return lax.dot_general(left, right, (((0,), (0,)), ((), ())), preferred_element_type=F32)


def nn(left, right):
    return jnp.dot(left, right, preferred_element_type=F32)


def norm(values):
    center = values - jnp.mean(values, axis=-1, keepdims=True)
    spread = jnp.mean(center * center, axis=-1, keepdims=True)
    rate = lax.rsqrt(spread + 1e-06)
    return center * rate, rate


def norm_back(normal, rate, grad):
    mean_grad = jnp.mean(grad, axis=-1, keepdims=True)
    mean_both = jnp.mean(grad * normal, axis=-1, keepdims=True)
    return rate * (grad - mean_grad - normal * mean_both)


def turn(values, cosine, sine):
    lanes = lax.broadcasted_iota(jnp.int32, values.shape, 1)
    other = jnp.where(
        lanes % HD < HD // 2, pltpu.roll(values, HC - HD // 2, 1), pltpu.roll(values, HD // 2, 1)
    )
    return values * cosine + other * sine


def params(mib):
    return pltpu.CompilerParams(vmem_limit_bytes=mib * MB)


def cost(flops, moved, exps=0):
    return pl.CostEstimate(flops=int(flops), bytes_accessed=int(moved), transcendentals=int(exps))


def whole(shape):
    return pl.BlockSpec(shape, lambda i, *_: (0,) * len(shape))


def columns(row, j):
    return pl.ds(pl.multiple_of((row ^ j) * HC, HC), HC)


def shape(dims, kind=BF16):
    return jax.ShapeDtypeStruct(dims, kind)


UB, QB, OB, DB, WIDE = 6144, 6656, 7168, 7296, 7424


def put(ref, start, at, value):
    cols = slice(start, start + value.shape[1])
    number = lax.broadcasted_iota(jnp.int32, (8, value.shape[1]), 0)
    ref[:, cols] = jnp.where(number == at, value, ref[:, cols])


def take(value, at):
    number = lax.broadcasted_iota(jnp.int32, value.shape, 0)
    return jnp.sum(jnp.where(number == at, value, 0.0), axis=0, keepdims=True)


def put_half(ref, start, value):
    cols = slice(start, start + value.shape[1])
    number = lax.broadcasted_iota(jnp.int32, (8, value.shape[1]), 0)
    both = jnp.concatenate([value, value], axis=0)
    ref[:, cols] = jnp.where(number // 4 == pl.program_id(0), both, ref[:, cols])


def unfold(ref, start, width):
    return jnp.concatenate([ref[i : i + 1, start : start + width] for i in range(8)], axis=1)


def prepare_kernel(row_ref, pos_ref, noise, ada, ab, qb, ob, ub, db, pack, silu, cp, sp, frames):
    row = row_ref[0]
    embed = noise[...].astype(F32)
    value = (embed / (1.0 + jnp.exp(-embed))).astype(BF16)
    own = jnp.where(
        row < 2,
        jnp.where(row == 0, value[:, :HC], value[:, HC : 2 * HC]),
        jnp.where(row == 2, value[:, 2 * HC : 3 * HC], value[:, 3 * HC :]),
    )
    silu[...] = own
    pack[:, UB:] = jnp.zeros((FPD, WIDE - UB), F32)
    for segment in range(6):
        cols = slice(segment * D, (segment + 1) * D)
        pack[:, cols] = nn(own, ada[:, cols])
    bias = pl.ds(pl.multiple_of(row * 1536, 512), 1536)
    pack[:, bias] = pack[:, bias] + ab[...].astype(F32)
    for i in range(2):
        at = 2 * row + i
        put(pack, UB, at, ub[:, i * 512 : (i + 1) * 512].astype(F32))
        put(pack, OB, at, ob[:, i * 128 : (i + 1) * 128].astype(F32))
        put(pack, DB, at, db[:, i * 128 : (i + 1) * 128].astype(F32))
    for i in range(3):
        chunk = 3 * row + i
        at = jnp.where(chunk < 4, chunk, chunk - 4)
        second = (chunk >= 4) & (chunk < 8)
        value = qb[:, i * HC : (i + 1) * HC].astype(F32)
        put(pack, QB, jnp.where(second, -1, at), value)
        put(pack, QB + HC, jnp.where(second, at, -1), value)

    def parts(dims):
        lane = lax.broadcasted_iota(jnp.int32, dims, 1)
        index = lane % (HD // 2)
        quarter, eighth = HD // 4, HD // 8
        in_frame = index < quarter
        in_row = (index >= quarter) & (index < quarter + eighth)
        offset = jnp.where(
            in_frame, index, jnp.where(in_row, index - quarter, index - quarter - eighth)
        ).astype(F32)
        length = jnp.where(in_frame, 1.0 * quarter, 1.0 * eighth)
        frequency = jnp.exp(-math.log(10000.0) * offset / length)
        sign = jnp.where(lane % HD < HD // 2, -1.0, 1.0)
        return in_frame, in_row, frequency, sign

    in_frame, in_row, frequency, sign = parts((TOK, HC))
    slot = lax.broadcasted_iota(jnp.int32, (TOK, HC), 0)
    patch = ((slot // PR) ^ row) * PR + slot % PR
    angle = jnp.where(in_row, patch // GRID, patch % GRID).astype(F32) * frequency
    cp[...] = jnp.where(in_frame, 0.0, jnp.cos(angle))
    sp[...] = jnp.where(in_frame, 0.0, jnp.sin(angle) * sign)
    in_frame, _, frequency, sign = parts((16, HC))
    slot = lax.broadcasted_iota(jnp.int32, (16, HC), 0)
    place = pos_ref[0] - PREV + (slot - FPD)
    for f in range(FPD):
        place = jnp.where(slot == f, pos_ref[f], place)
    angle = place.astype(F32) * frequency
    frames[:, :HC] = jnp.where(in_frame, jnp.cos(angle), 0.0)
    frames[:, HC:] = jnp.where(in_frame, jnp.sin(angle) * sign, 0.0)


def prepare(row, places, noise, ada, biases):
    return pl.pallas_call(
        prepare_kernel,
        out_shape=[
            shape((FPD, WIDE), F32),
            shape((FPD, HC)),
            shape((TOK, HC), F32),
            shape((TOK, HC), F32),
            shape((16, 2 * HC), F32),
        ],
        grid_spec=pltpu.PrefetchScalarGridSpec(
            num_scalar_prefetch=2,
            grid=(1,),
            in_specs=[whole((FPD, D)), whole((HC, 6 * D))]
            + [whole((1, b.shape[0])) for b in biases],
            out_specs=[
                whole((FPD, WIDE)),
                whole((FPD, HC)),
                whole((TOK, HC)),
                whole((TOK, HC)),
                whole((16, 2 * HC)),
            ],
        ),
        compiler_params=params(24),
        cost_estimate=cost(2 * 8 * HC * 6 * D, 4 * MB, 4 * TOK * HC),
        name="prepare",
    )(row, places, noise, ada, *[b[None] for b in biases])


def split_heads_kernel(row_ref, q, k, v, p0, p1, p23):
    for j, p in enumerate((p0, p1, p23.at[0], p23.at[1])):

        @pl.when(pl.program_id(0) == j)
        def _():
            p[:, :HC] = q[...]
            p[:, HC : 2 * HC] = k[...]
            p[:, 2 * HC :] = v[...]


def split_heads(row, weight):
    piece = (HC, 3 * HC)
    return pl.pallas_call(
        split_heads_kernel,
        out_shape=[shape(piece), shape(piece), shape((2,) + piece)],
        grid_spec=pltpu.PrefetchScalarGridSpec(
            num_scalar_prefetch=1,
            grid=(4,),
            in_specs=[
                pl.BlockSpec((HC, HC), lambda j, row, s=s: (0, 4 * s + (row[0] ^ j)))
                for s in range(3)
            ],
            out_specs=[whole(piece), whole(piece), whole((2,) + piece)],
        ),
        compiler_params=params(12),
        cost_estimate=cost(0, 3 * MB),
        name="split_heads",
    )(row, weight, weight, weight)


def cosines(cp, sp, frames, at):
    both = frames[pl.ds(at, 1), :]
    return cp[...] + both[:, :HC], sp[...] + both[:, HC:]


def project_kernel(own, row_ref, x0, x1, x2, x3, table, mods, w0, w1, w2, w3, cp, sp, fr, *outs):
    row = row_ref[0]
    f = pl.program_id(0)
    if own:
        h_ref, q_ref, k_ref, v_ref = outs
        first, at, angle = 0, f, f
    else:
        k_ref, v_ref, h_ref = outs
        first, at, angle = HC, f + FPD - PREV, f + FPD
    x = jnp.concatenate([r[0] for r in (x0, x1, x2, x3)], axis=0).astype(F32)
    normal, _ = norm(x)
    shift_row = mods[pl.ds(at, 1), :D]
    scale_row = mods[pl.ds(at, 1), D : 2 * D]
    hidden = (normal * (1.0 + scale_row) + shift_row).astype(BF16)
    where = (0,) if own else ()
    h_ref[where + (slice(None), slice(None))] = hidden
    low, high = table[pl.ds(row, 1), QB : QB + 2 * HC], table[pl.ds(row + 4, 1), QB : QB + HC]
    total = jnp.concatenate([low, high], axis=1)[:, first:]
    for j, w in enumerate((w0, w1, w2, w3)):
        total = total + nn(h_ref[where + (slice(None), columns(row, j))], w[:, first:])
    cosine, sine = cosines(cp, sp, fr, angle)
    if own:
        q_ref[0] = (turn(total[:, :HC], cosine, sine).astype(BF16).astype(F32) * 0.125).astype(BF16)
        total = total[:, HC:]
    k_ref[0] = turn(total[:, :HC], cosine, sine).astype(BF16)
    v_ref[0] = total[:, HC:].astype(BF16)


def project(own, row, xs, table, mods, weights, tables):
    frames = xs[0].shape[0]
    x_spec = pl.BlockSpec((1, PR, D), lambda f, *_: (f, 0, 0))
    out_spec = pl.BlockSpec((1, TOK, HC), lambda f, *_: (f, 0, 0))
    out = shape((frames, TOK, HC))
    if own:
        out_specs = [pl.BlockSpec((1, TOK, D), lambda f, *_: (f, 0, 0)), out_spec, out_spec, out_spec]
        out_shape = [shape((frames, TOK, D)), out, out, out]
        scratch = []
    else:
        out_specs = [out_spec, out_spec]
        out_shape = [out, out]
        scratch = [pltpu.VMEM((TOK, D), BF16)]
    return pl.pallas_call(
        lambda *refs: project_kernel(own, *refs),
        out_shape=out_shape,
        grid_spec=pltpu.PrefetchScalarGridSpec(
            num_scalar_prefetch=1,
            grid=(frames,),
            in_specs=[x_spec] * 4
            + [whole((FPD, WIDE)), whole(mods.shape)]
            + [whole((HC, 3 * HC))] * 4
            + [whole((TOK, HC)), whole((TOK, HC)), whole((16, 2 * HC))],
            out_specs=out_specs,
            scratch_shapes=scratch,
        ),
        compiler_params=params(20),
        cost_estimate=cost(2 * frames * TOK * D * 3 * HC, frames * TOK * D * 4 + 4 * MB),
        name="project_own" if own else "project_prev",
    )(row, *xs, table, mods, *weights, *tables)


def head_lanes():
    return lax.broadcasted_iota(jnp.int32, (TOK, HC), 1) // HD


def attend_kernel(pos_ref, q, k, v, kp, vp, o0, o1, o23, lse, qs, scores, acc, top, low):
    f = pl.program_id(0)
    place = pos_ref[f]
    lanes = head_lanes()
    query = q[0]
    for h in range(4):
        qs[pl.ds(h * TOK, TOK), :] = jnp.where(lanes == h, query, jnp.zeros_like(query))
    top[...] = jnp.full_like(top, -1e30)
    low[...] = jnp.zeros_like(low)
    acc[...] = jnp.zeros_like(acc)
    before = jnp.maximum(place - f, 0)
    start = jnp.maximum(f - place, 0)

    def score(keys, slot):
        for h in range(4):
            rows = pl.ds(h * TOK, TOK)
            s = nt(qs[rows, :], keys)
            scores[slot, rows, :] = s
            top[rows, :] = jnp.maximum(top[rows, :], jnp.maximum(s[:, :128], s[:, 128:]))

    def mix(values, slot):
        for h in range(4):
            rows = pl.ds(h * TOK, TOK)
            p = jnp.exp(scores[slot, rows, :] - jnp.concatenate([top[rows, :]] * 2, axis=1))
            low[rows, :] = low[rows, :] + (p[:, :128] + p[:, 128:])
            acc[rows, :] = acc[rows, :] + nn(p.astype(BF16), values)

    def run(step):
        def prev(i, _):
            at = PREV - before + i
            step(kp[at] if step is score else vp[at], i)
            return 0

        def own(g, _):
            step(k[g] if step is score else v[g], g - f + place)
            return 0

        lax.fori_loop(0, before, prev, 0)
        lax.fori_loop(start, f + 1, own, 0)

    run(score)
    for h in range(4):
        rows = pl.ds(h * TOK, TOK)
        top[rows, :] = jnp.broadcast_to(jnp.max(top[rows, :], axis=1, keepdims=True), (TOK, 128))
    run(mix)
    result = jnp.zeros((TOK, HC), F32)
    logs = jnp.zeros((TOK, 128), F32)
    narrow = lax.broadcasted_iota(jnp.int32, (TOK, 128), 1)
    for h in range(4):
        rows = pl.ds(h * TOK, TOK)
        total = jnp.sum(low[rows, :], axis=1, keepdims=True)
        result = jnp.where(lanes == h, acc[rows, :] / total, result)
        logs = jnp.where(narrow == h, top[rows, :] + jnp.log(total), logs)
    lse[0] = logs.T[:8]
    result = result.astype(BF16)
    o0[0] = result[:PR]
    o1[0] = result[PR : 2 * PR]
    o23[0, 0] = result[2 * PR : 3 * PR]
    o23[1, 0] = result[3 * PR :]


def attend(places, q, k, v, kp, vp):
    block = pl.BlockSpec((1, TOK, HC), lambda f, *_: (f, 0, 0))
    piece = pl.BlockSpec((1, PR, HC), lambda f, *_: (f, 0, 0))
    return pl.pallas_call(
        attend_kernel,
        out_shape=[shape((FPD, PR, HC))] * 2
        + [shape((2, FPD, PR, HC)), shape((FPD, 8, TOK), F32)],
        grid_spec=pltpu.PrefetchScalarGridSpec(
            num_scalar_prefetch=1,
            grid=(FPD,),
            in_specs=[block]
            + [whole((FPD, TOK, HC))] * 2
            + [whole((PREV, TOK, HC))] * 2,
            out_specs=[piece] * 2
            + [
                pl.BlockSpec((2, 1, PR, HC), lambda f, *_: (0, f, 0, 0)),
                pl.BlockSpec((1, 8, TOK), lambda f, *_: (f, 0, 0)),
            ],
            scratch_shapes=[
                pltpu.VMEM((4 * TOK, HC), BF16),
                pltpu.VMEM((8, 4 * TOK, TOK), F32),
                pltpu.VMEM((4 * TOK, HC), F32),
                pltpu.VMEM((4 * TOK, 128), F32),
                pltpu.VMEM((4 * TOK, 128), F32),
            ],
        ),
        compiler_params=params(58),
        cost_estimate=cost(36 * 4 * 2 * 2 * TOK**3, 6 * MB, 36 * 4 * TOK * TOK),
        name="attend",
    )(places, q, k, v, kp, vp)


def attend_back_kernel(own, pos_ref, q, k, v, g0, g1, g2, g3, o0, o1, o23, lse, *rest):
    if own:
        cp, sp, fr, before_ref, dq, dk, dv, qs, gs, ks, pl_scr, dl_scr, ds_scr, dq_acc = rest
        dk_acc, dv_acc = dk, dv
    else:
        dq, both_ref, qs, gs, ks, pl_scr, dl_scr, ds_scr, dq_acc, dk_acc, dv_acc = rest
    f = pl.program_id(0)
    place = pos_ref[f]
    lanes = head_lanes()

    @pl.when(f == 0)
    def _():
        for ref in (dk_acc, dv_acc):
            ref[...] = jnp.zeros_like(ref)

    def prelude():
        query = q[0]
        grad = jnp.concatenate([r[0] for r in (g0, g1, g2, g3)], axis=0)
        mixed = jnp.concatenate([o0[0], o1[0], o23[0, 0], o23[1, 0]], axis=0)
        for h in range(4):
            rows = pl.ds(h * TOK, TOK)
            qs[rows, :] = jnp.where(lanes == h, query, jnp.zeros_like(query))
            gs[rows, :] = jnp.where(lanes == h, grad, jnp.zeros_like(grad))
        both = grad.astype(F32) * mixed.astype(F32)
        pick = (
            lax.broadcasted_iota(jnp.int32, (8, HC), 1) // HD
            == lax.broadcasted_iota(jnp.int32, (8, HC), 0)
        ).astype(F32)
        return lax.dot_general(
            pick, both, (((1,), (1,)), ((), ())),
            preferred_element_type=F32, precision=lax.Precision.HIGHEST,
        )

    def step(delta, logs, at):
        keys, values = k[at], v[at]
        for h in range(4):
            rows = pl.ds(h * TOK, TOK)
            ks[rows, :] = jnp.where(lanes == h, keys, jnp.zeros_like(keys))
            p = jnp.exp(nt(keys, qs[rows, :]) - logs[h : h + 1])
            ds = (p * (nt(values, gs[rows, :]) - delta[h : h + 1])).astype(BF16)
            pl_scr[:, rows] = p.astype(BF16)
            dl_scr[:, rows] = ds
            ds_scr[rows, :] = ds
        dv_acc[at] = dv_acc[at] + nn(pl_scr[...], gs[...])
        dk_acc[at] = dk_acc[at] + nn(dl_scr[...], qs[...])
        dq_acc[...] = dq_acc[...] + tn(ds_scr[...], ks[...])

    def sweep(low, high):
        delta = prelude()
        logs = lse[0]
        dq_acc[...] = jnp.zeros_like(dq_acc)

        def one(at, _):
            step(delta, logs, at)
            return 0

        lax.fori_loop(low, high, one, 0)

    if own:
        sweep(jnp.maximum(f - place, 0), f + 1)
        cosine, sine = cosines(cp, sp, fr, f)
        dq[0] = turn((dq_acc[...] + before_ref[0]) * 0.125, cosine, -sine).astype(BF16)
    else:
        count = jnp.maximum(place - f, 0)

        @pl.when(count > 0)
        def _():
            sweep(PREV - count, PREV)
            dq[0] = dq_acc[...]

        @pl.when(count == 0)
        def _():
            dq[0] = jnp.zeros_like(dq_acc)

        @pl.when(f == FPD - 1)
        def _():
            both_ref[0] = dk_acc[...].astype(BF16)
            both_ref[1] = dv_acc[...].astype(BF16)


def attend_back(own, places, q, k, v, grads, mixed, lse, tables=None, before=None):
    block = pl.BlockSpec((1, TOK, HC), lambda f, *_: (f, 0, 0))
    piece = pl.BlockSpec((1, PR, HC), lambda f, *_: (f, 0, 0))
    count = FPD if own else PREV
    wide = pltpu.VMEM((4 * TOK, HC), BF16)
    tall = pltpu.VMEM((TOK, 4 * TOK), BF16)
    scratch = [wide, wide, wide, tall, tall, wide, pltpu.VMEM((TOK, HC), F32)]
    specs = []
    extra = ()
    if own:
        specs = [whole((TOK, HC)), whole((TOK, HC)), whole((16, 2 * HC)), block]
        extra = tuple(tables) + (before,)
    else:
        scratch += [pltpu.VMEM((PREV, TOK, HC), F32)] * 2
    return pl.pallas_call(
        lambda *refs: attend_back_kernel(own, *refs),
        out_shape=[shape((FPD, TOK, HC), BF16 if own else F32)]
        + ([shape((FPD, TOK, HC), F32)] * 2 if own else [shape((2, PREV, TOK, HC))]),
        grid_spec=pltpu.PrefetchScalarGridSpec(
            num_scalar_prefetch=1,
            grid=(FPD,),
            in_specs=[block]
            + [whole((count, TOK, HC))] * 2
            + [piece] * 6
            + [pl.BlockSpec((2, 1, PR, HC), lambda f, *_: (0, f, 0, 0))]
            + [pl.BlockSpec((1, 8, TOK), lambda f, *_: (f, 0, 0))]
            + specs,
            out_specs=[block]
            + ([whole((FPD, TOK, HC))] * 2 if own else [whole((2, PREV, TOK, HC))]),
            scratch_shapes=scratch,
        ),
        compiler_params=params(58),
        cost_estimate=cost(1000 if own else 12 * 4 * 5 * 2 * TOK**3, 1000 if own else 12 * MB),
        name="attend_back_own" if own else "attend_back_prev",
    )(places, q, k, v, *grads, *mixed, lse, *extra)


HALF = 4
RAW = HALF * PR


def flat(ref):
    return ref[...].reshape(RAW, ref.shape[-1])


def frames_of(value):
    return value.reshape(HALF, PR, value.shape[-1])


def segment(table, s):
    both = table[:, s * D : (s + 1) * D]
    return jnp.where(pl.program_id(0) == 0, both[:HALF], both[HALF:])[:, None, :]


def fold(out, start, width, row):
    @pl.when(pl.program_id(0) == 0)
    def _():
        out[:, start : start + width] = jnp.zeros((8, width), F32)

    for i in range(8):
        at = (slice(i, i + 1), slice(start, start + width))
        out[at] = out[at] + row[:, i * width : (i + 1) * width]


def mid_kernel(o0, o1, o2, o3, w0, w1, w2, w3, table, x, cot, branch, middle, hidden, down, dsum):
    total = unfold(table, OB, 128)
    for o, w in zip((o0, o1, o2, o3), (w0, w1, w2, w3)):
        total = total + nn(flat(o), w[...])
    branched = frames_of(total)
    branch[...] = branched
    mid_value = x[...].astype(F32) + segment(table, 2) * branched
    middle[...] = mid_value
    normal, _ = norm(mid_value)
    hidden[...] = (normal * (1.0 + segment(table, 4)) + segment(table, 3)).astype(BF16)
    grad = (segment(table, 5) * cot[...].astype(F32)).astype(BF16)
    down[...] = grad
    fold(dsum, 0, 128, jnp.sum(grad.astype(F32).reshape(RAW, D), axis=0, keepdims=True))


def half_spec(width):
    return pl.BlockSpec((HALF, PR, width), lambda i, *_: (i, 0, 0))


def mid(pieces, weights, table, x, cot):
    return pl.pallas_call(
        mid_kernel,
        out_shape=[
            shape((FPD, PR, D), F32),
            shape((FPD, PR, D), F32),
            shape((FPD, PR, D)),
            shape((FPD, PR, D)),
            shape((8, 128), F32),
        ],
        grid=(FPD // HALF,),
        in_specs=[half_spec(HC)] * 4
        + [whole((HC, D))] * 4
        + [whole((FPD, WIDE)), half_spec(D), half_spec(D)],
        out_specs=[half_spec(D)] * 4 + [whole((8, 128))],
        compiler_params=params(26),
        cost_estimate=cost(2 * 512 * D * D, 12 * MB),
        name="mid",
    )(*pieces, *weights, table, x, cot)


def mid_back_kernel(
    hg, middle, branch, cot, table, w0, w1, w2, w3, usum, dsum, mg, bg, a0, a1, a23, sums
):
    grad = hg[...]
    normal, rate = norm(middle[...])
    put_half(sums, D, jnp.sum(grad, axis=1))
    put_half(sums, 2 * D, jnp.sum(grad * normal, axis=1))
    total = cot[...].astype(F32) + norm_back(normal, rate, grad * (1.0 + segment(table, 4)))
    mg[...] = total
    put_half(sums, 0, jnp.sum(total * branch[...], axis=1))
    low = (segment(table, 2) * total).astype(BF16)
    bg[...] = low
    low = low.reshape(RAW, D)
    sums[:, 3 * D : 3 * D + NB] = usum[...]
    sums[:, 3 * D + NB : 3 * D + NB + 128] = dsum[...]
    fold(sums, 3 * D + NB + 128, 128, jnp.sum(low.astype(F32), axis=0, keepdims=True))
    for j, w in enumerate((w0, w1, w2, w3)):
        value = frames_of(nt(low, w[...]).astype(BF16))
        if j < 2:
            (a0, a1)[j][...] = value
        else:
            a23[j - 2] = value


def mid_back(hg, middle, branch, cot, table, weights, usum, dsum):
    return pl.pallas_call(
        mid_back_kernel,
        out_shape=[shape((FPD, PR, D), F32), shape((FPD, PR, D))]
        + [shape((FPD, PR, HC))] * 2
        + [shape((2, FPD, PR, HC)), shape((8, EARLY), F32)],
        grid=(FPD // HALF,),
        in_specs=[half_spec(D)] * 4
        + [whole((FPD, WIDE))]
        + [whole((HC, D))] * 4
        + [whole((8, NB)), whole((8, 128))],
        out_specs=[half_spec(D)] * 2
        + [half_spec(HC)] * 2
        + [pl.BlockSpec((2, HALF, PR, HC), lambda i: (0, i, 0, 0)), whole((8, EARLY))],
        compiler_params=params(26),
        cost_estimate=cost(2 * 512 * D * D, 12 * MB),
        name="mid_back",
    )(hg, middle, branch, cot, table, *weights, usum, dsum)


NB = 512
STEPS = FF // NB
PER = D // NB
TOKENS = FPD * PR


def block_of(t):
    phase = t // PER
    return ((phase % 2) * 2) ^ (phase // 2)


def up_column(t, row):
    return (row ^ block_of(t)) * PER + t % PER


def down_row(t):
    return block_of(t) * PER + t % PER


def down_spec(j):
    phase = (0, 2, 1, 3)[j]
    return pl.BlockSpec((NB, D), lambda t, row: (jnp.clip(t - phase * PER, 0, PER - 1), 0))


def pick_down(d0, d1, d2, d3):
    phase = pl.program_id(0) // PER
    return jnp.where(
        phase < 2,
        jnp.where(phase == 0, d0[...], d2[...]),
        jnp.where(phase == 2, d1[...], d3[...]),
    )


def feed_kernel(row_ref, h2, dg, u0, u1, u2, u3, table, d0, d1, d2, d3, act, upg, hg, usum):
    row = row_ref[0]
    ups = (u0, u1, u2, u3)
    down = pick_down(d0, d1, d2, d3)
    at = pl.ds(up_column(pl.program_id(0), row), 1)
    u = table[at, UB : UB + NB]
    for j, w in enumerate(ups):
        u = u + nn(h2[:, columns(row, j)], w[...])
    rate = math.sqrt(2.0 / math.pi)
    square = u * u
    half = 0.5 + 0.5 * jnp.tanh(u * (rate + (rate * 0.044715) * square))
    active = u * half
    act[...] = active.astype(BF16)
    slope = half + active * (1.0 - half) * (2.0 * rate + (6.0 * rate * 0.044715) * square)
    grad = (nt(dg[...], down) * slope).astype(BF16)
    upg[...] = grad
    put(usum, 0, up_column(pl.program_id(0), row), jnp.sum(grad.astype(F32), axis=0, keepdims=True))

    @pl.when(pl.program_id(0) == 0)
    def _():
        hg[...] = jnp.zeros_like(hg)

    for j, w in enumerate(ups):
        hg[:, columns(row, j)] = hg[:, columns(row, j)] + nt(grad, w[...])


def feed(row, h2, dg, ups, table, downs):
    tok = whole((TOKENS, D))
    block = pl.BlockSpec((TOKENS, NB), lambda t, row: (0, t))
    return pl.pallas_call(
        feed_kernel,
        out_shape=[
            shape((TOKENS, FF)),
            shape((TOKENS, FF)),
            shape((TOKENS, D), F32),
            shape((8, NB), F32),
        ],
        grid_spec=pltpu.PrefetchScalarGridSpec(
            num_scalar_prefetch=1,
            grid=(STEPS,),
            in_specs=[tok, tok]
            + [pl.BlockSpec((HC, NB), lambda t, row: (0, up_column(t, row[0])))] * 4
            + [whole((FPD, WIDE))]
            + [down_spec(j) for j in range(4)],
            out_specs=[block, block, tok, whole((8, NB))],
        ),
        compiler_params=params(58),
        cost_estimate=cost(3 * 2 * TOKENS * D * FF, 30 * MB, TOKENS * FF),
        name="feed",
    )(row, h2, dg, *ups, table, *downs)


def down_step(da, db, dg, act, part, dn):
    g = pl.program_id(0)
    down = jnp.where(g < PER, da[...], db[...])
    active = act[...]
    dn[...] = dn[...] + nn(active, down)
    part[0] = tn(active, dg[...]).astype(BF16)


def down_send_kernel(dg, act, da, db, part, dn):
    @pl.when(pl.program_id(0) == 0)
    def _():
        dn[...] = jnp.zeros_like(dn)

    down_step(da, db, dg, act, part, dn)


def down_keep_kernel(dg, act, da, db, before, table, middle, cot, part, out, gate, dn):
    @pl.when(pl.program_id(0) == 0)
    def _():
        dn[...] = before[...]

    down_step(da, db, dg, act, part, dn)

    @pl.when(pl.program_id(0) == STEPS // 2 - 1)
    def _():
        bias = unfold(table, DB, 128)
        for f in range(FPD):
            rows = slice(f * PR, (f + 1) * PR)
            value = dn[rows, :] + bias
            out[f] = (middle[f] + table[f : f + 1, 5 * D : 6 * D] * value).astype(BF16)
            gate[f : f + 1, :] = jnp.sum(cot[f].astype(F32) * value, axis=0, keepdims=True)


def down_half(first, dg, act, downs, extra=()):
    tok = whole((TOKENS, D))
    full = whole((FPD, PR, D))
    half = STEPS // 2
    weight = lambda k: pl.BlockSpec((NB, D), lambda g: (jnp.clip(g - k * PER, 0, PER - 1), 0))
    start = half if first else 0
    part = pl.BlockSpec((1, NB, D), lambda g: (g // PER, g % PER, 0))
    out_specs, out_shape, scratch, specs = [part], [shape((2, D, D))], [], []
    if first:
        out_specs += [tok]
        out_shape += [shape((TOKENS, D), F32)]
    else:
        specs = [tok, whole((FPD, WIDE)), full, full]
        out_specs += [full, whole((8, D))]
        out_shape += [shape((FPD, PR, D)), shape((8, D), F32)]
        scratch = [pltpu.VMEM((TOKENS, D), F32)]
    return pl.pallas_call(
        down_send_kernel if first else down_keep_kernel,
        out_shape=out_shape,
        grid=(half,),
        in_specs=[tok, pl.BlockSpec((TOKENS, NB), lambda g: (0, g + start)), weight(0), weight(1)]
        + specs,
        out_specs=out_specs,
        scratch_shapes=scratch,
        compiler_params=params(40),
        cost_estimate=cost(2 * TOKENS * D * FF, 14 * MB),
        name="down_weight_send" if first else "down_weight_keep",
    )(dg, act, *downs, *extra)


def up_weight_kernel(row_ref, h2, upg, uk, us):
    row = row_ref[0]
    grad = upg[...]
    for j, ref in enumerate((uk, us, uk, us)):
        ref[j // 2, 0] = tn(h2[:, columns(row, j)], grad).astype(BF16)


def up_weight_grad(row, h2, upg):
    up_out = pl.BlockSpec(
        (2, 1, HC, NB),
        lambda t, row: (0, up_column(t, row[0]) // PER, 0, up_column(t, row[0]) % PER),
    )
    return pl.pallas_call(
        up_weight_kernel,
        out_shape=[shape((2, 4, HC, D))] * 2,
        grid_spec=pltpu.PrefetchScalarGridSpec(
            num_scalar_prefetch=1,
            grid=(STEPS,),
            in_specs=[whole((TOKENS, D)), pl.BlockSpec((TOKENS, NB), lambda t, row: (0, t))],
            out_specs=[up_out, up_out],
        ),
        compiler_params=params(58),
        cost_estimate=cost(2 * TOKENS * D * FF, 14 * MB),
        name="up_weight_grad",
    )(row, h2, upg)


def out_weight_kernel(t0, t1, t2, t3, bg, keep, send):
    grad = bg[...].reshape(TOKENS, D)
    for j, t in enumerate((t0, t1, t2, t3)):
        ref = (keep, send)[j % 2]
        ref[j // 2] = tn(t[...].reshape(TOKENS, HC), grad).astype(BF16)


def out_weight_grad(pieces, bg):
    return pl.pallas_call(
        out_weight_kernel,
        out_shape=[shape((2, HC, D))] * 2,
        grid=(1,),
        in_specs=[whole((FPD, PR, HC))] * 4 + [whole((FPD, PR, D))],
        out_specs=[whole((2, HC, D))] * 2,
        compiler_params=params(14),
        cost_estimate=cost(2 * TOKENS * D * D, 4 * MB),
        name="out_weight_grad",
    )(*pieces, bg)


CHUNKS = 16
UP_ROWS, OUT_ROWS, DOWN_ROWS = D // CHUNKS, HC // CHUNKS, D // CHUNKS
FIRST = UP_ROWS + OUT_ROWS
ROWS = FIRST + DOWN_ROWS


def core_sum_kernel(ua, ub, da, db, oa, ob, out):
    def both(a, b):
        return (a.astype(F32) + b.astype(F32)).astype(BF16)

    for c in range(4):
        at = c * ROWS
        low, high = c * OUT_ROWS, (c + 1) * OUT_ROWS
        for i in range(4):
            to = at + i * OUT_ROWS
            out[0, to : to + OUT_ROWS] = both(ua[0, i, low:high], ub[0, i, low:high])
        out[0, at + UP_ROWS : at + FIRST] = both(oa[0, low:high], ob[0, low:high])
        low, high = c * DOWN_ROWS, (c + 1) * DOWN_ROWS
        out[0, at + FIRST : at + ROWS] = both(da[0, low:high], db[0, low:high])


def core_sum(up, down, out):
    ups = pl.BlockSpec((1, 4, 4 * OUT_ROWS, D), lambda j, c: (j, 0, c, 0))
    outs = pl.BlockSpec((1, 4 * OUT_ROWS, D), lambda j, c: (j, c, 0))
    downs = pl.BlockSpec((1, 4 * DOWN_ROWS, D), lambda j, c: (j, c, 0))
    return pl.pallas_call(
        core_sum_kernel,
        out_shape=shape((2, CHUNKS * ROWS, D)),
        grid=(2, CHUNKS // 4),
        in_specs=[ups, ups, downs, downs, outs, outs],
        out_specs=pl.BlockSpec((1, 4 * ROWS, D), lambda j, c: (j, c, 0)),
        compiler_params=params(58),
        cost_estimate=cost(1000, 1000),
        name="core_sum",
    )(*up, *down, *out)


def unpack_kernel(total, up, out, down):
    for k in range(4):
        at = k * ROWS
        for i in range(4):
            rows = slice(at + i * OUT_ROWS, at + (i + 1) * OUT_ROWS)
            up[k * OUT_ROWS : (k + 1) * OUT_ROWS, i * D : (i + 1) * D] = total[rows].astype(F32)
        out[k * OUT_ROWS : (k + 1) * OUT_ROWS] = total[at + UP_ROWS : at + FIRST].astype(F32)
        down[k * DOWN_ROWS : (k + 1) * DOWN_ROWS] = total[at + FIRST : at + ROWS].astype(F32)


def unpack(total):
    block = lambda i: (i, 0)
    return pl.pallas_call(
        unpack_kernel,
        out_shape=[shape((HC, FF), F32), shape((HC, D), F32), shape((D, D), F32)],
        grid=(4,),
        in_specs=[pl.BlockSpec((4 * ROWS, D), block)],
        out_specs=[
            pl.BlockSpec((4 * OUT_ROWS, FF), block),
            pl.BlockSpec((4 * OUT_ROWS, D), block),
            pl.BlockSpec((4 * DOWN_ROWS, D), block),
        ],
        compiler_params=params(24),
        cost_estimate=cost(0, 14 * MB),
        name="unpack",
    )(total)


LATE = 3 * D + 2 * HC
EARLY = 3 * D + NB + 256


def arrange_kernel(row_ref, a0, a1, a2, a3, late, far, out):
    row = row_ref[0]
    for j, a in enumerate((a0, a1, a2, a3)):
        for s in range(3):
            lanes = pl.ds(pl.multiple_of(s * D + (row ^ j) * HC, HC), HC)
            out[:, lanes] = a[:, s * HC : (s + 1) * HC]
    both = jnp.concatenate([late[...].astype(F32), far[...].astype(F32)], axis=0)
    out[:, 3 * D :] = both.astype(BF16)


def arrange(row, pieces, late, far):
    rows = pieces[0].shape[0]
    return pl.pallas_call(
        arrange_kernel,
        out_shape=shape((rows, 3 * D + LATE)),
        grid_spec=pltpu.PrefetchScalarGridSpec(
            num_scalar_prefetch=1,
            grid=(1,),
            in_specs=[whole((rows, 3 * HC))] * 4 + [whole((8, LATE))] * 2,
            out_specs=whole((rows, 3 * D + LATE)),
        ),
        compiler_params=params(16),
        cost_estimate=cost(0, 8 * rows * D),
        name="arrange",
    )(row, *pieces, late, far)


def stack_kernel(a0, a1, a2, a3, weights, sums):
    for k, a in enumerate((a0, a1, a2, a3)):
        weights[k] = a[:, : 3 * D]
        sums[k] = a[:, 3 * D :]


def stack(pieces):
    rows, width = pieces[0].shape
    return pl.pallas_call(
        stack_kernel,
        out_shape=[shape((4, rows, 3 * D)), shape((4, rows, LATE))],
        grid=(1,),
        in_specs=[whole((rows, width))] * 4,
        out_specs=[whole((4, rows, 3 * D)), whole((4, rows, LATE))],
        compiler_params=params(16),
        cost_estimate=cost(0, 2 * MB),
        name="stack",
    )(*pieces)


def place_kernel(index_ref, low, high, out):
    for m, a in enumerate((low.at[0], low.at[1], high.at[1], high.at[0])):

        @pl.when(pl.program_id(0) == m)
        def _():
            for k in range(4):
                out[0, index_ref[1] ^ k] = a[k].astype(F32)


def place(index, low, high):
    rows = low.shape[2]
    return pl.pallas_call(
        place_kernel,
        out_shape=shape((4, 4, rows, 3 * D), F32),
        grid_spec=pltpu.PrefetchScalarGridSpec(
            num_scalar_prefetch=1,
            grid=(4,),
            in_specs=[whole(low.shape)] * 2,
            out_specs=pl.BlockSpec((1, 4, rows, 3 * D), lambda i, index: (index[0] ^ i, 0, 0, 0)),
        ),
        compiler_params=params(24),
        cost_estimate=cost(0, 24 * rows * D),
        name="place",
    )(index, low, high).reshape(HC, 3 * D)


def project_back_kernel(row_ref, dq, dk, dv, rk, rv, w0, w1, w2, w3, cp, sp, fr, dp, h0, h2, hs, bsum):
    row = row_ref[0]
    f = pl.program_id(0)
    later = (f > 0).astype(F32)
    keys = dk[0] + later * rk[0, 0].astype(F32)
    values = dv[0] + later * rv[0, 0].astype(F32)
    cosine, sine = cosines(cp, sp, fr, f)
    dp[0, :, :HC] = dq[0]
    dp[0, :, HC : 2 * HC] = turn(keys, cosine, -sine).astype(BF16)
    dp[0, :, 2 * HC :] = values.astype(BF16)
    grad = dp[0]
    sums = jnp.sum(grad.astype(F32), axis=0, keepdims=True)

    @pl.when(f == 0)
    def _():
        bsum[...] = jnp.zeros_like(bsum)

    number = lax.broadcasted_iota(jnp.int32, (8, 2 * HC), 0)
    bsum[...] = bsum[...] + jnp.where(number == row, sums[:, : 2 * HC], 0.0)
    bsum[:, :HC] = bsum[:, :HC] + jnp.where(number[:, :HC] == row + 4, sums[:, 2 * HC :], 0.0)
    for j, w in enumerate((w0, w1, w2, w3)):
        part = nt(grad, w[...]).astype(BF16)
        at = (0, slice(None), columns(row, j))
        h0[at] = part[:PR]
        hs[(0,) + at] = part[PR : 2 * PR]
        h2[at] = part[2 * PR : 3 * PR]
        hs[(1,) + at] = part[3 * PR :]


def project_back(row, dq, dk, dv, returned, weights, tables):
    block = pl.BlockSpec((1, TOK, HC), lambda f, *_: (f, 0, 0))
    late = [
        pl.BlockSpec((1, 1, TOK, HC), lambda f, *_, i=i: (i, jnp.maximum(f - 1, 0), 0, 0))
        for i in range(2)
    ]
    piece = pl.BlockSpec((1, PR, D), lambda f, *_: (f, 0, 0))
    return pl.pallas_call(
        project_back_kernel,
        out_shape=[
            shape((FPD, TOK, 3 * HC)),
            shape((FPD, PR, D)),
            shape((FPD, PR, D)),
            shape((2, FPD, PR, D)),
            shape((8, 2 * HC), F32),
        ],
        grid_spec=pltpu.PrefetchScalarGridSpec(
            num_scalar_prefetch=1,
            grid=(FPD,),
            in_specs=[block] * 3
            + late
            + [whole((HC, 3 * HC))] * 4
            + [whole((TOK, HC)), whole((TOK, HC)), whole((16, 2 * HC))],
            out_specs=[
                pl.BlockSpec((1, TOK, 3 * HC), lambda f, *_: (f, 0, 0)),
                piece,
                piece,
                pl.BlockSpec((2, 1, PR, D), lambda f, *_: (0, f, 0, 0)),
                whole((8, 2 * HC)),
            ],
        ),
        compiler_params=params(20),
        cost_estimate=cost(2 * FPD * TOK * D * 3 * HC, 14 * MB),
        name="project_back",
    )(row, dq, dk, dv, returned, returned, *weights, *tables)


def weight_kernel(row_ref, h, dp, w):
    w[0] = tn(h[...], dp[...]).astype(BF16)


def project_weight(row, hidden, dproj):
    tokens = FPD * TOK
    return pl.pallas_call(
        weight_kernel,
        out_shape=shape((4, HC, 3 * HC)),
        grid_spec=pltpu.PrefetchScalarGridSpec(
            num_scalar_prefetch=1,
            grid=(4,),
            in_specs=[
                pl.BlockSpec((tokens, HC), lambda j, row: (0, row[0] ^ j)),
                whole((tokens, 3 * HC)),
            ],
            out_specs=pl.BlockSpec((1, HC, 3 * HC), lambda j, row: (j, 0, 0)),
        ),
        compiler_params=params(20),
        cost_estimate=cost(2 * tokens * D * 3 * HC, 9 * MB),
        name="project_weight",
    )(row, hidden.reshape(tokens, D), dproj.reshape(tokens, 3 * HC))


def input_back_kernel(x, h0, near, far, table, mg, bsum, gate, out, sums):
    grad = h0[...].astype(F32) + near[0].astype(F32) + far[...].astype(F32)
    normal, rate = norm(x[...].astype(F32))
    put_half(sums, 0, jnp.sum(grad, axis=1))
    put_half(sums, D, jnp.sum(grad * normal, axis=1))
    sums[:, 2 * D : 3 * D] = gate[...]
    sums[:, 3 * D :] = bsum[...]
    out[...] = mg[...] + norm_back(normal, rate, grad * (1.0 + segment(table, 1)))


def input_back(x, h0, near, far, table, mg, bsum, gate):
    return pl.pallas_call(
        input_back_kernel,
        out_shape=[shape((FPD, PR, D), F32), shape((8, LATE), F32)],
        grid=(FPD // HALF,),
        in_specs=[half_spec(D)] * 2
        + [pl.BlockSpec((1, HALF, PR, D), lambda i: (0, i, 0, 0))]
        + [half_spec(D), whole((FPD, WIDE)), half_spec(D), whole((8, 2 * HC)), whole((8, D))],
        out_specs=[half_spec(D), whole((8, LATE))],
        compiler_params=params(20),
        cost_estimate=cost(20 * 512 * D, 10 * MB),
        name="input_back",
    )(x, h0, near, far, table, mg, bsum, gate)


def join_kernel(a0, a1, a2, a3, out):
    for k, a in enumerate((a0, a1, a2, a3)):
        out[2 * k : 2 * k + 2] = a[...]


def join(pieces):
    width = pieces[0].shape[-1]
    return pl.pallas_call(
        join_kernel,
        out_shape=shape((8, 8, width)),
        grid=(1,),
        in_specs=[whole((2, 8, width))] * 4,
        out_specs=whole((8, 8, width)),
        compiler_params=params(16),
        cost_estimate=cost(0, 2 * MB),
        name="join",
    )(*pieces)


def final_kernel(row_ref, *refs):
    row = row_ref[0]
    low, high, *early = refs[:6]
    ada, ab, qb, ob, ub, db, asum = refs[6:]
    late = [low.at[0], low.at[1], high.at[0], high.at[1]]
    early = [early[0], early[3], early[1], early[2]]

    def rows(ref, cols):
        value = ref[:, :, cols].astype(F32)
        return value.reshape(64, value.shape[-1])

    left = [rows(s, slice(EARLY, EARLY + HC)).astype(BF16) for s in early]
    for segment in range(6):
        source, start = ((late, 0), (late, 1), (early, 0), (early, 1), (early, 2), (late, 2))[segment]
        cols = slice(start * D, (start + 1) * D)
        product, total = 0.0, 0.0
        for s, ref in zip(left, source):
            right = rows(ref, cols)
            total = total + jnp.sum(right, axis=0, keepdims=True)
            product = product + tn(s, right.astype(BF16))
        at = segment * D
        ada[:, at : at + D] = product
        asum[0:1, at : at + D] = total

    def fold8(value):
        value = jnp.sum(value, axis=0)
        return value if value.shape[0] == 8 else value[:8] + value[8:]

    def bias(source, start, stop):
        return sum(
            fold8(ref[:, :, start:stop].astype(F32)) for ref in source
        )

    ab[...] = asum[0:1, pl.ds(pl.multiple_of(row * 1536, 512), 1536)]
    folded = bias(late, 3 * D, LATE)
    for i in range(3):
        chunk = 3 * row + i
        at = jnp.where(chunk < 4, chunk, chunk - 4)
        second = (chunk >= 4) & (chunk < 8)
        value = jnp.where(second, folded[:, HC:], folded[:, :HC])
        qb[:, i * HC : (i + 1) * HC] = take(value, at)
    folded = bias(early, 3 * D, EARLY)
    for i in range(2):
        at = 2 * row + i
        ub[:, i * NB : (i + 1) * NB] = take(folded[:, :NB], at)
        db[:, i * 128 : (i + 1) * 128] = take(folded[:, NB : NB + 128], at)
        ob[:, i * 128 : (i + 1) * 128] = take(folded[:, NB + 128 :], at)


def final_sums(row, late, early):
    sizes = (1536, 768, 256, 1024, 256)
    return pl.pallas_call(
        final_kernel,
        out_shape=[shape((HC, 6 * D), F32)] + [shape((1, n), F32) for n in sizes],
        grid_spec=pltpu.PrefetchScalarGridSpec(
            num_scalar_prefetch=1,
            grid=(1,),
            in_specs=[whole((2, 4, 16, LATE))] * 2
            + [whole((8, 8, EARLY + HC))] * 4,
            out_specs=[whole((HC, 6 * D))] + [whole((1, n)) for n in sizes],
            scratch_shapes=[pltpu.VMEM((8, 6 * D), F32)],
        ),
        compiler_params=params(28),
        cost_estimate=cost(2 * 256 * HC * 6 * D, 10 * MB),
        name="final_sums",
    )(row, *late, *early)


def row_sum(value):
    value = value + swap(value, CORE)
    return value + swap(value, DIRECT)


def row_pieces(value):
    return [value, swap(value, CORE), swap(value, DIRECT), swap(value, DIRECT ^ CORE)]


def by_row(pieces, row):
    a, b, c, d = pieces
    odd, high = row % 2 == 1, row >= 2
    a, b = jnp.where(odd, b, a), jnp.where(odd, a, b)
    c, d = jnp.where(odd, d, c), jnp.where(odd, c, d)
    return jnp.stack(
        [
            jnp.where(high, c, a),
            jnp.where(high, d, b),
            jnp.where(high, a, c),
            jnp.where(high, b, d),
        ]
    )


def quarter_rows(value, bit, index, axis):
    rows = value.shape[1] // 4
    at = lambda m: lax.dynamic_slice_in_dim(value, (index[axis] ^ m) * rows, rows, 1)
    return [at(0)] + [swap(at(m), bit * m) for m in (1, 2, 3)]


def add_all(parts):
    return sum(part.astype(F32) for part in parts).astype(BF16)


def exchange_rows(value, bit, index, axis):
    return add_all(quarter_rows(value, bit, index, axis))


def turn_heads(own, beside, across, order=lambda piece: piece):
    across = swap(across, DIRECT)
    return [own, swap(beside, CORE), across[0], swap(order(across)[1], CORE)]


def per_device(
    activations,
    noise_embed,
    frame_position,
    cotangent,
    ada_weight,
    ada_bias,
    qkv_weight,
    qkv_bias,
    out_weight,
    out_bias,
    up_weight,
    up_bias,
    down_weight,
    down_bias,
):
    row = lax.axis_index(("xl", "c")).astype(jnp.int32)
    row_arg = row.reshape(1)
    index = [lax.axis_index("y").astype(jnp.int32), lax.axis_index("z").astype(jnp.int32)]
    index_arg = jnp.stack(index)

    x0 = activations
    x2 = swap(x0, DIRECT)
    x1 = swap(x0, CORE)
    p0 = shift(activations[1:], 1)
    biases = (ada_bias, qkv_bias, out_bias, up_bias, down_bias)
    heads = list(split_heads(row_arg, qkv_weight))
    noise, heads[1] = lax.optimization_barrier((noise_embed, heads[1]))
    part, silu_own, *tables = prepare(row_arg, frame_position, noise, ada_weight, biases)
    across = swap(heads[2], OTHER)
    qkv_pieces = [heads[0], swap(heads[1], CORE), across]
    part = part + swap(part, CORE)
    table = part + swap(part, DIRECT)
    x2, p0, table, *qkv_pieces = lax.optimization_barrier((x2, p0, table, *qkv_pieces))

    qkv_pieces = qkv_pieces[:2] + [qkv_pieces[2][0], swap(qkv_pieces[2][1], CORE)]
    x3 = swap(x2, CORE)
    p2 = swap(p0, DIRECT)
    p1 = swap(p0, CORE)
    before_mods = shift(table[:, : 2 * D], 1)

    out_own, up_own, _ = lax.optimization_barrier((out_weight, up_weight, table))
    outs2 = swap(out_own, OTHER)
    ups2 = swap(up_own, OTHER)

    hidden1, q, k, v = project(True, row_arg, (x0, x1, x2, x3), table, table, qkv_pieces, tables)
    p2, down_own, q, before_mods = lax.optimization_barrier((p2, down_weight, q, before_mods))
    p3 = swap(p2, CORE)
    downs2 = swap(down_own, DIRECT)
    kp, vp = project(
        False, row_arg, (p0, p1, p2, p3), table, before_mods, qkv_pieces, tables
    )
    *mixed, lse = attend(frame_position, q, k, v, kp, vp)
    outs2, ups2, downs2, lse = lax.optimization_barrier((outs2, ups2, downs2, lse))
    outs = [out_weight, swap(out_own, CORE), outs2, swap(outs2, CORE)]
    ups = [up_weight, swap(up_own, CORE), ups2, swap(ups2, CORE)]
    downs = [down_weight, swap(down_own, CORE), downs2, swap(downs2, CORE)]
    turned = turn_heads(*mixed)
    branch, middle, hidden2, down_grad, dsum = mid(turned, outs, table, x0, cotangent)
    h2 = hidden2.reshape(TOKENS, D)
    dg = down_grad.reshape(TOKENS, D)
    act, upg, hg, usum = feed(row_arg, h2, dg, ups, table, downs)
    mg, bg, *ag, early = mid_back(
        hg.reshape(FPD, PR, D), middle, branch, cotangent, table, outs, usum, dsum
    )
    late = []
    back = turn_heads(*ag[:2], ag[2], order=lambda piece: late.append(piece) or piece)[:2]

    early = early + swap(early, CORE)
    upg, early, _ = lax.optimization_barrier((upg, early, bg))
    early_far = swap(early, DIRECT)
    uk, us = up_weight_grad(row_arg, h2, upg)
    us = swap(us, CORE)
    dg_later, early_far, uk = lax.optimization_barrier((dg, early_far, uk))
    early = jnp.concatenate([(early + early_far).astype(BF16), silu_own], axis=1)
    early_far = swap(early, FAR)
    ds_part, dn = down_half(True, dg_later, act, (downs[1], downs[3]))
    ds_part_far = swap(ds_part, CORE)
    dn, early, early_far, bg_later, us, far_back, *back = lax.optimization_barrier(
        (dn, early, early_far, bg, us, *late, *back)
    )
    early = jnp.stack([early, early_far])
    early_parts = [early] + [swap(early, m) for m in (16, 32, 48)]
    ok, os = out_weight_grad(turned, bg_later)
    os = swap(os, CORE)
    dk_part, layer_output, gate = down_half(
        False, dg_later, act, (downs[0], downs[2]), (dn, table, middle, cotangent)
    )
    dk_part, early_parts, ds_part_far, os, far_back = lax.optimization_barrier(
        (dk_part, early_parts, ds_part_far, os, far_back)
    )
    back += [far_back[0], swap(far_back[1], CORE)]
    packed = core_sum((uk, us), (dk_part, ds_part_far), (ok, os))
    packed, back = lax.optimization_barrier((packed, back))
    scattered = lax.psum_scatter(packed, ("y", "z"), scatter_dimension=1, tiled=True)

    dq_before, both = attend_back(False, frame_position, q, kp, vp, back, mixed, lse)
    returned = shift(both, -1)
    dq, dk, dv = attend_back(
        True, frame_position, q, k, v, back, mixed, lse, tables, dq_before
    )
    early_parts, dq = lax.optimization_barrier((early_parts, dq))
    early = join(early_parts)
    early_all = [early] + [swap(early, m) for m in (4, 8, 12)]
    dq, early = lax.optimization_barrier((dq, early))
    early = early[0].astype(F32)

    dproj, h0, h2_part, send, bsum = project_back(row_arg, dq, dk, dv, returned, qkv_pieces, tables)
    near = swap(send, CORE)
    qkv_parts = project_weight(row_arg, hidden1, dproj)
    far_part = (h2_part.astype(F32) + near[1].astype(F32)).astype(BF16)
    far = swap(far_part, DIRECT)
    far_part, qkv_parts, *early_all = lax.optimization_barrier((far_part, qkv_parts, *early_all))
    quarters = quarter_rows(qkv_parts, 4, index, 0)
    input_grad, late = input_back(x0, h0, near, far, table, mg, bsum, gate)
    late_near = swap(late, CORE)
    late, *quarters = lax.optimization_barrier((late, *quarters))
    quarters = quarter_rows(add_all(quarters), 16, index, 1)
    late = late + late_near
    late_far = swap(late, DIRECT)
    late, *quarters = lax.optimization_barrier((late, *quarters))
    qkv_parts = add_all(quarters)
    qkv_far = swap(qkv_parts, FAR)
    scattered, late, late_far, qkv_parts = lax.optimization_barrier(
        (scattered, late, late_far, qkv_parts)
    )
    late = late + late_far
    late_low = late.astype(BF16)
    late_far = swap(late_low, FAR)
    share_far = swap(scattered[1], DIRECT)
    late_low, qkv_far = lax.optimization_barrier((late_low, qkv_far))
    qkv_parts = add_all([qkv_parts, qkv_far])
    turned = turn_heads(qkv_parts[0], qkv_parts[1], qkv_parts[2:])
    turned, share_far = lax.optimization_barrier((turned, share_far))
    share = scattered[0].astype(F32) + share_far.astype(F32)
    share_far = swap(share.astype(BF16), FAR)
    last = arrange(row_arg, turned, late_low, late_far)

    share, share_far, last = lax.optimization_barrier((share, share_far, last))
    share = (share + share_far.astype(F32)).astype(BF16)
    totals = lax.all_gather(share, ("y", "z"), axis=0, tiled=True)
    weights, sums_late = stack([last] + [swap(last, m) for m in (16, 32, 48)])
    weights = jnp.stack([weights, swap(weights, 4)])
    sums_late = jnp.stack([sums_late, swap(sums_late, 12)])
    weights_far, sums_far = swap(weights, 12), swap(sums_late, 4)
    up_total, out_total, down_total = unpack(totals)
    qkv_total = place(index_arg, weights, weights_far)

    ada_total, *bias_sums = final_sums(row_arg, (sums_late, sums_far), early_all)
    ada_sum, qkv_sum, out_sum, up_sum, down_sum = [b[0] for b in bias_sums]
    mod_own = jnp.concatenate(
        [late[:, : 2 * D], early[:, : 3 * D], late[:, 2 * D : 3 * D]], axis=1
    ).astype(BF16)
    silu_grad = nt(mod_own, ada_weight)
    silu_grad = by_row(row_pieces(silu_grad), row).transpose(1, 0, 2).reshape(FPD, D)
    embed = noise_embed.astype(F32)
    sigma = jax.nn.sigmoid(embed)
    embed_grad = silu_grad * (sigma * (1.0 + embed * (1.0 - sigma)))

    return (
        layer_output,
        input_grad,
        embed_grad,
        ada_total,
        ada_sum,
        qkv_total,
        qkv_sum,
        out_total,
        out_sum,
        up_total,
        up_sum,
        down_total,
        down_sum,
    )


def solution(mesh):
    fine = Mesh(mesh.devices.reshape(2, 4, 4, 2, 2), AXES)
    seq, row = ("xh", "z", "y"), ("xl", "c")
    token, weight, vector = P(seq, row, None), P(row, None), P(row)
    in_specs = (token, P(seq, None), P(seq), token) + (weight, vector) * 5
    out_specs = (token, token, P(seq, None)) + (weight, vector) * 5
    return jax.shard_map(
        per_device, mesh=fine, in_specs=in_specs, out_specs=out_specs, check_vma=False
    )
```

profile of v0, /device:TPU:6, one launch (start us, length us, event | category | flops | bytes accessed | tf_op | source)
XLA Modules:
  0.0 562.3 jit_solution(5309661721042883289)
XLA Ops:
  19.2 18.3 %collective-permute-done.3 = f32[8,7424]{1,0:T(8,128)S(1)} collective-permute-done((f32[8,7424]{1,0:T(8,128)S(1)}, f32[8,7424]{1,0:T(8,128)S(1)}, u32[]{:S(2)}, u32[]{:S(2)}) %collective-permute-start.3) | collective-permute-done | bytes 237600 | tf_op jit(solution)/shard_map/ppermute | solution.py:27
  37.6 21.6 %collective-permute-done.1.refs_1_ = bf16[7,64,1024]{2,1,0:T(8,128)(2,1)} collective-permute-done((bf16[7,64,1024]{2,1,0:T(8,128)(2,1)}, bf16[7,64,1024]{2,1,0:T(8,128)(2,1)}, u32[]{:S(2)}, u32[]{:S(2)}) %collective-permute-start.1) | collective-permute-done | bytes 917536 | tf_op jit(solution)/shard_map/ppermute | solution.py:31
  62.7 10.0 %project_own.1 = (bf16[8,256,1024]{2,1,0:T(8,128)(2,1)S(1)}, bf16[8,256,256]{2,1,0:T(8,128)(2,1)S(1)}, bf16[8,256,256]{2,1,0:T(8,128)(2,1)S(1)}, bf16[8,256,256]{2,1,0:T(8,128)(2,1)S(1)}) custom-call(s32[1]{0:T(128)} %bitcast.row_ref.refs_0_, bf16[8,64,1024]{2,1,0:T(8,128)(2,1)S(1)} %copy-done.3, bf16[8,64,1024]{2,1,0:T(8,128)(2,1)S(1)} %collective-permute-done.7.refs_2_, ...), custom_call_target="tpu_custom_call" | custom-call | flops 3221225472 | bytes 12582912 | tf_op jit(solution)/shard_map/project_own/pallas_call | solution.py:280
  75.7 12.0 %collective-permute-done.10.refs_6_ = f32[8,2048]{1,0:T(8,128)S(1)} collective-permute-done((f32[8,2048]{1,0:T(8,128)S(1)}, f32[8,2048]{1,0:T(8,128)S(1)}, u32[]{:S(2)}, u32[]{:S(2)}) %collective-permute-start.10) | collective-permute-done | bytes 65568 | tf_op jit(solution)/shard_map/ppermute | solution.py:31
  94.8 8.1 %project_prev.1 = (bf16[7,256,256]{2,1,0:T(8,128)(2,1)S(1)}, bf16[7,256,256]{2,1,0:T(8,128)(2,1)S(1)}) custom-call(s32[1]{0:T(128)} %bitcast.row_ref.refs_0_, bf16[7,64,1024]{2,1,0:T(8,128)(2,1)} %collective-permute-done.1.refs_1_, bf16[7,64,1024]{2,1,0:T(8,128)(2,1)S(1)} %collective-permute-done.11.refs_2_, ...), custom_call_target="tpu_custom_call" | custom-call | flops 2818572288 | bytes 11534336 | tf_op jit(solution)/shard_map/project_prev/pallas_call | solution.py:280
  104.8 32.3 %attend.1 = (bf16[8,64,256]{2,1,0:T(8,128)(2,1)}, bf16[8,64,256]{2,1,0:T(8,128)(2,1)}, bf16[2,8,64,256]{3,2,1,0:T(8,128)(2,1)}, f32[8,8,256]{2,1,0:T(8,128)}) custom-call(s32[8]{0:T(128)} %refs_0_.3, bf16[8,256,256]{2,1,0:T(8,128)(2,1)} %copy-done.17, bf16[8,256,256]{2,1,0:T(8,128)(2,1)} %copy-done.18, bf16[8,256,256]{2,1,0:T(8,128)(2,1)} %copy-done.19, ...), custom_call_target="tpu_custom_call" | custom-call | flops 9663676416 | bytes 6291456 | tf_op jit(solution)/shard_map/attend/pallas_call | solution.py:367
  139.6 12.9 %collective-permute-done.14 = bf16[2,8,64,256]{3,2,1,0:T(8,128)(2,1)S(1)} collective-permute-done((bf16[2,8,64,256]{3,2,1,0:T(8,128)(2,1)}, bf16[2,8,64,256]{3,2,1,0:T(8,128)(2,1)S(1)}, u32[]{:S(2)}, u32[]{:S(2)}) %collective-permute-start.14) | collective-permute-done | bytes 524320 | tf_op jit(solution)/shard_map/ppermute | solution.py:27
  167.7 26.9 %feed.1 = (bf16[512,4096]{1,0:T(8,128)(2,1)}, bf16[512,4096]{1,0:T(8,128)(2,1)}, f32[512,1024]{1,0:T(8,128)}, f32[8,512]{1,0:T(8,128)}) custom-call(s32[1]{0:T(128)} %bitcast.row_ref.refs_0_, bf16[512,1024]{1,0:T(8,128)(2,1)} %bitcast.70, bf16[512,1024]{1,0:T(8,128)(2,1)} %bitcast.67, bf16[256,4096]{1,0:T(8,128)(2,1)} %u0.1, ...), custom_call_target="tpu_custom_call" | custom-call | flops 12884901888 | bytes 31457280 | tf_op jit(solution)/shard_map/feed/pallas_call | solution.py:686
  208.6 10.9 %up_weight_grad.1 = (bf16[2,4,256,1024]{3,2,1,0:T(8,128)(2,1)}, bf16[2,4,256,1024]{3,2,1,0:T(8,128)(2,1)}) custom-call(s32[1]{0:T(128)} %bitcast.row_ref.refs_0_, bf16[512,1024]{1,0:T(8,128)(2,1)} %bitcast.71, bf16[512,4096]{1,0:T(8,128)(2,1)} %get-tuple-element.202.upg), custom_call_target="tpu_custom_call" | custom-call | flops 4294967296 | bytes 14680064 | tf_op jit(solution)/shard_map/up_weight_grad/pallas_call | solution.py:784
  229.7 6.6 %down_weight_send.1 = (bf16[2,1024,1024]{2,1,0:T(8,128)(2,1)S(1)}, f32[512,1024]{1,0:T(8,128)S(1)}) custom-call(bf16[512,1024]{1,0:T(8,128)(2,1)S(1)} %bitcast.68, bf16[512,4096]{1,0:T(8,128)(2,1)} %get-tuple-element.205.act, bf16[1024,1024]{1,0:T(8,128)(2,1)S(1)} %copy-done.49, bf16[1024,1024]{1,0:T(8,128)(2,1)S(1)} %copy-done.51), custom_call_target="tpu_custom_call" | custom-call | flops 4294967296 | bytes 14680064 | tf_op jit(solution)/shard_map/down_weight_send/pallas_call | solution.py:758
  243.9 9.5 %collective-permute-done.27 = bf16[8,4096]{1,0:T(8,128)(2,1)S(1)} collective-permute-done((bf16[8,4096]{1,0:T(8,128)(2,1)S(1)}, bf16[8,4096]{1,0:T(8,128)(2,1)S(1)}, u32[]{:S(2)}, u32[]{:S(2)}) %collective-permute-start.27) | collective-permute-done | bytes 65568 | tf_op jit(solution)/shard_map/ppermute | solution.py:27
  256.3 4.6 collective-permute-start.33
  260.9 9.4 %down_weight_keep.1 = (bf16[2,1024,1024]{2,1,0:T(8,128)(2,1)}, bf16[8,64,1024]{2,1,0:T(8,128)(2,1)}, f32[8,1024]{1,0:T(8,128)S(1)}) custom-call(bf16[512,1024]{1,0:T(8,128)(2,1)S(1)} %bitcast.69, bf16[512,4096]{1,0:T(8,128)(2,1)} %get-tuple-element.205.act, bf16[1024,1024]{1,0:T(8,128)(2,1)} %da.1, bf16[1024,1024]{1,0:T(8,128)(2,1)} %collective-permute-done.19.d2.db, ...), custom_call_target="tpu_custom_call" | custom-call | flops 4294967296 | bytes 14680064 | tf_op jit(solution)/shard_map/down_weight_keep/pallas_call | solution.py:758
  273.9 12.0 %core_sum.1 = bf16[2,2304,1024]{2,1,0:T(8,128)(2,1)} custom-call(bf16[2,4,256,1024]{3,2,1,0:T(8,128)(2,1)} %get-tuple-element.226.ua, bf16[2,4,256,1024]{3,2,1,0:T(8,128)(2,1)} %copy-done.76, bf16[2,1024,1024]{2,1,0:T(8,128)(2,1)} %get-tuple-element.228.da, bf16[2,1024,1024]{2,1,0:T(8,128)(2,1)} %collective-permute-done.34.db, ...), custom_call_target="tpu_custom_call" | custom-call | flops 1000 | bytes 1000 | tf_op jit(solution)/shard_map/core_sum/pallas_call | solution.py:844
  286.6 19.5 %attend_back_prev.1 = (f32[8,256,256]{2,1,0:T(8,128)}, bf16[2,7,256,256]{3,2,1,0:T(8,128)(2,1)}) custom-call(s32[8]{0:T(128)} %refs_0_.3, bf16[8,256,256]{2,1,0:T(8,128)(2,1)} %copy-done.17, bf16[7,256,256]{2,1,0:T(8,128)(2,1)} %copy-done.74, bf16[7,256,256]{2,1,0:T(8,128)(2,1)} %copy-done.75, bf16[8,64,256]{2,1,0:T(8,128)(2,1)} %copy-done.32, ...), custom_call_target="tpu_custom_call" | custom-call | flops 8053063680 | bytes 12582912 | tf_op jit(solution)/shard_map/attend_back_prev/pallas_call | solution.py:490
  306.3 32.1 %attend_back_own.1 = (bf16[8,256,256]{2,1,0:T(8,128)(2,1)}, f32[8,256,256]{2,1,0:T(8,128)}, f32[8,256,256]{2,1,0:T(8,128)}) custom-call(s32[8]{0:T(128)} %refs_0_.3, bf16[8,256,256]{2,1,0:T(8,128)(2,1)} %copy-done.17, bf16[8,256,256]{2,1,0:T(8,128)(2,1)} %copy-done.18, bf16[8,256,256]{2,1,0:T(8,128)(2,1)} %copy-done.19, bf16[8,64,256]{2,1,0:T(8,128)(2,1)} %copy-done.32, ...), custom_call_target="tpu_custom_call" | custom-call | flops 1000 | bytes 1000 | tf_op jit(solution)/shard_map/attend_back_own/pallas_call | solution.py:490
  339.2 17.5 %collective-permute-done.37.rk.rv = bf16[2,7,256,256]{3,2,1,0:T(8,128)(2,1)S(1)} collective-permute-done((bf16[2,7,256,256]{3,2,1,0:T(8,128)(2,1)}, bf16[2,7,256,256]{3,2,1,0:T(8,128)(2,1)S(1)}, u32[]{:S(2)}, u32[]{:S(2)}) %collective-permute-start.37) | collective-permute-done | bytes 1835040 | tf_op jit(solution)/shard_map/ppermute | solution.py:31
  361.2 7.5 %project_back.1 = (bf16[8,256,768]{2,1,0:T(8,128)(2,1)S(1)}, bf16[8,64,1024]{2,1,0:T(8,128)(2,1)S(1)}, bf16[8,64,1024]{2,1,0:T(8,128)(2,1)S(1)}, bf16[2,8,64,1024]{3,2,1,0:T(8,128)(2,1)S(1)}, f32[8,512]{1,0:T(8,128)S(1)}) custom-call(s32[1]{0:T(128)} %bitcast.row_ref.refs_0_, bf16[8,256,256]{2,1,0:T(8,128)(2,1)S(1)} %copy-done.59, ...), custom_call_target="tpu_custom_call" | custom-call | flops 3221225472 | bytes 14680064 | tf_op jit(solution)/shard_map/project_back/pallas_call | solution.py:997
  380.8 4.8 project_weight.1
  385.6 6.4 %collective-permute-done.40.refs_3_ = bf16[8,8,4096]{2,1,0:T(8,128)(2,1)} collective-permute-done((bf16[8,8,4096]{2,1,0:T(8,128)(2,1)}, bf16[8,8,4096]{2,1,0:T(8,128)(2,1)}, u32[]{:S(2)}, u32[]{:S(2)}) %collective-permute-start.40) | collective-permute-done | bytes 524320 | tf_op jit(solution)/shard_map/ppermute | solution.py:27
  392.0 14.0 %collective-permute-done.41.refs_4_ = bf16[8,8,4096]{2,1,0:T(8,128)(2,1)} collective-permute-done((bf16[8,8,4096]{2,1,0:T(8,128)(2,1)}, bf16[8,8,4096]{2,1,0:T(8,128)(2,1)}, u32[]{:S(2)}, u32[]{:S(2)}) %collective-permute-start.41) | collective-permute-done | bytes 524320 | tf_op jit(solution)/shard_map/ppermute | solution.py:27
  416.1 4.2 input_back.1
  420.3 4.2 collective-permute-done.43
  424.5 11.2 %collective-permute-done.44 = bf16[4,64,768]{2,1,0:T(8,128)(2,1)} collective-permute-done((bf16[4,64,768]{2,1,0:T(8,128)(2,1)}, bf16[4,64,768]{2,1,0:T(8,128)(2,1)}, u32[]{:S(2)}, u32[]{:S(2)}) %collective-permute-start.44) | collective-permute-done | bytes 393248 | tf_op jit(solution)/shard_map/ppermute | solution.py:27
  439.7 4.6 collective-permute-start.49
  446.9 7.6 %collective-permute-start.54 = (bf16[4,16,768]{2,1,0:T(8,128)(2,1)S(1)}, bf16[4,16,768]{2,1,0:T(8,128)(2,1)S(1)}, u32[]{:S(2)}, u32[]{:S(2)}) collective-permute-start(bf16[4,16,768]{2,1,0:T(8,128)(2,1)S(1)} %add_convert_fusion.3), channel_id=1, source_target_pairs={{0,64},{1,65},{2,66},{3,67},{4,68},{5,69},{6,70},{7,71},{8,72},{9,... | collective-permute-start | bytes 294920 | tf_op jit(solution)/shard_map/ppermute | solution.py:27
  466.7 4.8 collective-permute-start.59
  471.6 5.6 collective-permute-done.60.far
  492.0 9.8 %collective-permute-done.66 = bf16[4,16,3072]{2,1,0:T(8,128)(2,1)S(1)} collective-permute-done((bf16[4,16,3072]{2,1,0:T(8,128)(2,1)S(1)}, bf16[4,16,3072]{2,1,0:T(8,128)(2,1)S(1)}, u32[]{:S(2)}, u32[]{:S(2)}) %collective-permute-start.66) | collective-permute-done | bytes 393248 | tf_op jit(solution)/shard_map/ppermute | solution.py:27
  510.7 20.4 %collective-permute-done.67.high = bf16[2,4,16,3072]{3,2,1,0:T(8,128)(2,1)S(1)} collective-permute-done((bf16[2,4,16,3072]{3,2,1,0:T(8,128)(2,1)S(1)}, bf16[2,4,16,3072]{3,2,1,0:T(8,128)(2,1)S(1)}, u32[]{:S(2)}, u32[]{:S(2)}) %collective-permute-start.67) | collective-permute-done | bytes 786464 | tf_op jit(solution)/shard_map/ppermute | solution.py:27
  533.9 6.1 %collective-permute-done.65.refs_1_ = bf16[2,4,16,3584]{3,2,1,0:T(8,128)(2,1)S(1)} collective-permute-done((bf16[2,4,16,3584]{3,2,1,0:T(8,128)(2,1)S(1)}, bf16[2,4,16,3584]{3,2,1,0:T(8,128)(2,1)S(1)}, u32[]{:S(2)}, u32[]{:S(2)}) %collective-permute-start.65) | collective-permute-done | bytes 917536 | tf_op jit(solution)/shard_map/ppermute | solution.py:27
  540.0 7.7 %final_sums.1 = (f32[256,6144]{1,0:T(8,128)}, f32[1,1536]{1,0:T(1,128)S(1)}, f32[1,768]{1,0:T(1,128)S(1)}, f32[1,256]{1,0:T(1,128)}, f32[1,1024]{1,0:T(1,128)}, /*index=5*/f32[1,256]{1,0:T(1,128)}) custom-call(s32[1]{0:T(128)} %bitcast.row_ref.refs_0_, bf16[2,4,16,3584]{3,2,1,0:T(8,128)(2,1)S(1)} %pad_maximum_fusion.refs_0_, ...), custom_call_target="tpu_custom_call" | custom-call | flops 805306368 | bytes 10485760 | tf_op jit(solution)/shard_map/final_sums/pallas_call | solution.py:1146
  (351 shorter events, 163.7 us)
Async XLA Ops:
  7.2 447.4 %reduce-scatter.2.cloned.1.call-start = ((), (), s32[]{:S(2)}) async-start(), calls=%async_computation.1 | async-start | bytes 10027008 | tf_op jit(solution)/shard_map/reduce_scatter | solution.py:1300
  7.2 51.9 %collective-permute-start = (bf16[8,64,1024]{2,1,0:T(8,128)(2,1)}, bf16[8,64,1024]{2,1,0:T(8,128)(2,1)S(1)}, u32[]{:S(2)}, u32[]{:S(2)}) collective-permute-start(bf16[8,64,1024]{2,1,0:T(8,128)(2,1)} %x.3), channel_id=1, source_target_pairs={{0,2},{1,3},{2,0},{3,1},{4,6},{5,7},{6,4},{7,5},{8,10},{9,11},{10,... | collective-permute-start | bytes 3145736 | tf_op jit(solution)/shard_map/ppermute | solution.py:27
  10.4 48.8 %collective-permute-start.1 = (bf16[7,64,1024]{2,1,0:T(8,128)(2,1)}, bf16[7,64,1024]{2,1,0:T(8,128)(2,1)}, u32[]{:S(2)}, u32[]{:S(2)}) collective-permute-start(bf16[7,64,1024]{2,1,0:T(8,128)(2,1)} %slice.63), channel_id=1, source_target_pairs={{0,4},{1,5},{2,6},{3,7},{4,8},{5,9},{6,10},{7,11},{8,12},{9,13},{1... | collective-permute-start | bytes 2752520 | tf_op jit(solution)/shard_map/ppermute | solution.py:31
  12.6 25.0 %collective-permute-start.5 = (bf16[2,256,768]{2,1,0:T(8,128)(2,1)S(1)}, bf16[2,256,768]{2,1,0:T(8,128)(2,1)S(1)}, u32[]{:S(2)}, u32[]{:S(2)}) collective-permute-start(bf16[2,256,768]{2,1,0:T(8,128)(2,1)S(1)} %get-tuple-element.163), channel_id=1, source_target_pairs={{0,66},{1,67},{2,64},{3,65},{4,70},{5,71},{6,68},{7,69},{8,74},{9,... | collective-permute-start | bytes 2359304 | tf_op jit(solution)/shard_map/ppermute | solution.py:27
  16.5 21.1 %collective-permute-start.4 = (bf16[256,768]{1,0:T(8,128)(2,1)S(1)}, bf16[256,768]{1,0:T(8,128)(2,1)S(1)}, u32[]{:S(2)}, u32[]{:S(2)}) collective-permute-start(bf16[256,768]{1,0:T(8,128)(2,1)S(1)} %get-tuple-element.162), channel_id=1, source_target_pairs={{0,1},{1,0},{2,3},{3,2},{4,5},{5,4},{6,7},{7,6},{8,9},{9,8},{10,11... | collective-permute-start | bytes 1179656 | tf_op jit(solution)/shard_map/ppermute | solution.py:27
  18.0 19.5 %collective-permute-start.3 = (f32[8,7424]{1,0:T(8,128)S(1)}, f32[8,7424]{1,0:T(8,128)S(1)}, u32[]{:S(2)}, u32[]{:S(2)}) collective-permute-start(f32[8,7424]{1,0:T(8,128)S(1)} %add.88), channel_id=1, source_target_pairs={{0,2},{1,3},{2,0},{3,1},{4,6},{5,7},{6,4},{7,5},{8,10},{9,11},{10,... | collective-permute-start | bytes 712712 | tf_op jit(solution)/shard_map/ppermute | solution.py:27
  37.5 22.9 %collective-permute-start.7 = (bf16[8,64,1024]{2,1,0:T(8,128)(2,1)S(1)}, bf16[8,64,1024]{2,1,0:T(8,128)(2,1)S(1)}, u32[]{:S(2)}, u32[]{:S(2)}) collective-permute-start(bf16[8,64,1024]{2,1,0:T(8,128)(2,1)S(1)} %copy-done.3), channel_id=1, source_target_pairs={{0,1},{1,0},{2,3},{3,2},{4,5},{5,4},{6,7},{7,6},{8,9},{9,8},{10,11... | collective-permute-start | bytes 3145736 | tf_op jit(solution)/shard_map/ppermute | solution.py:27
  59.2 28.6 %collective-permute-start.6 = (bf16[7,64,1024]{2,1,0:T(8,128)(2,1)}, bf16[7,64,1024]{2,1,0:T(8,128)(2,1)S(1)}, u32[]{:S(2)}, u32[]{:S(2)}) collective-permute-start(bf16[7,64,1024]{2,1,0:T(8,128)(2,1)} %collective-permute-done.1.refs_1_), channel_id=1, source_target_pairs={{0,2},{1,3},{2,0},{3,1},{4,6},{5,7},{6,4},{7,5},{8,10},{9,11},{10,... | collective-permute-start | bytes 2752520 | tf_op jit(solution)/shard_map/ppermute | solution.py:27
  60.4 27.3 %collective-permute-start.10 = (f32[8,2048]{1,0:T(8,128)S(1)}, f32[8,2048]{1,0:T(8,128)S(1)}, u32[]{:S(2)}, u32[]{:S(2)}) collective-permute-start(f32[8,2048]{1,0:T(8,128)S(1)} %slice.66), channel_id=1, source_target_pairs={{0,4},{1,5},{2,6},{3,7},{4,8},{5,9},{6,10},{7,11},{8,12},{9,13},{1... | collective-permute-start | bytes 196616 | tf_op jit(solution)/shard_map/ppermute | solution.py:31
  60.5 77.3 %collective-permute-start.18 = (bf16[256,4096]{1,0:T(8,128)(2,1)}, bf16[256,4096]{1,0:T(8,128)(2,1)}, u32[]{:S(2)}, u32[]{:S(2)}) collective-permute-start(bf16[256,4096]{1,0:T(8,128)(2,1)} %u0.1), channel_id=1, source_target_pairs={{0,66},{1,67},{2,64},{3,65},{4,70},{5,71},{6,68},{7,69},{8,74},{9,... | collective-permute-start | bytes 6291464 | tf_op jit(solution)/shard_map/ppermute | solution.py:27
  87.8 49.9 %collective-permute-start.19 = (bf16[1024,1024]{1,0:T(8,128)(2,1)}, bf16[1024,1024]{1,0:T(8,128)(2,1)}, u32[]{:S(2)}, u32[]{:S(2)}) collective-permute-start(bf16[1024,1024]{1,0:T(8,128)(2,1)} %da.1), channel_id=1, source_target_pairs={{0,2},{1,3},{2,0},{3,1},{4,6},{5,7},{6,4},{7,5},{8,10},{9,11},{10,... | collective-permute-start | bytes 6291464 | tf_op jit(solution)/shard_map/ppermute | solution.py:27
  89.2 49.2 %collective-permute-start.16 = (bf16[256,1024]{1,0:T(8,128)(2,1)S(1)}, bf16[256,1024]{1,0:T(8,128)(2,1)S(1)}, u32[]{:S(2)}, u32[]{:S(2)}) collective-permute-start(bf16[256,1024]{1,0:T(8,128)(2,1)S(1)} %copy-done.13), channel_id=1, source_target_pairs={{0,1},{1,0},{2,3},{3,2},{4,5},{5,4},{6,7},{7,6},{8,9},{9,8},{10,11... | collective-permute-start | bytes 1572872 | tf_op jit(solution)/shard_map/ppermute | solution.py:27
  92.6 44.5 %collective-permute-start.17 = (bf16[256,1024]{1,0:T(8,128)(2,1)S(1)}, bf16[256,1024]{1,0:T(8,128)(2,1)S(1)}, u32[]{:S(2)}, u32[]{:S(2)}) collective-permute-start(bf16[256,1024]{1,0:T(8,128)(2,1)S(1)} %copy-done.13), channel_id=1, source_target_pairs={{0,66},{1,67},{2,64},{3,65},{4,70},{5,71},{6,68},{7,69},{8,74},{9,... | collective-permute-start | bytes 1572872 | tf_op jit(solution)/shard_map/ppermute | solution.py:27
  94.7 70.3 %collective-permute-start.21 = (bf16[256,4096]{1,0:T(8,128)(2,1)}, bf16[256,4096]{1,0:T(8,128)(2,1)}, u32[]{:S(2)}, u32[]{:S(2)}) collective-permute-start(bf16[256,4096]{1,0:T(8,128)(2,1)} %u0.1), channel_id=1, source_target_pairs={{0,1},{1,0},{2,3},{3,2},{4,5},{5,4},{6,7},{7,6},{8,9},{9,8},{10,11... | collective-permute-start | bytes 6291464 | tf_op jit(solution)/shard_map/ppermute | solution.py:27
  137.1 28.0 %collective-permute-start.23 = (bf16[1024,1024]{1,0:T(8,128)(2,1)}, bf16[1024,1024]{1,0:T(8,128)(2,1)S(1)}, u32[]{:S(2)}, u32[]{:S(2)}) collective-permute-start(bf16[1024,1024]{1,0:T(8,128)(2,1)} %da.1), channel_id=1, source_target_pairs={{0,1},{1,0},{2,3},{3,2},{4,5},{5,4},{6,7},{7,6},{8,9},{9,8},{10,11... | collective-permute-start | bytes 6291464 | tf_op jit(solution)/shard_map/ppermute | solution.py:27
  137.7 27.3 %collective-permute-start.22 = (bf16[256,4096]{1,0:T(8,128)(2,1)}, bf16[256,4096]{1,0:T(8,128)(2,1)S(1)}, u32[]{:S(2)}, u32[]{:S(2)}) collective-permute-start(bf16[256,4096]{1,0:T(8,128)(2,1)} %collective-permute-done.18.u2), channel_id=1, source_target_pairs={{0,1},{1,0},{2,3},{3,2},{4,5},{5,4},{6,7},{7,6},{8,9},{9,8},{10,11... | collective-permute-start | bytes 6291464 | tf_op jit(solution)/shard_map/ppermute | solution.py:27
  138.0 27.1 %collective-permute-start.24 = (bf16[1024,1024]{1,0:T(8,128)(2,1)}, bf16[1024,1024]{1,0:T(8,128)(2,1)S(1)}, u32[]{:S(2)}, u32[]{:S(2)}) collective-permute-start(bf16[1024,1024]{1,0:T(8,128)(2,1)} %collective-permute-done.19.d2.db), channel_id=1, source_target_pairs={{0,1},{1,0},{2,3},{3,2},{4,5},{5,4},{6,7},{7,6},{8,9},{9,8},{10,11... | collective-permute-start | bytes 6291464 | tf_op jit(solution)/shard_map/ppermute | solution.py:27
  219.5 34.0 %collective-permute-start.28 = (bf16[2,4,256,1024]{3,2,1,0:T(8,128)(2,1)}, bf16[2,4,256,1024]{3,2,1,0:T(8,128)(2,1)S(1)}, u32[]{:S(2)}, u32[]{:S(2)}) collective-permute-start(bf16[2,4,256,1024]{3,2,1,0:T(8,128)(2,1)} %get-tuple-element.209), channel_id=1, source_target_pairs={{0,1},{1,0},{2,3},{3,2},{4,5},{5,4},{6,7},{7,6},{8,9},{9,8},{10,11... | collective-permute-start | bytes 12582920 | tf_op jit(solution)/shard_map/ppermute | solution.py:27
  236.3 34.5 %collective-permute-start.34 = (bf16[2,1024,1024]{2,1,0:T(8,128)(2,1)S(1)}, bf16[2,1024,1024]{2,1,0:T(8,128)(2,1)}, u32[]{:S(2)}, u32[]{:S(2)}) collective-permute-start(bf16[2,1024,1024]{2,1,0:T(8,128)(2,1)S(1)} %get-tuple-element.218), channel_id=1, source_target_pairs={{0,1},{1,0},{2,3},{3,2},{4,5},{5,4},{6,7},{7,6},{8,9},{9,8},{10,11... | collective-permute-start | bytes 12582920 | tf_op jit(solution)/shard_map/ppermute | solution.py:27
  236.4 17.1 %collective-permute-start.29 = (bf16[2,8,64,256]{3,2,1,0:T(8,128)(2,1)S(1)}, bf16[2,8,64,256]{3,2,1,0:T(8,128)(2,1)S(1)}, u32[]{:S(2)}, u32[]{:S(2)}) collective-permute-start(bf16[2,8,64,256]{3,2,1,0:T(8,128)(2,1)S(1)} %copy-done.61), channel_id=1, source_target_pairs={{0,2},{1,3},{2,0},{3,1},{4,6},{5,7},{6,4},{7,5},{8,10},{9,11},{10,... | collective-permute-start | bytes 1572872 | tf_op jit(solution)/shard_map/ppermute | solution.py:27
  286.6 262.3 %all-gather.2.cloned.1.call-start = ((), (), s32[]{:S(2)}) async-start(), calls=%async_computation.2 | async-start | bytes 5013504 | tf_op jit(solution)/shard_map/all_gather | solution.py:1346
  306.1 50.6 %collective-permute-start.37 = (bf16[2,7,256,256]{3,2,1,0:T(8,128)(2,1)}, bf16[2,7,256,256]{3,2,1,0:T(8,128)(2,1)S(1)}, u32[]{:S(2)}, u32[]{:S(2)}) collective-permute-start(bf16[2,7,256,256]{3,2,1,0:T(8,128)(2,1)} %get-tuple-element.250), channel_id=1, source_target_pairs={{0,124},{1,125},{2,126},{3,127},{4,0},{5,1},{6,2},{7,3},{8,4},{9,5... | collective-permute-start | bytes 5505032 | tf_op jit(solution)/shard_map/ppermute | solution.py:31
  370.4 21.6 %collective-permute-start.40 = (bf16[8,8,4096]{2,1,0:T(8,128)(2,1)}, bf16[8,8,4096]{2,1,0:T(8,128)(2,1)}, u32[]{:S(2)}, u32[]{:S(2)}) collective-permute-start(bf16[8,8,4096]{2,1,0:T(8,128)(2,1)} %join.1.refs_2_), channel_id=1, source_target_pairs={{0,4},{1,5},{2,6},{3,7},{4,0},{5,1},{6,2},{7,3},{8,12},{9,13},{10,... | collective-permute-start | bytes 1572872 | tf_op jit(solution)/shard_map/ppermute | solution.py:27
  370.4 35.6 %collective-permute-start.41 = (bf16[8,8,4096]{2,1,0:T(8,128)(2,1)}, bf16[8,8,4096]{2,1,0:T(8,128)(2,1)}, u32[]{:S(2)}, u32[]{:S(2)}) collective-permute-start(bf16[8,8,4096]{2,1,0:T(8,128)(2,1)} %join.1.refs_2_), channel_id=1, source_target_pairs={{0,8},{1,9},{2,10},{3,11},{4,12},{5,13},{6,14},{7,15},{8,0},{9,1},... | collective-permute-start | bytes 1572872 | tf_op jit(solution)/shard_map/ppermute | solution.py:27
  372.6 34.4 %collective-permute-start.42 = (bf16[8,8,4096]{2,1,0:T(8,128)(2,1)}, bf16[8,8,4096]{2,1,0:T(8,128)(2,1)}, u32[]{:S(2)}, u32[]{:S(2)}) collective-permute-start(bf16[8,8,4096]{2,1,0:T(8,128)(2,1)} %join.1.refs_2_), channel_id=1, source_target_pairs={{0,12},{1,13},{2,14},{3,15},{4,8},{5,9},{6,10},{7,11},{8,4},{9,5},... | collective-permute-start | bytes 1572872 | tf_op jit(solution)/shard_map/ppermute | solution.py:27
  376.5 36.6 %collective-permute-start.39 = (bf16[8,64,1024]{2,1,0:T(8,128)(2,1)}, bf16[8,64,1024]{2,1,0:T(8,128)(2,1)}, u32[]{:S(2)}, u32[]{:S(2)}) collective-permute-start(bf16[8,64,1024]{2,1,0:T(8,128)(2,1)} %fusion), channel_id=1, source_target_pairs={{0,2},{1,3},{2,0},{3,1},{4,6},{5,7},{6,4},{7,5},{8,10},{9,11},{10,... | collective-permute-start | bytes 3145736 | tf_op jit(solution)/shard_map/ppermute | solution.py:27
  408.2 16.3 %collective-permute-start.43 = (bf16[4,64,768]{2,1,0:T(8,128)(2,1)}, bf16[4,64,768]{2,1,0:T(8,128)(2,1)}, u32[]{:S(2)}, u32[]{:S(2)}) collective-permute-start(bf16[4,64,768]{2,1,0:T(8,128)(2,1)} %get-tuple-element.305), channel_id=1, source_target_pairs={{0,4},{1,5},{2,6},{3,7},{4,0},{5,1},{6,2},{7,3},{8,12},{9,13},{10,... | collective-permute-start | bytes 1179656 | tf_op jit(solution)/shard_map/ppermute | solution.py:27
  408.2 27.5 %collective-permute-start.44 = (bf16[4,64,768]{2,1,0:T(8,128)(2,1)}, bf16[4,64,768]{2,1,0:T(8,128)(2,1)}, u32[]{:S(2)}, u32[]{:S(2)}) collective-permute-start(bf16[4,64,768]{2,1,0:T(8,128)(2,1)} %get-tuple-element.304), channel_id=1, source_target_pairs={{0,8},{1,9},{2,10},{3,11},{4,12},{5,13},{6,14},{7,15},{8,0},{9,1},... | collective-permute-start | bytes 1179656 | tf_op jit(solution)/shard_map/ppermute | solution.py:27
  410.4 27.6 %collective-permute-start.45 = (bf16[4,64,768]{2,1,0:T(8,128)(2,1)}, bf16[4,64,768]{2,1,0:T(8,128)(2,1)}, u32[]{:S(2)}, u32[]{:S(2)}) collective-permute-start(bf16[4,64,768]{2,1,0:T(8,128)(2,1)} %get-tuple-element.303), channel_id=1, source_target_pairs={{0,12},{1,13},{2,14},{3,15},{4,8},{5,9},{6,10},{7,11},{8,4},{9,5},... | collective-permute-start | bytes 1179656 | tf_op jit(solution)/shard_map/ppermute | solution.py:27
  420.3 24.0 %collective-permute-start.46 = (f32[8,3584]{1,0:T(8,128)S(1)}, f32[8,3584]{1,0:T(8,128)S(1)}, u32[]{:S(2)}, u32[]{:S(2)}) collective-permute-start(f32[8,3584]{1,0:T(8,128)S(1)} %get-tuple-element.263), channel_id=1, source_target_pairs={{0,1},{1,0},{2,3},{3,2},{4,5},{5,4},{6,7},{7,6},{8,9},{9,8},{10,11... | collective-permute-start | bytes 344072 | tf_op jit(solution)/shard_map/ppermute | solution.py:27
  501.9 29.3 %collective-permute-start.67 = (bf16[2,4,16,3072]{3,2,1,0:T(8,128)(2,1)S(1)}, bf16[2,4,16,3072]{3,2,1,0:T(8,128)(2,1)S(1)}, u32[]{:S(2)}, u32[]{:S(2)}) collective-permute-start(bf16[2,4,16,3072]{3,2,1,0:T(8,128)(2,1)S(1)} %pad_maximum_fusion.1.low), channel_id=1, source_target_pairs={{0,12},{1,13},{2,14},{3,15},{4,8},{5,9},{6,10},{7,11},{8,4},{9,5},... | collective-permute-start | bytes 2359304 | tf_op jit(solution)/shard_map/ppermute | solution.py:27
  504.2 35.8 %collective-permute-start.65 = (bf16[2,4,16,3584]{3,2,1,0:T(8,128)(2,1)S(1)}, bf16[2,4,16,3584]{3,2,1,0:T(8,128)(2,1)S(1)}, u32[]{:S(2)}, u32[]{:S(2)}) collective-permute-start(bf16[2,4,16,3584]{3,2,1,0:T(8,128)(2,1)S(1)} %pad_maximum_fusion.refs_0_), channel_id=1, source_target_pairs={{0,4},{1,5},{2,6},{3,7},{4,0},{5,1},{6,2},{7,3},{8,12},{9,13},{10,... | collective-permute-start | bytes 2752520 | tf_op jit(solution)/shard_map/ppermute | solution.py:27
  (125 other events, 1765.0 us)
Sparse Core Ops, SparseCore 0:
  286.0 155.6 reduce-scatter.1
  478.2 65.7 all-gather.1
where the time goes:
time: 573 us; the launch traced here: 562 us
  Pallas kernels  210 us (37%)
  waiting for transfers between devices  209 us (36%)
  starting transfers between devices  68.2 us (12%)
  local copies, waits for them, and re-layouts  52 us (9%)
  between operations  15.6 us (3%)
  other arithmetic  7 us (1%)
    ppermute x65, waiting for transfers between devices, swap(): return lax.ppermute(value, AXES, [(i, i ^ mask) for i in range(128)])  158 us
    ppermute x65, starting transfers between devices, swap(): return lax.ppermute(value, AXES, [(i, i ^ mask) for i in range(128)])  66.5 us
    pallas_call x2, Pallas kernels, attend_back(): pl.pallas_call(lambda *refs: attend_back_kernel(own, *refs), out_shape=[s...  51.6 us
    ppermute x3, waiting for transfers between devices, shift(): lax.ppermute(value, AXES, [(i, (i + 4 * steps) % 128) for i in range(128)])  51.1 us
    unnamed x174, local copies, waits for them, and re-layouts  45.8 us
    pallas_call x1, Pallas kernels, attend(): pl.pallas_call(attend_kernel, out_shape=[shape((FPD, PR, HC))] * 2 + [sha...  32.3 us
    pallas_call x1, Pallas kernels, feed(): pl.pallas_call(feed_kernel, out_shape=[shape((TOKENS, FF)), shape((TOKENS...  26.9 us
    pallas_call x2, Pallas kernels, project(): pl.pallas_call(lambda *refs: project_kernel(own, *refs), out_shape=out_sh...  18.1 us
  transfers between devices with their start and end apart: 70, of which 36 were waited for; matrix products, arithmetic and copies ran while one was open for 2% of the time, Pallas kernels for 29%

commit v1 on v0

--- a/solution.py
+++ b/solution.py
@@ -300,97 +300,155 @@
     return lax.broadcasted_iota(jnp.int32, (TOK, HC), 1) // HD
 
 
-def attend_kernel(pos_ref, q, k, v, kp, vp, o0, o1, o23, lse, qs, scores, acc, top, low):
-    f = pl.program_id(0)
-    place = pos_ref[f]
+def spread_queries(q, qs):
     lanes = head_lanes()
     query = q[0]
     for h in range(4):
         qs[pl.ds(h * TOK, TOK), :] = jnp.where(lanes == h, query, jnp.zeros_like(query))
-    top[...] = jnp.full_like(top, -1e30)
-    low[...] = jnp.zeros_like(low)
-    acc[...] = jnp.zeros_like(acc)
-    before = jnp.maximum(place - f, 0)
-    start = jnp.maximum(f - place, 0)
-
-    def score(keys, slot):
+
+
+def sweep_scores(low_at, high_at, k, qs, scores, top):
+    def one(at, _):
+        keys = k[at]
         for h in range(4):
             rows = pl.ds(h * TOK, TOK)
             s = nt(qs[rows, :], keys)
-            scores[slot, rows, :] = s
+            scores[at - low_at, rows, :] = s
             top[rows, :] = jnp.maximum(top[rows, :], jnp.maximum(s[:, :128], s[:, 128:]))
-
-    def mix(values, slot):
-        for h in range(4):
-            rows = pl.ds(h * TOK, TOK)
-            p = jnp.exp(scores[slot, rows, :] - jnp.concatenate([top[rows, :]] * 2, axis=1))
-            low[rows, :] = low[rows, :] + (p[:, :128] + p[:, 128:])
-            acc[rows, :] = acc[rows, :] + nn(p.astype(BF16), values)
-
-    def run(step):
-        def prev(i, _):
-            at = PREV - before + i
-            step(kp[at] if step is score else vp[at], i)
-            return 0
-
-        def own(g, _):
-            step(k[g] if step is score else v[g], g - f + place)
-            return 0
-
-        lax.fori_loop(0, before, prev, 0)
-        lax.fori_loop(start, f + 1, own, 0)
-
-    run(score)
+        return 0
+
+    lax.fori_loop(low_at, high_at, one, 0)
     for h in range(4):
         rows = pl.ds(h * TOK, TOK)
         top[rows, :] = jnp.broadcast_to(jnp.max(top[rows, :], axis=1, keepdims=True), (TOK, 128))
-    run(mix)
+
+
+def sweep_values(low_at, high_at, v, scores, top, low, acc):
+    low[...] = jnp.zeros_like(low)
+    acc[...] = jnp.zeros_like(acc)
+
+    def one(at, _):
+        values = v[at]
+        for h in range(4):
+            rows = pl.ds(h * TOK, TOK)
+            p = jnp.exp(scores[at - low_at, rows, :] - jnp.concatenate([top[rows, :]] * 2, axis=1))
+            low[rows, :] = low[rows, :] + (p[:, :128] + p[:, 128:])
+            acc[rows, :] = acc[rows, :] + nn(p.astype(BF16), values)
+        return 0
+
+    lax.fori_loop(low_at, high_at, one, 0)
+
+
+def attend_own_kernel(pos_ref, q, k, v, mixed, stats, qs, scores, acc, top, low):
+    f = pl.program_id(0)
+    start = jnp.maximum(f - pos_ref[f], 0)
+    spread_queries(q, qs)
+    top[...] = jnp.full_like(top, -1e30)
+    sweep_scores(start, f + 1, k, qs, scores, top)
+    sweep_values(start, f + 1, v, scores, top, low, acc)
+    lanes = head_lanes()
+    narrow = lax.broadcasted_iota(jnp.int32, (TOK, 128), 1)
     result = jnp.zeros((TOK, HC), F32)
-    logs = jnp.zeros((TOK, 128), F32)
-    narrow = lax.broadcasted_iota(jnp.int32, (TOK, 128), 1)
+    state = jnp.zeros((TOK, 128), F32)
     for h in range(4):
         rows = pl.ds(h * TOK, TOK)
-        total = jnp.sum(low[rows, :], axis=1, keepdims=True)
-        result = jnp.where(lanes == h, acc[rows, :] / total, result)
-        logs = jnp.where(narrow == h, top[rows, :] + jnp.log(total), logs)
-    lse[0] = logs.T[:8]
-    result = result.astype(BF16)
-    o0[0] = result[:PR]
-    o1[0] = result[PR : 2 * PR]
-    o23[0, 0] = result[2 * PR : 3 * PR]
-    o23[1, 0] = result[3 * PR :]
-
-
-def attend(places, q, k, v, kp, vp):
+        result = jnp.where(lanes == h, acc[rows, :], result)
+        state = jnp.where(narrow == h, top[rows, :], state)
+        state = jnp.where(narrow == 4 + h, jnp.sum(low[rows, :], axis=1, keepdims=True), state)
+    mixed[0] = result
+    stats[0] = state
+
+
+def attend_prev_kernel(
+    pos_ref, q, k, v, mixed, stats, o0, o1, o23, lse, qs, scores, acc, top, low, result, logs
+):
+    f = pl.program_id(0)
+    count = jnp.maximum(pos_ref[f] - f, 0)
+    lanes = head_lanes()
+    narrow = lax.broadcasted_iota(jnp.int32, (TOK, 128), 1)
+    state = stats[0]
+
+    def finish(part):
+        total_mixed = jnp.zeros((TOK, HC), F32)
+        total_logs = jnp.zeros((TOK, 128), F32)
+        for h in range(4):
+            largest, total, value = part(h, state[:, h : h + 1], state[:, 4 + h : 5 + h])
+            total_mixed = jnp.where(lanes == h, value / total, total_mixed)
+            total_logs = jnp.where(narrow == h, largest + jnp.log(total), total_logs)
+        result[...] = total_mixed.astype(BF16)
+        logs[...] = total_logs
+
+    @pl.when(count == 0)
+    def _():
+        finish(lambda h, largest, total: (largest, total, mixed[0]))
+
+    @pl.when(count > 0)
+    def _():
+        spread_queries(q, qs)
+        for h in range(4):
+            top[pl.ds(h * TOK, TOK), :] = jnp.broadcast_to(state[:, h : h + 1], (TOK, 128))
+        sweep_scores(PREV - count, PREV, k, qs, scores, top)
+        sweep_values(PREV - count, PREV, v, scores, top, low, acc)
+
+        def part(h, largest, total):
+            rows = pl.ds(h * TOK, TOK)
+            most = top[rows, :1]
+            fade = jnp.exp(largest - most)
+            total = total * fade + jnp.sum(low[rows, :], axis=1, keepdims=True)
+            return most, total, mixed[0] * fade + acc[rows, :]
+
+        finish(part)
+
+    lse[0] = logs[...].T[:8]
+    o0[0] = result[:PR, :]
+    o1[0] = result[PR : 2 * PR, :]
+    o23[0, 0] = result[2 * PR : 3 * PR, :]
+    o23[1, 0] = result[3 * PR :, :]
+
+
+def attend(own, places, q, k, v, state=()):
     block = pl.BlockSpec((1, TOK, HC), lambda f, *_: (f, 0, 0))
+    narrow = pl.BlockSpec((1, TOK, 128), lambda f, *_: (f, 0, 0))
     piece = pl.BlockSpec((1, PR, HC), lambda f, *_: (f, 0, 0))
-    return pl.pallas_call(
-        attend_kernel,
-        out_shape=[shape((FPD, PR, HC))] * 2
-        + [shape((2, FPD, PR, HC)), shape((FPD, 8, TOK), F32)],
+    count = FPD if own else PREV
+    scratch = [
+        pltpu.VMEM((4 * TOK, HC), BF16),
+        pltpu.VMEM((8, 4 * TOK, TOK), F32),
+        pltpu.VMEM((4 * TOK, HC), F32),
+        pltpu.VMEM((4 * TOK, 128), F32),
+        pltpu.VMEM((4 * TOK, 128), F32),
+    ]
+    specs = [block] + [whole((count, TOK, HC))] * 2
+    if own:
+        out_shape = [shape((FPD, TOK, HC), F32), shape((FPD, TOK, 128), F32)]
+        out_specs = [block, narrow]
+    else:
+        specs += [block, narrow]
+        out_shape = [shape((FPD, PR, HC))] * 2 + [
+            shape((2, FPD, PR, HC)),
+            shape((FPD, 8, TOK), F32),
+        ]
+        out_specs = [piece] * 2 + [
+            pl.BlockSpec((2, 1, PR, HC), lambda f, *_: (0, f, 0, 0)),
+            pl.BlockSpec((1, 8, TOK), lambda f, *_: (f, 0, 0)),
+        ]
+        scratch += [pltpu.VMEM((TOK, HC), BF16), pltpu.VMEM((TOK, 128), F32)]
+    return pl.pallas_call(
+        attend_own_kernel if own else attend_prev_kernel,
+        out_shape=out_shape,
         grid_spec=pltpu.PrefetchScalarGridSpec(
             num_scalar_prefetch=1,
             grid=(FPD,),
-            in_specs=[block]
-            + [whole((FPD, TOK, HC))] * 2
-            + [whole((PREV, TOK, HC))] * 2,
-            out_specs=[piece] * 2
-            + [
-                pl.BlockSpec((2, 1, PR, HC), lambda f, *_: (0, f, 0, 0)),
-                pl.BlockSpec((1, 8, TOK), lambda f, *_: (f, 0, 0)),
-            ],
-            scratch_shapes=[
-                pltpu.VMEM((4 * TOK, HC), BF16),
-                pltpu.VMEM((8, 4 * TOK, TOK), F32),
-                pltpu.VMEM((4 * TOK, HC), F32),
-                pltpu.VMEM((4 * TOK, 128), F32),
-                pltpu.VMEM((4 * TOK, 128), F32),
-            ],
+            in_specs=specs,
+            out_specs=out_specs,
+            scratch_shapes=scratch,
         ),
-        compiler_params=params(58),
-        cost_estimate=cost(36 * 4 * 2 * 2 * TOK**3, 6 * MB, 36 * 4 * TOK * TOK),
-        name="attend",
-    )(places, q, k, v, kp, vp)
+        compiler_params=params(40),
+        cost_estimate=cost(
+            (30 if own else 12) * 4 * 2 * 2 * TOK**3, 6 * MB, 30 * 4 * TOK * TOK
+        ),
+        name="attend_own" if own else "attend_prev",
+    )(places, q, k, v, *state)
 
 
 def attend_back_kernel(own, pos_ref, q, k, v, g0, g1, g2, g3, o0, o1, o23, lse, *rest):
@@ -1249,13 +1307,15 @@
     ups2 = swap(up_own, OTHER)
 
     hidden1, q, k, v = project(True, row_arg, (x0, x1, x2, x3), table, table, qkv_pieces, tables)
-    p2, down_own, q, before_mods = lax.optimization_barrier((p2, down_weight, q, before_mods))
+    down_own, q, before_mods = lax.optimization_barrier((down_weight, q, before_mods))
+    downs2 = swap(down_own, DIRECT)
+    state = attend(True, frame_position, q, k, v)
+    p2, *state = lax.optimization_barrier((p2, *state))
     p3 = swap(p2, CORE)
-    downs2 = swap(down_own, DIRECT)
     kp, vp = project(
         False, row_arg, (p0, p1, p2, p3), table, before_mods, qkv_pieces, tables
     )
-    *mixed, lse = attend(frame_position, q, k, v, kp, vp)
+    *mixed, lse = attend(False, frame_position, q, kp, vp, state)
     outs2, ups2, downs2, lse = lax.optimization_barrier((outs2, ups2, downs2, lse))
     outs = [out_weight, swap(out_own, CORE), outs2, swap(outs2, CORE)]
     ups = [up_weight, swap(up_own, CORE), ups2, swap(ups2, CORE)]

time: 573 us -> 576 us (level)
  Pallas kernels: 210 us -> 193 us
  starting transfers between devices: 68.2 us -> 83.5 us
  waiting for transfers between devices: 209 us -> 219 us
    ppermute x65, starting transfers between devices: 66.5 us -> 77.3 us  [swap(): return lax.ppermute(value, AXES, [(i, i ^ mask) for i in range(128)])]
    pallas_call x2, Pallas kernels: 51.6 us -> 41 us  [attend_back(): pl.pallas_call(lambda *refs: attend_back_kernel(own, *refs), out_shape=[s...]
    ppermute x3, waiting for transfers between devices: 51.1 us -> 59 us  [shift(): lax.ppermute(value, AXES, [(i, (i + 4 * steps) % 128) for i in range(128)])]
    pallas_call x1 -> x2, Pallas kernels: 32.3 us -> 26.6 us  [attend(): pl.pallas_call(attend_own_kernel if own else attend_prev_kernel, out_shap...]
    unnamed x174 -> x190, local copies, waits for them, and re-layouts: 45.8 us -> 42.4 us
  transfers between devices with their start and end apart: 70 -> 70, of which waited for: 36 -> 38; matrix products, arithmetic and copies ran while one was open for 2% -> 2% of each run, Pallas kernels for 29% -> 26%
where the time goes in v1:
time: 576 us; the launch traced here: 568 us
  waiting for transfers between devices  219 us (38%)
  Pallas kernels  193 us (34%)
  starting transfers between devices  83.5 us (14%)
  local copies, waits for them, and re-layouts  48.5 us (8%)
  between operations  15.7 us (3%)
  other arithmetic  6.98 us (1%)
    ppermute x65, waiting for transfers between devices, swap(): return lax.ppermute(value, AXES, [(i, i ^ mask) for i in range(128)])  160 us
    ppermute x65, starting transfers between devices, swap(): return lax.ppermute(value, AXES, [(i, i ^ mask) for i in range(128)])  77.3 us
    ppermute x3, waiting for transfers between devices, shift(): lax.ppermute(value, AXES, [(i, (i + 4 * steps) % 128) for i in range(128)])  59 us
    unnamed x190, local copies, waits for them, and re-layouts  42.4 us
    pallas_call x2, Pallas kernels, attend_back(): pl.pallas_call(lambda *refs: attend_back_kernel(own, *refs), out_shape=[s...  41 us
    pallas_call x1, Pallas kernels, feed(): pl.pallas_call(feed_kernel, out_shape=[shape((TOKENS, FF)), shape((TOKENS...  26.9 us
    pallas_call x2, Pallas kernels, attend(): pl.pallas_call(attend_own_kernel if own else attend_prev_kernel, out_shap...  26.6 us
    pallas_call x2, Pallas kernels, project(): pl.pallas_call(lambda *refs: project_kernel(own, *refs), out_shape=out_sh...  18.1 us
  transfers between devices with their start and end apart: 70, of which 38 were waited for; matrix products, arithmetic and copies ran while one was open for 2% of the time, Pallas kernels for 26%

profile of v1, /device:TPU:6, one launch (start us, length us, event | category | flops | bytes accessed | tf_op | source)
XLA Modules:
  0.0 567.7 jit_solution(13735767330184369293)
XLA Ops:
  19.2 18.3 %collective-permute-done.4 = f32[8,7424]{1,0:T(8,128)S(1)} collective-permute-done((f32[8,7424]{1,0:T(8,128)S(1)}, f32[8,7424]{1,0:T(8,128)S(1)}, u32[]{:S(2)}, u32[]{:S(2)}) %collective-permute-start.4) | collective-permute-done | bytes 237600 | tf_op jit(solution)/shard_map/ppermute | solution.py:27
  37.6 21.6 %collective-permute-done.2.refs_1_ = bf16[7,64,1024]{2,1,0:T(8,128)(2,1)} collective-permute-done((bf16[7,64,1024]{2,1,0:T(8,128)(2,1)}, bf16[7,64,1024]{2,1,0:T(8,128)(2,1)}, u32[]{:S(2)}, u32[]{:S(2)}) %collective-permute-start.2) | collective-permute-done | bytes 917536 | tf_op jit(solution)/shard_map/ppermute | solution.py:31
  65.7 9.9 %project_own.1 = (bf16[8,256,1024]{2,1,0:T(8,128)(2,1)S(1)}, bf16[8,256,256]{2,1,0:T(8,128)(2,1)S(1)}, bf16[8,256,256]{2,1,0:T(8,128)(2,1)S(1)}, bf16[8,256,256]{2,1,0:T(8,128)(2,1)S(1)}) custom-call(s32[1]{0:T(128)} %bitcast.row_ref.refs_0_, bf16[8,64,1024]{2,1,0:T(8,128)(2,1)S(1)} %copy-done.3, bf16[8,64,1024]{2,1,0:T(8,128)(2,1)S(1)} %collective-permute-done.refs_2_, ...), custom_call_target="tpu_custom_call" | custom-call | flops 3221225472 | bytes 12582912 | tf_op jit(solution)/shard_map/project_own/pallas_call | solution.py:280
  75.7 12.7 %collective-permute-done.9.refs_6_ = f32[8,2048]{1,0:T(8,128)S(1)} collective-permute-done((f32[8,2048]{1,0:T(8,128)S(1)}, f32[8,2048]{1,0:T(8,128)S(1)}, u32[]{:S(2)}, u32[]{:S(2)}) %collective-permute-start.9) | collective-permute-done | bytes 65568 | tf_op jit(solution)/shard_map/ppermute | solution.py:31
  89.3 17.0 %attend_own.1 = (f32[8,256,256]{2,1,0:T(8,128)S(1)}, f32[8,256,128]{2,1,0:T(8,128)S(1)}) custom-call(s32[8]{0:T(128)S(1)} %copy-done.50, bf16[8,256,256]{2,1,0:T(8,128)(2,1)S(1)} %get-tuple-element.177.q.refs_1_, bf16[8,256,256]{2,1,0:T(8,128)(2,1)S(1)} %get-tuple-element.179.k.refs_2_, bf16[8,256,256]{2,1,0:T(8,128)(2,1)S(1)} %get-tuple-element.180.v.refs_3_), custom_call_target="tpu_custom_call" | custom-call | flops 8053063680 | bytes 6291456 | tf_op jit(solution)/shard_map/attend_own/pallas_call | solution.py:436
  107.0 14.3 %collective-permute-start.17 = (bf16[256,1024]{1,0:T(8,128)(2,1)S(1)}, bf16[256,1024]{1,0:T(8,128)(2,1)S(1)}, u32[]{:S(2)}, u32[]{:S(2)}) collective-permute-start(bf16[256,1024]{1,0:T(8,128)(2,1)S(1)} %copy-done.13), channel_id=1, source_target_pairs={{0,66},{1,67},{2,64},{3,65},{4,70},{5,71},{6,68},{7,69},{8,74},{9,... | collective-permute-start | bytes 1572872 | tf_op jit(solution)/shard_map/ppermute | solution.py:27
  121.8 8.2 %project_prev.1 = (bf16[7,256,256]{2,1,0:T(8,128)(2,1)S(1)}, bf16[7,256,256]{2,1,0:T(8,128)(2,1)S(1)}) custom-call(s32[1]{0:T(128)} %bitcast.row_ref.refs_0_, bf16[7,64,1024]{2,1,0:T(8,128)(2,1)} %collective-permute-done.2.refs_1_, bf16[7,64,1024]{2,1,0:T(8,128)(2,1)S(1)} %collective-permute-done.10.refs_2_, ...), custom_call_target="tpu_custom_call" | custom-call | flops 2818572288 | bytes 11534336 | tf_op jit(solution)/shard_map/project_prev/pallas_call | solution.py:280
  130.1 9.7 %attend_prev.1 = (bf16[8,64,256]{2,1,0:T(8,128)(2,1)S(1)}, bf16[8,64,256]{2,1,0:T(8,128)(2,1)S(1)}, bf16[2,8,64,256]{3,2,1,0:T(8,128)(2,1)S(1)}, f32[8,8,256]{2,1,0:T(8,128)S(1)}) custom-call(s32[8]{0:T(128)S(1)} %copy-done.50, bf16[8,256,256]{2,1,0:T(8,128)(2,1)S(1)} %get-tuple-element.177.q.refs_1_, bf16[7,256,256]{2,1,0:T(8,128)(2,1)S(1)} %get-tuple-element.185.k.refs_2_, ...), custom_call_target="tpu_custom_call" | custom-call | flops 3221225472 | bytes 6291456 | tf_op jit(solution)/shard_map/attend_prev/pallas_call | solution.py:436
  142.2 12.7 %collective-permute-done.14 = bf16[2,8,64,256]{3,2,1,0:T(8,128)(2,1)S(1)} collective-permute-done((bf16[2,8,64,256]{3,2,1,0:T(8,128)(2,1)S(1)}, bf16[2,8,64,256]{3,2,1,0:T(8,128)(2,1)S(1)}, u32[]{:S(2)}, u32[]{:S(2)}) %collective-permute-start.14) | collective-permute-done | bytes 524320 | tf_op jit(solution)/shard_map/ppermute | solution.py:27
  169.4 26.9 %feed.1 = (bf16[512,4096]{1,0:T(8,128)(2,1)}, bf16[512,4096]{1,0:T(8,128)(2,1)}, f32[512,1024]{1,0:T(8,128)}, f32[8,512]{1,0:T(8,128)}) custom-call(s32[1]{0:T(128)} %bitcast.row_ref.refs_0_, bf16[512,1024]{1,0:T(8,128)(2,1)} %bitcast.70, bf16[512,1024]{1,0:T(8,128)(2,1)} %bitcast.67, bf16[256,4096]{1,0:T(8,128)(2,1)} %u0.1, bf16[256,4096]{1,0:T(8,128)(2,1)} %copy-done.91, ...), custom_call_target="tpu_custom_call" | custom-call | flops 12884901888 | bytes 31457280 | tf_op jit(solution)/shard_map/feed/pallas_call | solution.py:744
  210.3 10.8 %up_weight_grad.1 = (bf16[2,4,256,1024]{3,2,1,0:T(8,128)(2,1)}, bf16[2,4,256,1024]{3,2,1,0:T(8,128)(2,1)}) custom-call(s32[1]{0:T(128)} %bitcast.row_ref.refs_0_, bf16[512,1024]{1,0:T(8,128)(2,1)} %bitcast.71, bf16[512,4096]{1,0:T(8,128)(2,1)} %get-tuple-element.210.upg), custom_call_target="tpu_custom_call" | custom-call | flops 4294967296 | bytes 14680064 | tf_op jit(solution)/shard_map/up_weight_grad/pallas_call | solution.py:842
  231.5 6.6 %down_weight_send.1 = (bf16[2,1024,1024]{2,1,0:T(8,128)(2,1)S(1)}, f32[512,1024]{1,0:T(8,128)S(1)}) custom-call(bf16[512,1024]{1,0:T(8,128)(2,1)S(1)} %bitcast.68, bf16[512,4096]{1,0:T(8,128)(2,1)} %get-tuple-element.213.act, bf16[1024,1024]{1,0:T(8,128)(2,1)S(1)} %copy-done.56, bf16[1024,1024]{1,0:T(8,128)(2,1)S(1)} %copy-done.58), custom_call_target="tpu_custom_call" | custom-call | flops 4294967296 | bytes 14680064 | tf_op jit(solution)/shard_map/down_weight_send/pallas_call | solution.py:816
  239.9 5.8 %collective-permute-done.30.refs_5_ = bf16[8,64,256]{2,1,0:T(8,128)(2,1)S(1)} collective-permute-done((bf16[8,64,256]{2,1,0:T(8,128)(2,1)S(1)}, bf16[8,64,256]{2,1,0:T(8,128)(2,1)S(1)}, u32[]{:S(2)}, u32[]{:S(2)}) %collective-permute-start.30) | collective-permute-done | bytes 262176 | tf_op jit(solution)/shard_map/ppermute | solution.py:27
  245.7 7.1 %collective-permute-done.27 = bf16[8,4096]{1,0:T(8,128)(2,1)S(1)} collective-permute-done((bf16[8,4096]{1,0:T(8,128)(2,1)S(1)}, bf16[8,4096]{1,0:T(8,128)(2,1)S(1)}, u32[]{:S(2)}, u32[]{:S(2)}) %collective-permute-start.27) | collective-permute-done | bytes 65568 | tf_op jit(solution)/shard_map/ppermute | solution.py:27
  257.5 4.6 collective-permute-start.33
  262.1 8.4 %down_weight_keep.1 = (bf16[2,1024,1024]{2,1,0:T(8,128)(2,1)}, bf16[8,64,1024]{2,1,0:T(8,128)(2,1)}, f32[8,1024]{1,0:T(8,128)S(1)}) custom-call(bf16[512,1024]{1,0:T(8,128)(2,1)S(1)} %bitcast.69, bf16[512,4096]{1,0:T(8,128)(2,1)} %get-tuple-element.213.act, bf16[1024,1024]{1,0:T(8,128)(2,1)S(1)} %copy-done.52, bf16[1024,1024]{1,0:T(8,128)(2,1)S(1)} %copy-done.54, ...), custom_call_target="tpu_custom_call" | custom-call | flops 4294967296 | bytes 14680064 | tf_op jit(solution)/shard_map/down_weight_keep/pallas_call | solution.py:816
  274.2 12.0 %core_sum.1 = bf16[2,2304,1024]{2,1,0:T(8,128)(2,1)} custom-call(bf16[2,4,256,1024]{3,2,1,0:T(8,128)(2,1)} %get-tuple-element.234.ua, bf16[2,4,256,1024]{3,2,1,0:T(8,128)(2,1)} %copy-done.83, bf16[2,1024,1024]{2,1,0:T(8,128)(2,1)} %get-tuple-element.236.da, bf16[2,1024,1024]{2,1,0:T(8,128)(2,1)} %collective-permute-done.34.db, ...), custom_call_target="tpu_custom_call" | custom-call | flops 1000 | bytes 1000 | tf_op jit(solution)/shard_map/core_sum/pallas_call | solution.py:902
  286.9 13.5 %attend_back_prev.1 = (f32[8,256,256]{2,1,0:T(8,128)}, bf16[2,7,256,256]{3,2,1,0:T(8,128)(2,1)}) custom-call(s32[8]{0:T(128)} %refs_0_.3, bf16[8,256,256]{2,1,0:T(8,128)(2,1)} %copy-done.17, bf16[7,256,256]{2,1,0:T(8,128)(2,1)} %copy-done.81, bf16[7,256,256]{2,1,0:T(8,128)(2,1)} %copy-done.82, bf16[8,64,256]{2,1,0:T(8,128)(2,1)} %copy-done.34, ...), custom_call_target="tpu_custom_call" | custom-call | flops 8053063680 | bytes 12582912 | tf_op jit(solution)/shard_map/attend_back_prev/pallas_call | solution.py:548
  305.1 27.5 %attend_back_own.1 = (bf16[8,256,256]{2,1,0:T(8,128)(2,1)}, f32[8,256,256]{2,1,0:T(8,128)}, f32[8,256,256]{2,1,0:T(8,128)}) custom-call(s32[8]{0:T(128)} %refs_0_.3, bf16[8,256,256]{2,1,0:T(8,128)(2,1)} %copy-done.17, bf16[8,256,256]{2,1,0:T(8,128)(2,1)} %copy-done.18, bf16[8,256,256]{2,1,0:T(8,128)(2,1)} %copy-done.19, bf16[8,64,256]{2,1,0:T(8,128)(2,1)} %copy-done.34, ...), custom_call_target="tpu_custom_call" | custom-call | flops 1000 | bytes 1000 | tf_op jit(solution)/shard_map/attend_back_own/pallas_call | solution.py:548
  333.4 24.7 %collective-permute-done.37.rk.rv = bf16[2,7,256,256]{3,2,1,0:T(8,128)(2,1)S(1)} collective-permute-done((bf16[2,7,256,256]{3,2,1,0:T(8,128)(2,1)}, bf16[2,7,256,256]{3,2,1,0:T(8,128)(2,1)S(1)}, u32[]{:S(2)}, u32[]{:S(2)}) %collective-permute-start.37) | collective-permute-done | bytes 1835040 | tf_op jit(solution)/shard_map/ppermute | solution.py:31
  362.6 7.5 %project_back.1 = (bf16[8,256,768]{2,1,0:T(8,128)(2,1)S(1)}, bf16[8,64,1024]{2,1,0:T(8,128)(2,1)S(1)}, bf16[8,64,1024]{2,1,0:T(8,128)(2,1)S(1)}, bf16[2,8,64,1024]{3,2,1,0:T(8,128)(2,1)S(1)}, f32[8,512]{1,0:T(8,128)S(1)}) custom-call(s32[1]{0:T(128)} %bitcast.row_ref.refs_0_, bf16[8,256,256]{2,1,0:T(8,128)(2,1)S(1)} %copy-done.66, ...), custom_call_target="tpu_custom_call" | custom-call | flops 3221225472 | bytes 14680064 | tf_op jit(solution)/shard_map/project_back/pallas_call | solution.py:1055
  371.8 9.9 %collective-permute-start.41 = (bf16[8,8,4096]{2,1,0:T(8,128)(2,1)}, bf16[8,8,4096]{2,1,0:T(8,128)(2,1)}, u32[]{:S(2)}, u32[]{:S(2)}) collective-permute-start(bf16[8,8,4096]{2,1,0:T(8,128)(2,1)} %join.1.refs_2_), channel_id=1, source_target_pairs={{0,8},{1,9},{2,10},{3,11},{4,12},{5,13},{6,14},{7,15},{8,0},{9,1},... | collective-permute-start | bytes 1572872 | tf_op jit(solution)/shard_map/ppermute | solution.py:27
  388.0 4.8 project_weight.1
  396.7 14.4 %collective-permute-done.41.refs_4_ = bf16[8,8,4096]{2,1,0:T(8,128)(2,1)} collective-permute-done((bf16[8,8,4096]{2,1,0:T(8,128)(2,1)}, bf16[8,8,4096]{2,1,0:T(8,128)(2,1)}, u32[]{:S(2)}, u32[]{:S(2)}) %collective-permute-start.41) | collective-permute-done | bytes 524320 | tf_op jit(solution)/shard_map/ppermute | solution.py:27
  424.6 5.3 collective-permute-done.43
  429.9 13.0 %collective-permute-done.44 = bf16[4,64,768]{2,1,0:T(8,128)(2,1)} collective-permute-done((bf16[4,64,768]{2,1,0:T(8,128)(2,1)}, bf16[4,64,768]{2,1,0:T(8,128)(2,1)}, u32[]{:S(2)}, u32[]{:S(2)}) %collective-permute-start.44) | collective-permute-done | bytes 393248 | tf_op jit(solution)/shard_map/ppermute | solution.py:27
  470.0 4.9 collective-permute-start.59
  475.0 5.6 collective-permute-done.60.far
  495.3 9.8 %collective-permute-done.66 = bf16[4,16,3072]{2,1,0:T(8,128)(2,1)S(1)} collective-permute-done((bf16[4,16,3072]{2,1,0:T(8,128)(2,1)S(1)}, bf16[4,16,3072]{2,1,0:T(8,128)(2,1)S(1)}, u32[]{:S(2)}, u32[]{:S(2)}) %collective-permute-start.66) | collective-permute-done | bytes 393248 | tf_op jit(solution)/shard_map/ppermute | solution.py:27
  515.5 19.7 %collective-permute-done.67.high = bf16[2,4,16,3072]{3,2,1,0:T(8,128)(2,1)S(1)} collective-permute-done((bf16[2,4,16,3072]{3,2,1,0:T(8,128)(2,1)S(1)}, bf16[2,4,16,3072]{3,2,1,0:T(8,128)(2,1)S(1)}, u32[]{:S(2)}, u32[]{:S(2)}) %collective-permute-start.67) | collective-permute-done | bytes 786464 | tf_op jit(solution)/shard_map/ppermute | solution.py:27
  537.9 7.6 %collective-permute-done.65.refs_1_ = bf16[2,4,16,3584]{3,2,1,0:T(8,128)(2,1)S(1)} collective-permute-done((bf16[2,4,16,3584]{3,2,1,0:T(8,128)(2,1)S(1)}, bf16[2,4,16,3584]{3,2,1,0:T(8,128)(2,1)S(1)}, u32[]{:S(2)}, u32[]{:S(2)}) %collective-permute-start.65) | collective-permute-done | bytes 917536 | tf_op jit(solution)/shard_map/ppermute | solution.py:27
  545.5 7.7 %final_sums.1 = (f32[256,6144]{1,0:T(8,128)}, f32[1,1536]{1,0:T(1,128)S(1)}, f32[1,768]{1,0:T(1,128)S(1)}, f32[1,256]{1,0:T(1,128)}, f32[1,1024]{1,0:T(1,128)}, /*index=5*/f32[1,256]{1,0:T(1,128)}) custom-call(s32[1]{0:T(128)} %bitcast.row_ref.refs_0_, bf16[2,4,16,3584]{3,2,1,0:T(8,128)(2,1)S(1)} %pad_maximum_fusion.refs_0_, ...), custom_call_target="tpu_custom_call" | custom-call | flops 805306368 | bytes 10485760 | tf_op jit(solution)/shard_map/final_sums/pallas_call | solution.py:1204
  (368 shorter events, 169.6 us)
Async XLA Ops:
  7.2 450.7 %reduce-scatter.2.cloned.1.call-start = ((), (), s32[]{:S(2)}) async-start(), calls=%async_computation.1 | async-start | bytes 10027008 | tf_op jit(solution)/shard_map/reduce_scatter | solution.py:1360
  7.2 51.9 %collective-permute-start.1 = (bf16[8,64,1024]{2,1,0:T(8,128)(2,1)}, bf16[8,64,1024]{2,1,0:T(8,128)(2,1)S(1)}, u32[]{:S(2)}, u32[]{:S(2)}) collective-permute-start(bf16[8,64,1024]{2,1,0:T(8,128)(2,1)} %x.3), channel_id=1, source_target_pairs={{0,2},{1,3},{2,0},{3,1},{4,6},{5,7},{6,4},{7,5},{8,10},{9,11},{10,... | collective-permute-start | bytes 3145736 | tf_op jit(solution)/shard_map/ppermute | solution.py:27
  10.4 48.8 %collective-permute-start.2 = (bf16[7,64,1024]{2,1,0:T(8,128)(2,1)}, bf16[7,64,1024]{2,1,0:T(8,128)(2,1)}, u32[]{:S(2)}, u32[]{:S(2)}) collective-permute-start(bf16[7,64,1024]{2,1,0:T(8,128)(2,1)} %slice.63), channel_id=1, source_target_pairs={{0,4},{1,5},{2,6},{3,7},{4,8},{5,9},{6,10},{7,11},{8,12},{9,13},{1... | collective-permute-start | bytes 2752520 | tf_op jit(solution)/shard_map/ppermute | solution.py:31
  12.6 25.0 %collective-permute-start.6 = (bf16[2,256,768]{2,1,0:T(8,128)(2,1)S(1)}, bf16[2,256,768]{2,1,0:T(8,128)(2,1)S(1)}, u32[]{:S(2)}, u32[]{:S(2)}) collective-permute-start(bf16[2,256,768]{2,1,0:T(8,128)(2,1)S(1)} %get-tuple-element.167), channel_id=1, source_target_pairs={{0,66},{1,67},{2,64},{3,65},{4,70},{5,71},{6,68},{7,69},{8,74},{9,... | collective-permute-start | bytes 2359304 | tf_op jit(solution)/shard_map/ppermute | solution.py:27
  16.5 21.1 %collective-permute-start.5 = (bf16[256,768]{1,0:T(8,128)(2,1)S(1)}, bf16[256,768]{1,0:T(8,128)(2,1)S(1)}, u32[]{:S(2)}, u32[]{:S(2)}) collective-permute-start(bf16[256,768]{1,0:T(8,128)(2,1)S(1)} %get-tuple-element.166), channel_id=1, source_target_pairs={{0,1},{1,0},{2,3},{3,2},{4,5},{5,4},{6,7},{7,6},{8,9},{9,8},{10,11... | collective-permute-start | bytes 1179656 | tf_op jit(solution)/shard_map/ppermute | solution.py:27
  18.0 19.5 %collective-permute-start.4 = (f32[8,7424]{1,0:T(8,128)S(1)}, f32[8,7424]{1,0:T(8,128)S(1)}, u32[]{:S(2)}, u32[]{:S(2)}) collective-permute-start(f32[8,7424]{1,0:T(8,128)S(1)} %add.88), channel_id=1, source_target_pairs={{0,2},{1,3},{2,0},{3,1},{4,6},{5,7},{6,4},{7,5},{8,10},{9,11},{10,... | collective-permute-start | bytes 712712 | tf_op jit(solution)/shard_map/ppermute | solution.py:27
  37.5 23.3 %collective-permute-start = (bf16[8,64,1024]{2,1,0:T(8,128)(2,1)S(1)}, bf16[8,64,1024]{2,1,0:T(8,128)(2,1)S(1)}, u32[]{:S(2)}, u32[]{:S(2)}) collective-permute-start(bf16[8,64,1024]{2,1,0:T(8,128)(2,1)S(1)} %copy-done.3), channel_id=1, source_target_pairs={{0,1},{1,0},{2,3},{3,2},{4,5},{5,4},{6,7},{7,6},{8,9},{9,8},{10,11... | collective-permute-start | bytes 3145736 | tf_op jit(solution)/shard_map/ppermute | solution.py:27
  59.8 47.1 %collective-permute-start.10 = (bf16[7,64,1024]{2,1,0:T(8,128)(2,1)}, bf16[7,64,1024]{2,1,0:T(8,128)(2,1)S(1)}, u32[]{:S(2)}, u32[]{:S(2)}) collective-permute-start(bf16[7,64,1024]{2,1,0:T(8,128)(2,1)} %collective-permute-done.2.refs_1_), channel_id=1, source_target_pairs={{0,1},{1,0},{2,3},{3,2},{4,5},{5,4},{6,7},{7,6},{8,9},{9,8},{10,11... | collective-permute-start | bytes 2752520 | tf_op jit(solution)/shard_map/ppermute | solution.py:27
  59.9 46.4 %collective-permute-start.11 = (bf16[7,64,1024]{2,1,0:T(8,128)(2,1)}, bf16[7,64,1024]{2,1,0:T(8,128)(2,1)S(1)}, u32[]{:S(2)}, u32[]{:S(2)}) collective-permute-start(bf16[7,64,1024]{2,1,0:T(8,128)(2,1)} %collective-permute-done.2.refs_1_), channel_id=1, source_target_pairs={{0,2},{1,3},{2,0},{3,1},{4,6},{5,7},{6,4},{7,5},{8,10},{9,11},{10,... | collective-permute-start | bytes 2752520 | tf_op jit(solution)/shard_map/ppermute | solution.py:27
  60.8 27.6 %collective-permute-start.9 = (f32[8,2048]{1,0:T(8,128)S(1)}, f32[8,2048]{1,0:T(8,128)S(1)}, u32[]{:S(2)}, u32[]{:S(2)}) collective-permute-start(f32[8,2048]{1,0:T(8,128)S(1)} %slice.66), channel_id=1, source_target_pairs={{0,4},{1,5},{2,6},{3,7},{4,8},{5,9},{6,10},{7,11},{8,12},{9,13},{1... | collective-permute-start | bytes 196616 | tf_op jit(solution)/shard_map/ppermute | solution.py:31
  63.0 77.4 %collective-permute-start.18 = (bf16[256,4096]{1,0:T(8,128)(2,1)}, bf16[256,4096]{1,0:T(8,128)(2,1)}, u32[]{:S(2)}, u32[]{:S(2)}) collective-permute-start(bf16[256,4096]{1,0:T(8,128)(2,1)} %u0.1), channel_id=1, source_target_pairs={{0,66},{1,67},{2,64},{3,65},{4,70},{5,71},{6,68},{7,69},{8,74},{9,... | collective-permute-start | bytes 6291464 | tf_op jit(solution)/shard_map/ppermute | solution.py:27
  88.4 51.9 %collective-permute-start.19 = (bf16[1024,1024]{1,0:T(8,128)(2,1)S(1)}, bf16[1024,1024]{1,0:T(8,128)(2,1)S(1)}, u32[]{:S(2)}, u32[]{:S(2)}) collective-permute-start(bf16[1024,1024]{1,0:T(8,128)(2,1)S(1)} %copy-done.51), channel_id=1, source_target_pairs={{0,2},{1,3},{2,0},{3,1},{4,6},{5,7},{6,4},{7,5},{8,10},{9,11},{10,... | collective-permute-start | bytes 6291464 | tf_op jit(solution)/shard_map/ppermute | solution.py:27
  106.5 34.5 %collective-permute-start.16 = (bf16[256,1024]{1,0:T(8,128)(2,1)S(1)}, bf16[256,1024]{1,0:T(8,128)(2,1)S(1)}, u32[]{:S(2)}, u32[]{:S(2)}) collective-permute-start(bf16[256,1024]{1,0:T(8,128)(2,1)S(1)} %copy-done.13), channel_id=1, source_target_pairs={{0,1},{1,0},{2,3},{3,2},{4,5},{5,4},{6,7},{7,6},{8,9},{9,8},{10,11... | collective-permute-start | bytes 1572872 | tf_op jit(solution)/shard_map/ppermute | solution.py:27
  107.0 32.8 %collective-permute-start.17 = (bf16[256,1024]{1,0:T(8,128)(2,1)S(1)}, bf16[256,1024]{1,0:T(8,128)(2,1)S(1)}, u32[]{:S(2)}, u32[]{:S(2)}) collective-permute-start(bf16[256,1024]{1,0:T(8,128)(2,1)S(1)} %copy-done.13), channel_id=1, source_target_pairs={{0,66},{1,67},{2,64},{3,65},{4,70},{5,71},{6,68},{7,69},{8,74},{9,... | collective-permute-start | bytes 1572872 | tf_op jit(solution)/shard_map/ppermute | solution.py:27
  121.3 44.7 %collective-permute-start.21 = (bf16[256,4096]{1,0:T(8,128)(2,1)}, bf16[256,4096]{1,0:T(8,128)(2,1)S(1)}, u32[]{:S(2)}, u32[]{:S(2)}) collective-permute-start(bf16[256,4096]{1,0:T(8,128)(2,1)} %u0.1), channel_id=1, source_target_pairs={{0,1},{1,0},{2,3},{3,2},{4,5},{5,4},{6,7},{7,6},{8,9},{9,8},{10,11... | collective-permute-start | bytes 6291464 | tf_op jit(solution)/shard_map/ppermute | solution.py:27
  139.8 26.2 %collective-permute-start.23 = (bf16[1024,1024]{1,0:T(8,128)(2,1)S(1)}, bf16[1024,1024]{1,0:T(8,128)(2,1)S(1)}, u32[]{:S(2)}, u32[]{:S(2)}) collective-permute-start(bf16[1024,1024]{1,0:T(8,128)(2,1)S(1)} %copy-done.51), channel_id=1, source_target_pairs={{0,1},{1,0},{2,3},{3,2},{4,5},{5,4},{6,7},{7,6},{8,9},{9,8},{10,11... | collective-permute-start | bytes 6291464 | tf_op jit(solution)/shard_map/ppermute | solution.py:27
  140.4 25.7 %collective-permute-start.22 = (bf16[256,4096]{1,0:T(8,128)(2,1)}, bf16[256,4096]{1,0:T(8,128)(2,1)S(1)}, u32[]{:S(2)}, u32[]{:S(2)}) collective-permute-start(bf16[256,4096]{1,0:T(8,128)(2,1)} %collective-permute-done.18.u2), channel_id=1, source_target_pairs={{0,1},{1,0},{2,3},{3,2},{4,5},{5,4},{6,7},{7,6},{8,9},{9,8},{10,11... | collective-permute-start | bytes 6291464 | tf_op jit(solution)/shard_map/ppermute | solution.py:27
  140.5 25.6 %collective-permute-start.24 = (bf16[1024,1024]{1,0:T(8,128)(2,1)S(1)}, bf16[1024,1024]{1,0:T(8,128)(2,1)S(1)}, u32[]{:S(2)}, u32[]{:S(2)}) collective-permute-start(bf16[1024,1024]{1,0:T(8,128)(2,1)S(1)} %collective-permute-done.19.d2.db), channel_id=1, source_target_pairs={{0,1},{1,0},{2,3},{3,2},{4,5},{5,4},{6,7},{7,6},{8,9},{9,8},{10,11... | collective-permute-start | bytes 6291464 | tf_op jit(solution)/shard_map/ppermute | solution.py:27
  221.1 31.9 %collective-permute-start.28 = (bf16[2,4,256,1024]{3,2,1,0:T(8,128)(2,1)}, bf16[2,4,256,1024]{3,2,1,0:T(8,128)(2,1)S(1)}, u32[]{:S(2)}, u32[]{:S(2)}) collective-permute-start(bf16[2,4,256,1024]{3,2,1,0:T(8,128)(2,1)} %get-tuple-element.217), channel_id=1, source_target_pairs={{0,1},{1,0},{2,3},{3,2},{4,5},{5,4},{6,7},{7,6},{8,9},{9,8},{10,11... | collective-permute-start | bytes 12582920 | tf_op jit(solution)/shard_map/ppermute | solution.py:27
  238.1 33.0 %collective-permute-start.34 = (bf16[2,1024,1024]{2,1,0:T(8,128)(2,1)S(1)}, bf16[2,1024,1024]{2,1,0:T(8,128)(2,1)}, u32[]{:S(2)}, u32[]{:S(2)}) collective-permute-start(bf16[2,1024,1024]{2,1,0:T(8,128)(2,1)S(1)} %get-tuple-element.226), channel_id=1, source_target_pairs={{0,1},{1,0},{2,3},{3,2},{4,5},{5,4},{6,7},{7,6},{8,9},{9,8},{10,11... | collective-permute-start | bytes 12582920 | tf_op jit(solution)/shard_map/ppermute | solution.py:27
  286.9 267.5 %all-gather.2.cloned.1.call-start = ((), (), s32[]{:S(2)}) async-start(), calls=%async_computation.2 | async-start | bytes 5013504 | tf_op jit(solution)/shard_map/all_gather | solution.py:1406
  300.4 57.7 %collective-permute-start.37 = (bf16[2,7,256,256]{3,2,1,0:T(8,128)(2,1)}, bf16[2,7,256,256]{3,2,1,0:T(8,128)(2,1)S(1)}, u32[]{:S(2)}, u32[]{:S(2)}) collective-permute-start(bf16[2,7,256,256]{3,2,1,0:T(8,128)(2,1)} %get-tuple-element.258), channel_id=1, source_target_pairs={{0,124},{1,125},{2,126},{3,127},{4,0},{5,1},{6,2},{7,3},{8,4},{9,5... | collective-permute-start | bytes 5505032 | tf_op jit(solution)/shard_map/ppermute | solution.py:31
  371.8 24.9 %collective-permute-start.40 = (bf16[8,8,4096]{2,1,0:T(8,128)(2,1)}, bf16[8,8,4096]{2,1,0:T(8,128)(2,1)}, u32[]{:S(2)}, u32[]{:S(2)}) collective-permute-start(bf16[8,8,4096]{2,1,0:T(8,128)(2,1)} %join.1.refs_2_), channel_id=1, source_target_pairs={{0,4},{1,5},{2,6},{3,7},{4,0},{5,1},{6,2},{7,3},{8,12},{9,13},{10,... | collective-permute-start | bytes 1572872 | tf_op jit(solution)/shard_map/ppermute | solution.py:27
  371.8 39.3 %collective-permute-start.41 = (bf16[8,8,4096]{2,1,0:T(8,128)(2,1)}, bf16[8,8,4096]{2,1,0:T(8,128)(2,1)}, u32[]{:S(2)}, u32[]{:S(2)}) collective-permute-start(bf16[8,8,4096]{2,1,0:T(8,128)(2,1)} %join.1.refs_2_), channel_id=1, source_target_pairs={{0,8},{1,9},{2,10},{3,11},{4,12},{5,13},{6,14},{7,15},{8,0},{9,1},... | collective-permute-start | bytes 1572872 | tf_op jit(solution)/shard_map/ppermute | solution.py:27
  381.7 29.7 %collective-permute-start.42 = (bf16[8,8,4096]{2,1,0:T(8,128)(2,1)}, bf16[8,8,4096]{2,1,0:T(8,128)(2,1)}, u32[]{:S(2)}, u32[]{:S(2)}) collective-permute-start(bf16[8,8,4096]{2,1,0:T(8,128)(2,1)} %join.1.refs_2_), channel_id=1, source_target_pairs={{0,12},{1,13},{2,14},{3,15},{4,8},{5,9},{6,10},{7,11},{8,4},{9,5},... | collective-permute-start | bytes 1572872 | tf_op jit(solution)/shard_map/ppermute | solution.py:27
  383.1 34.2 %collective-permute-start.39 = (bf16[8,64,1024]{2,1,0:T(8,128)(2,1)}, bf16[8,64,1024]{2,1,0:T(8,128)(2,1)}, u32[]{:S(2)}, u32[]{:S(2)}) collective-permute-start(bf16[8,64,1024]{2,1,0:T(8,128)(2,1)} %fusion), channel_id=1, source_target_pairs={{0,2},{1,3},{2,0},{3,1},{4,6},{5,7},{6,4},{7,5},{8,10},{9,11},{10,... | collective-permute-start | bytes 3145736 | tf_op jit(solution)/shard_map/ppermute | solution.py:27
  412.5 17.4 %collective-permute-start.43 = (bf16[4,64,768]{2,1,0:T(8,128)(2,1)}, bf16[4,64,768]{2,1,0:T(8,128)(2,1)}, u32[]{:S(2)}, u32[]{:S(2)}) collective-permute-start(bf16[4,64,768]{2,1,0:T(8,128)(2,1)} %get-tuple-element.313), channel_id=1, source_target_pairs={{0,4},{1,5},{2,6},{3,7},{4,0},{5,1},{6,2},{7,3},{8,12},{9,13},{10,... | collective-permute-start | bytes 1179656 | tf_op jit(solution)/shard_map/ppermute | solution.py:27
  412.5 30.4 %collective-permute-start.44 = (bf16[4,64,768]{2,1,0:T(8,128)(2,1)}, bf16[4,64,768]{2,1,0:T(8,128)(2,1)}, u32[]{:S(2)}, u32[]{:S(2)}) collective-permute-start(bf16[4,64,768]{2,1,0:T(8,128)(2,1)} %get-tuple-element.312), channel_id=1, source_target_pairs={{0,8},{1,9},{2,10},{3,11},{4,12},{5,13},{6,14},{7,15},{8,0},{9,1},... | collective-permute-start | bytes 1179656 | tf_op jit(solution)/shard_map/ppermute | solution.py:27
  415.9 28.6 %collective-permute-start.45 = (bf16[4,64,768]{2,1,0:T(8,128)(2,1)}, bf16[4,64,768]{2,1,0:T(8,128)(2,1)}, u32[]{:S(2)}, u32[]{:S(2)}) collective-permute-start(bf16[4,64,768]{2,1,0:T(8,128)(2,1)} %get-tuple-element.311), channel_id=1, source_target_pairs={{0,12},{1,13},{2,14},{3,15},{4,8},{5,9},{6,10},{7,11},{8,4},{9,5},... | collective-permute-start | bytes 1179656 | tf_op jit(solution)/shard_map/ppermute | solution.py:27
  424.6 26.1 %collective-permute-start.46 = (f32[8,3584]{1,0:T(8,128)S(1)}, f32[8,3584]{1,0:T(8,128)S(1)}, u32[]{:S(2)}, u32[]{:S(2)}) collective-permute-start(f32[8,3584]{1,0:T(8,128)S(1)} %get-tuple-element.271), channel_id=1, source_target_pairs={{0,1},{1,0},{2,3},{3,2},{4,5},{5,4},{6,7},{7,6},{8,9},{9,8},{10,11... | collective-permute-start | bytes 344072 | tf_op jit(solution)/shard_map/ppermute | solution.py:27
  505.1 30.1 %collective-permute-start.67 = (bf16[2,4,16,3072]{3,2,1,0:T(8,128)(2,1)S(1)}, bf16[2,4,16,3072]{3,2,1,0:T(8,128)(2,1)S(1)}, u32[]{:S(2)}, u32[]{:S(2)}) collective-permute-start(bf16[2,4,16,3072]{3,2,1,0:T(8,128)(2,1)S(1)} %pad_maximum_fusion.1.low), channel_id=1, source_target_pairs={{0,12},{1,13},{2,14},{3,15},{4,8},{5,9},{6,10},{7,11},{8,4},{9,5},... | collective-permute-start | bytes 2359304 | tf_op jit(solution)/shard_map/ppermute | solution.py:27
  510.1 35.4 %collective-permute-start.65 = (bf16[2,4,16,3584]{3,2,1,0:T(8,128)(2,1)S(1)}, bf16[2,4,16,3584]{3,2,1,0:T(8,128)(2,1)S(1)}, u32[]{:S(2)}, u32[]{:S(2)}) collective-permute-start(bf16[2,4,16,3584]{3,2,1,0:T(8,128)(2,1)S(1)} %pad_maximum_fusion.refs_0_), channel_id=1, source_target_pairs={{0,4},{1,5},{2,6},{3,7},{4,0},{5,1},{6,2},{7,3},{8,12},{9,13},{10,... | collective-permute-start | bytes 2752520 | tf_op jit(solution)/shard_map/ppermute | solution.py:27
  (133 other events, 2223.8 us)
Sparse Core Ops, SparseCore 0:
  286.3 160.1 reduce-scatter.1
  481.5 64.6 all-gather.1

commit v2 on v1

--- a/solution.py
+++ b/solution.py
@@ -1302,15 +1302,15 @@
     p1 = swap(p0, CORE)
     before_mods = shift(table[:, : 2 * D], 1)
 
-    out_own, up_own, _ = lax.optimization_barrier((out_weight, up_weight, table))
+    out_own = after(out_weight, table)
     outs2 = swap(out_own, OTHER)
+
+    hidden1, q, k, v = project(True, row_arg, (x0, x1, x2, x3), table, table, qkv_pieces, tables)
+    outs2, up_own, down_own, q = lax.optimization_barrier((outs2, up_weight, down_weight, q))
     ups2 = swap(up_own, OTHER)
-
-    hidden1, q, k, v = project(True, row_arg, (x0, x1, x2, x3), table, table, qkv_pieces, tables)
-    down_own, q, before_mods = lax.optimization_barrier((down_weight, q, before_mods))
     downs2 = swap(down_own, DIRECT)
     state = attend(True, frame_position, q, k, v)
-    p2, *state = lax.optimization_barrier((p2, *state))
+    p2, before_mods, *state = lax.optimization_barrier((p2, before_mods, *state))
     p3 = swap(p2, CORE)
     kp, vp = project(
         False, row_arg, (p0, p1, p2, p3), table, before_mods, qkv_pieces, tables

time: 576 us -> 568 us (0.986)
  waiting for transfers between devices: 219 us -> 192 us
  Pallas kernels: 193 us -> 212 us
    ppermute x3, waiting for transfers between devices: 59 us -> 21.5 us  [shift(): lax.ppermute(value, AXES, [(i, (i + 4 * steps) % 128) for i in range(128)])]
    ppermute x3, starting transfers between devices: 6.24 us -> 20 us  [shift(): lax.ppermute(value, AXES, [(i, (i + 4 * steps) % 128) for i in range(128)])]
    ppermute x65, starting transfers between devices: 77.3 us -> 65.4 us  [swap(): return lax.ppermute(value, AXES, [(i, i ^ mask) for i in range(128)])]
    pallas_call x2, Pallas kernels: 41 us -> 52.7 us  [attend_back(): pl.pallas_call(lambda *refs: attend_back_kernel(own, *refs), out_shape=[s...]
    ppermute x65, waiting for transfers between devices: 160 us -> 171 us  [swap(): return lax.ppermute(value, AXES, [(i, i ^ mask) for i in range(128)])]
    pallas_call x2, Pallas kernels: 26.6 us -> 33.9 us  [attend(): pl.pallas_call(attend_own_kernel if own else attend_prev_kernel, out_shap...]
    unnamed x190 -> x194, local copies, waits for them, and re-layouts: 42.4 us -> 44.5 us
  transfers between devices with their start and end apart: 70 -> 70, of which waited for: 38 -> 37; matrix products, arithmetic and copies ran while one was open for 2% -> 2% of each run, Pallas kernels for 26% -> 30%
where the time goes in v2:
time: 568 us; the launch traced here: 563 us
  Pallas kernels  212 us (37%)
  waiting for transfers between devices  192 us (34%)
  starting transfers between devices  85.4 us (15%)
  local copies, waits for them, and re-layouts  50.6 us (9%)
  between operations  15.5 us (3%)
  other arithmetic  6.99 us (1%)
    ppermute x65, waiting for transfers between devices, swap(): return lax.ppermute(value, AXES, [(i, i ^ mask) for i in range(128)])  171 us
    ppermute x65, starting transfers between devices, swap(): return lax.ppermute(value, AXES, [(i, i ^ mask) for i in range(128)])  65.4 us
    pallas_call x2, Pallas kernels, attend_back(): pl.pallas_call(lambda *refs: attend_back_kernel(own, *refs), out_shape=[s...  52.7 us
    unnamed x194, local copies, waits for them, and re-layouts  44.5 us
    pallas_call x2, Pallas kernels, attend(): pl.pallas_call(attend_own_kernel if own else attend_prev_kernel, out_shap...  33.9 us
    pallas_call x1, Pallas kernels, feed(): pl.pallas_call(feed_kernel, out_shape=[shape((TOKENS, FF)), shape((TOKENS...  26.8 us
    ppermute x3, waiting for transfers between devices, shift(): lax.ppermute(value, AXES, [(i, (i + 4 * steps) % 128) for i in range(128)])  21.5 us
    ppermute x3, starting transfers between devices, shift(): lax.ppermute(value, AXES, [(i, (i + 4 * steps) % 128) for i in range(128)])  20 us
  transfers between devices with their start and end apart: 70, of which 37 were waited for; matrix products, arithmetic and copies ran while one was open for 2% of the time, Pallas kernels for 30%

profile of v2, /device:TPU:6, one launch (start us, length us, event | category | flops | bytes accessed | tf_op | source)
XLA Modules:
  0.0 563.4 jit_solution(8421278791988425906)
XLA Ops:
  19.3 18.3 %collective-permute-done.3 = f32[8,7424]{1,0:T(8,128)S(1)} collective-permute-done((f32[8,7424]{1,0:T(8,128)S(1)}, f32[8,7424]{1,0:T(8,128)S(1)}, u32[]{:S(2)}, u32[]{:S(2)}) %collective-permute-start.3) | collective-permute-done | bytes 237600 | tf_op jit(solution)/shard_map/ppermute | solution.py:27
  37.6 21.5 %collective-permute-done.1.refs_1_ = bf16[7,64,1024]{2,1,0:T(8,128)(2,1)S(1)} collective-permute-done((bf16[7,64,1024]{2,1,0:T(8,128)(2,1)}, bf16[7,64,1024]{2,1,0:T(8,128)(2,1)S(1)}, u32[]{:S(2)}, u32[]{:S(2)}) %collective-permute-start.1) | collective-permute-done | bytes 917536 | tf_op jit(solution)/shard_map/ppermute | solution.py:31
  63.1 11.1 %project_own.1 = (bf16[8,256,1024]{2,1,0:T(8,128)(2,1)S(1)}, bf16[8,256,256]{2,1,0:T(8,128)(2,1)S(1)}, bf16[8,256,256]{2,1,0:T(8,128)(2,1)S(1)}, bf16[8,256,256]{2,1,0:T(8,128)(2,1)S(1)}) custom-call(s32[1]{0:T(128)} %bitcast.row_ref.refs_0_, bf16[8,64,1024]{2,1,0:T(8,128)(2,1)S(1)} %copy-done.3, bf16[8,64,1024]{2,1,0:T(8,128)(2,1)S(1)} %collective-permute-done.7.refs_2_, ...), custom_call_target="tpu_custom_call" | custom-call | flops 3221225472 | bytes 12582912 | tf_op jit(solution)/shard_map/project_own/pallas_call | solution.py:280
  79.0 29.3 %attend_own.1 = (f32[8,256,256]{2,1,0:T(8,128)S(1)}, f32[8,256,128]{2,1,0:T(8,128)S(1)}) custom-call(s32[8]{0:T(128)S(1)} %copy-done.50, bf16[8,256,256]{2,1,0:T(8,128)(2,1)S(1)} %get-tuple-element.179.q.refs_1_, bf16[8,256,256]{2,1,0:T(8,128)(2,1)S(1)} %get-tuple-element.181.k.refs_2_, bf16[8,256,256]{2,1,0:T(8,128)(2,1)S(1)} %get-tuple-element.182.v.refs_3_), custom_call_target="tpu_custom_call" | custom-call | flops 8053063680 | bytes 6291456 | tf_op jit(solution)/shard_map/attend_own/pallas_call | solution.py:436
  111.2 7.2 %project_prev.1 = (bf16[7,256,256]{2,1,0:T(8,128)(2,1)S(1)}, bf16[7,256,256]{2,1,0:T(8,128)(2,1)S(1)}) custom-call(s32[1]{0:T(128)} %bitcast.row_ref.refs_0_, bf16[7,64,1024]{2,1,0:T(8,128)(2,1)S(1)} %copy-done.68, bf16[7,64,1024]{2,1,0:T(8,128)(2,1)S(1)} %collective-permute-done.10.refs_2_, bf16[7,64,1024]{2,1,0:T(8,128)(2,1)S(1)} %collective-permute-done.11.refs_3_, ...), custom_call_target="tpu_custom_call" | custom-call | flops 2818572288 | bytes 11534336 | tf_op jit(solution)/shard_map/project_prev/pallas_call | solution.py:280
  118.4 4.7 attend_prev.1
  125.5 5.2 collective-permute-done.19.d2.db
  131.5 13.5 %collective-permute-done.15 = bf16[2,8,64,256]{3,2,1,0:T(8,128)(2,1)S(1)} collective-permute-done((bf16[2,8,64,256]{3,2,1,0:T(8,128)(2,1)S(1)}, bf16[2,8,64,256]{3,2,1,0:T(8,128)(2,1)S(1)}, u32[]{:S(2)}, u32[]{:S(2)}) %collective-permute-start.15) | collective-permute-done | bytes 524320 | tf_op jit(solution)/shard_map/ppermute | solution.py:27
  159.0 26.8 %feed.1 = (bf16[512,4096]{1,0:T(8,128)(2,1)}, bf16[512,4096]{1,0:T(8,128)(2,1)}, f32[512,1024]{1,0:T(8,128)}, f32[8,512]{1,0:T(8,128)}) custom-call(s32[1]{0:T(128)} %bitcast.row_ref.refs_0_, bf16[512,1024]{1,0:T(8,128)(2,1)} %bitcast.70, bf16[512,1024]{1,0:T(8,128)(2,1)} %bitcast.67, bf16[256,4096]{1,0:T(8,128)(2,1)} %u0.1, ...), custom_call_target="tpu_custom_call" | custom-call | flops 12884901888 | bytes 31457280 | tf_op jit(solution)/shard_map/feed/pallas_call | solution.py:744
  199.8 10.8 %up_weight_grad.1 = (bf16[2,4,256,1024]{3,2,1,0:T(8,128)(2,1)}, bf16[2,4,256,1024]{3,2,1,0:T(8,128)(2,1)}) custom-call(s32[1]{0:T(128)} %bitcast.row_ref.refs_0_, bf16[512,1024]{1,0:T(8,128)(2,1)} %bitcast.71, bf16[512,4096]{1,0:T(8,128)(2,1)} %get-tuple-element.212.upg), custom_call_target="tpu_custom_call" | custom-call | flops 4294967296 | bytes 14680064 | tf_op jit(solution)/shard_map/up_weight_grad/pallas_call | solution.py:842
  211.8 4.9 collective-permute-done.26
  221.2 6.6 %down_weight_send.1 = (bf16[2,1024,1024]{2,1,0:T(8,128)(2,1)S(1)}, f32[512,1024]{1,0:T(8,128)S(1)}) custom-call(bf16[512,1024]{1,0:T(8,128)(2,1)S(1)} %bitcast.68, bf16[512,4096]{1,0:T(8,128)(2,1)} %get-tuple-element.215.act, bf16[1024,1024]{1,0:T(8,128)(2,1)S(1)} %copy-done.56, bf16[1024,1024]{1,0:T(8,128)(2,1)S(1)} %copy-done.58), custom_call_target="tpu_custom_call" | custom-call | flops 4294967296 | bytes 14680064 | tf_op jit(solution)/shard_map/down_weight_send/pallas_call | solution.py:816
  230.3 5.0 collective-permute-done.30.refs_5_
  235.3 8.4 %collective-permute-done.27 = bf16[8,4096]{1,0:T(8,128)(2,1)S(1)} collective-permute-done((bf16[8,4096]{1,0:T(8,128)(2,1)S(1)}, bf16[8,4096]{1,0:T(8,128)(2,1)S(1)}, u32[]{:S(2)}, u32[]{:S(2)}) %collective-permute-start.27) | collective-permute-done | bytes 65568 | tf_op jit(solution)/shard_map/ppermute | solution.py:27
  252.8 8.4 %down_weight_keep.1 = (bf16[2,1024,1024]{2,1,0:T(8,128)(2,1)}, bf16[8,64,1024]{2,1,0:T(8,128)(2,1)}, f32[8,1024]{1,0:T(8,128)S(1)}) custom-call(bf16[512,1024]{1,0:T(8,128)(2,1)S(1)} %bitcast.69, bf16[512,4096]{1,0:T(8,128)(2,1)} %get-tuple-element.215.act, bf16[1024,1024]{1,0:T(8,128)(2,1)S(1)} %copy-done.52, bf16[1024,1024]{1,0:T(8,128)(2,1)S(1)} %copy-done.54, ...), custom_call_target="tpu_custom_call" | custom-call | flops 4294967296 | bytes 14680064 | tf_op jit(solution)/shard_map/down_weight_keep/pallas_call | solution.py:816
  264.8 12.0 %core_sum.1 = bf16[2,2304,1024]{2,1,0:T(8,128)(2,1)} custom-call(bf16[2,4,256,1024]{3,2,1,0:T(8,128)(2,1)} %get-tuple-element.236.ua, bf16[2,4,256,1024]{3,2,1,0:T(8,128)(2,1)} %copy-done.85, bf16[2,1024,1024]{2,1,0:T(8,128)(2,1)} %get-tuple-element.238.da, bf16[2,1024,1024]{2,1,0:T(8,128)(2,1)} %collective-permute-done.34.db, ...), custom_call_target="tpu_custom_call" | custom-call | flops 1000 | bytes 1000 | tf_op jit(solution)/shard_map/core_sum/pallas_call | solution.py:902
  277.6 8.4 %attend_back_prev.1 = (f32[8,256,256]{2,1,0:T(8,128)}, bf16[2,7,256,256]{3,2,1,0:T(8,128)(2,1)}) custom-call(s32[8]{0:T(128)} %refs_0_.3, bf16[8,256,256]{2,1,0:T(8,128)(2,1)} %copy-done.17, bf16[7,256,256]{2,1,0:T(8,128)(2,1)} %copy-done.83, bf16[7,256,256]{2,1,0:T(8,128)(2,1)} %copy-done.84, bf16[8,64,256]{2,1,0:T(8,128)(2,1)} %copy-done.34, ...), custom_call_target="tpu_custom_call" | custom-call | flops 8053063680 | bytes 12582912 | tf_op jit(solution)/shard_map/attend_back_prev/pallas_call | solution.py:548
  285.9 18.3 %collective-permute-start.37 = (bf16[2,7,256,256]{3,2,1,0:T(8,128)(2,1)}, bf16[2,7,256,256]{3,2,1,0:T(8,128)(2,1)S(1)}, u32[]{:S(2)}, u32[]{:S(2)}) collective-permute-start(bf16[2,7,256,256]{3,2,1,0:T(8,128)(2,1)} %get-tuple-element.260), channel_id=1, source_target_pairs={{0,124},{1,125},{2,126},{3,127},{4,0},{5,1},{6,2},{7,3},{8,4},{9,5... | collective-permute-start | bytes 5505032 | tf_op jit(solution)/shard_map/ppermute | solution.py:31
  304.3 44.4 %attend_back_own.1 = (bf16[8,256,256]{2,1,0:T(8,128)(2,1)}, f32[8,256,256]{2,1,0:T(8,128)}, f32[8,256,256]{2,1,0:T(8,128)}) custom-call(s32[8]{0:T(128)} %refs_0_.3, bf16[8,256,256]{2,1,0:T(8,128)(2,1)} %copy-done.17, bf16[8,256,256]{2,1,0:T(8,128)(2,1)} %copy-done.18, bf16[8,256,256]{2,1,0:T(8,128)(2,1)} %copy-done.19, bf16[8,64,256]{2,1,0:T(8,128)(2,1)} %copy-done.34, ...), custom_call_target="tpu_custom_call" | custom-call | flops 1000 | bytes 1000 | tf_op jit(solution)/shard_map/attend_back_own/pallas_call | solution.py:548
  354.0 7.5 %project_back.1 = (bf16[8,256,768]{2,1,0:T(8,128)(2,1)S(1)}, bf16[8,64,1024]{2,1,0:T(8,128)(2,1)S(1)}, bf16[8,64,1024]{2,1,0:T(8,128)(2,1)S(1)}, bf16[2,8,64,1024]{3,2,1,0:T(8,128)(2,1)S(1)}, f32[8,512]{1,0:T(8,128)S(1)}) custom-call(s32[1]{0:T(128)} %bitcast.row_ref.refs_0_, bf16[8,256,256]{2,1,0:T(8,128)(2,1)S(1)} %copy-done.66, ...), custom_call_target="tpu_custom_call" | custom-call | flops 3221225472 | bytes 14680064 | tf_op jit(solution)/shard_map/project_back/pallas_call | solution.py:1055
  363.6 13.0 %collective-permute-start.41 = (bf16[8,8,4096]{2,1,0:T(8,128)(2,1)}, bf16[8,8,4096]{2,1,0:T(8,128)(2,1)}, u32[]{:S(2)}, u32[]{:S(2)}) collective-permute-start(bf16[8,8,4096]{2,1,0:T(8,128)(2,1)} %join.1.refs_2_), channel_id=1, source_target_pairs={{0,8},{1,9},{2,10},{3,11},{4,12},{5,13},{6,14},{7,15},{8,0},{9,1},... | collective-permute-start | bytes 1572872 | tf_op jit(solution)/shard_map/ppermute | solution.py:27
  384.1 4.8 project_weight.1
  388.9 19.5 %collective-permute-done.41.refs_4_ = bf16[8,8,4096]{2,1,0:T(8,128)(2,1)} collective-permute-done((bf16[8,8,4096]{2,1,0:T(8,128)(2,1)}, bf16[8,8,4096]{2,1,0:T(8,128)(2,1)}, u32[]{:S(2)}, u32[]{:S(2)}) %collective-permute-start.41) | collective-permute-done | bytes 524320 | tf_op jit(solution)/shard_map/ppermute | solution.py:27
  421.9 5.9 %collective-permute-done.43 = bf16[4,64,768]{2,1,0:T(8,128)(2,1)} collective-permute-done((bf16[4,64,768]{2,1,0:T(8,128)(2,1)}, bf16[4,64,768]{2,1,0:T(8,128)(2,1)}, u32[]{:S(2)}, u32[]{:S(2)}) %collective-permute-start.43) | collective-permute-done | bytes 393248 | tf_op jit(solution)/shard_map/ppermute | solution.py:27
  427.8 13.4 %collective-permute-done.44 = bf16[4,64,768]{2,1,0:T(8,128)(2,1)} collective-permute-done((bf16[4,64,768]{2,1,0:T(8,128)(2,1)}, bf16[4,64,768]{2,1,0:T(8,128)(2,1)}, u32[]{:S(2)}, u32[]{:S(2)}) %collective-permute-start.44) | collective-permute-done | bytes 393248 | tf_op jit(solution)/shard_map/ppermute | solution.py:27
  454.3 5.0 collective-permute-done.54
  472.2 5.5 collective-permute-done.60.far
  484.5 5.1 collective-permute-done.62.a2
  494.5 8.9 %collective-permute-done.66 = bf16[4,16,3072]{2,1,0:T(8,128)(2,1)S(1)} collective-permute-done((bf16[4,16,3072]{2,1,0:T(8,128)(2,1)S(1)}, bf16[4,16,3072]{2,1,0:T(8,128)(2,1)S(1)}, u32[]{:S(2)}, u32[]{:S(2)}) %collective-permute-start.66) | collective-permute-done | bytes 393248 | tf_op jit(solution)/shard_map/ppermute | solution.py:27
  514.1 19.5 %collective-permute-done.67.high = bf16[2,4,16,3072]{3,2,1,0:T(8,128)(2,1)S(1)} collective-permute-done((bf16[2,4,16,3072]{3,2,1,0:T(8,128)(2,1)S(1)}, bf16[2,4,16,3072]{3,2,1,0:T(8,128)(2,1)S(1)}, u32[]{:S(2)}, u32[]{:S(2)}) %collective-permute-start.67) | collective-permute-done | bytes 786464 | tf_op jit(solution)/shard_map/ppermute | solution.py:27
  536.2 5.1 collective-permute-done.65.refs_1_
  541.4 7.7 %final_sums.1 = (f32[256,6144]{1,0:T(8,128)}, f32[1,1536]{1,0:T(1,128)S(1)}, f32[1,768]{1,0:T(1,128)S(1)}, f32[1,256]{1,0:T(1,128)}, f32[1,1024]{1,0:T(1,128)}, /*index=5*/f32[1,256]{1,0:T(1,128)}) custom-call(s32[1]{0:T(128)} %bitcast.row_ref.refs_0_, bf16[2,4,16,3584]{3,2,1,0:T(8,128)(2,1)S(1)} %pad_maximum_fusion.refs_0_, ...), custom_call_target="tpu_custom_call" | custom-call | flops 805306368 | bytes 10485760 | tf_op jit(solution)/shard_map/final_sums/pallas_call | solution.py:1204
  (372 shorter events, 162.4 us)
Async XLA Ops:
  7.2 447.1 %reduce-scatter.2.cloned.1.call-start = ((), (), s32[]{:S(2)}) async-start(), calls=%async_computation.1 | async-start | bytes 10027008 | tf_op jit(solution)/shard_map/reduce_scatter | solution.py:1360
  7.2 51.8 %collective-permute-start = (bf16[8,64,1024]{2,1,0:T(8,128)(2,1)}, bf16[8,64,1024]{2,1,0:T(8,128)(2,1)}, u32[]{:S(2)}, u32[]{:S(2)}) collective-permute-start(bf16[8,64,1024]{2,1,0:T(8,128)(2,1)} %x.3), channel_id=1, source_target_pairs={{0,2},{1,3},{2,0},{3,1},{4,6},{5,7},{6,4},{7,5},{8,10},{9,11},{10,... | collective-permute-start | bytes 3145736 | tf_op jit(solution)/shard_map/ppermute | solution.py:27
  10.4 48.7 %collective-permute-start.1 = (bf16[7,64,1024]{2,1,0:T(8,128)(2,1)}, bf16[7,64,1024]{2,1,0:T(8,128)(2,1)S(1)}, u32[]{:S(2)}, u32[]{:S(2)}) collective-permute-start(bf16[7,64,1024]{2,1,0:T(8,128)(2,1)} %slice.63), channel_id=1, source_target_pairs={{0,4},{1,5},{2,6},{3,7},{4,8},{5,9},{6,10},{7,11},{8,12},{9,13},{1... | collective-permute-start | bytes 2752520 | tf_op jit(solution)/shard_map/ppermute | solution.py:31
  12.6 25.0 %collective-permute-start.5 = (bf16[2,256,768]{2,1,0:T(8,128)(2,1)S(1)}, bf16[2,256,768]{2,1,0:T(8,128)(2,1)S(1)}, u32[]{:S(2)}, u32[]{:S(2)}) collective-permute-start(bf16[2,256,768]{2,1,0:T(8,128)(2,1)S(1)} %get-tuple-element.168), channel_id=1, source_target_pairs={{0,66},{1,67},{2,64},{3,65},{4,70},{5,71},{6,68},{7,69},{8,74},{9,... | collective-permute-start | bytes 2359304 | tf_op jit(solution)/shard_map/ppermute | solution.py:27
  16.5 21.1 %collective-permute-start.4 = (bf16[256,768]{1,0:T(8,128)(2,1)S(1)}, bf16[256,768]{1,0:T(8,128)(2,1)S(1)}, u32[]{:S(2)}, u32[]{:S(2)}) collective-permute-start(bf16[256,768]{1,0:T(8,128)(2,1)S(1)} %get-tuple-element.167), channel_id=1, source_target_pairs={{0,1},{1,0},{2,3},{3,2},{4,5},{5,4},{6,7},{7,6},{8,9},{9,8},{10,11... | collective-permute-start | bytes 1179656 | tf_op jit(solution)/shard_map/ppermute | solution.py:27
  18.0 19.5 %collective-permute-start.3 = (f32[8,7424]{1,0:T(8,128)S(1)}, f32[8,7424]{1,0:T(8,128)S(1)}, u32[]{:S(2)}, u32[]{:S(2)}) collective-permute-start(f32[8,7424]{1,0:T(8,128)S(1)} %add.88), channel_id=1, source_target_pairs={{0,2},{1,3},{2,0},{3,1},{4,6},{5,7},{6,4},{7,5},{8,10},{9,11},{10,... | collective-permute-start | bytes 712712 | tf_op jit(solution)/shard_map/ppermute | solution.py:27
  37.5 25.5 %collective-permute-start.7 = (bf16[8,64,1024]{2,1,0:T(8,128)(2,1)S(1)}, bf16[8,64,1024]{2,1,0:T(8,128)(2,1)S(1)}, u32[]{:S(2)}, u32[]{:S(2)}) collective-permute-start(bf16[8,64,1024]{2,1,0:T(8,128)(2,1)S(1)} %copy-done.3), channel_id=1, source_target_pairs={{0,1},{1,0},{2,3},{3,2},{4,5},{5,4},{6,7},{7,6},{8,9},{9,8},{10,11... | collective-permute-start | bytes 3145736 | tf_op jit(solution)/shard_map/ppermute | solution.py:27
  62.8 46.1 %collective-permute-start.10 = (bf16[7,64,1024]{2,1,0:T(8,128)(2,1)}, bf16[7,64,1024]{2,1,0:T(8,128)(2,1)S(1)}, u32[]{:S(2)}, u32[]{:S(2)}) collective-permute-start(bf16[7,64,1024]{2,1,0:T(8,128)(2,1)} %copy-done.67), channel_id=1, source_target_pairs={{0,1},{1,0},{2,3},{3,2},{4,5},{5,4},{6,7},{7,6},{8,9},{9,8},{10,11... | collective-permute-start | bytes 2752520 | tf_op jit(solution)/shard_map/ppermute | solution.py:27
  63.0 45.3 %collective-permute-start.11 = (bf16[7,64,1024]{2,1,0:T(8,128)(2,1)}, bf16[7,64,1024]{2,1,0:T(8,128)(2,1)S(1)}, u32[]{:S(2)}, u32[]{:S(2)}) collective-permute-start(bf16[7,64,1024]{2,1,0:T(8,128)(2,1)} %copy-done.67), channel_id=1, source_target_pairs={{0,2},{1,3},{2,0},{3,1},{4,6},{5,7},{6,4},{7,5},{8,10},{9,11},{10,... | collective-permute-start | bytes 2752520 | tf_op jit(solution)/shard_map/ppermute | solution.py:27
  63.0 45.2 %collective-permute-start.12 = (f32[8,2048]{1,0:T(8,128)S(1)}, f32[8,2048]{1,0:T(8,128)S(1)}, u32[]{:S(2)}, u32[]{:S(2)}) collective-permute-start(f32[8,2048]{1,0:T(8,128)S(1)} %slice.66), channel_id=1, source_target_pairs={{0,4},{1,5},{2,6},{3,7},{4,8},{5,9},{6,10},{7,11},{8,12},{9,13},{1... | collective-permute-start | bytes 196616 | tf_op jit(solution)/shard_map/ppermute | solution.py:31
  76.3 49.2 %collective-permute-start.18 = (bf16[256,4096]{1,0:T(8,128)(2,1)S(1)}, bf16[256,4096]{1,0:T(8,128)(2,1)}, u32[]{:S(2)}, u32[]{:S(2)}) collective-permute-start(bf16[256,4096]{1,0:T(8,128)(2,1)S(1)} %copy-done.93), channel_id=1, source_target_pairs={{0,66},{1,67},{2,64},{3,65},{4,70},{5,71},{6,68},{7,69},{8,74},{9,... | collective-permute-start | bytes 6291464 | tf_op jit(solution)/shard_map/ppermute | solution.py:27
  79.0 51.7 %collective-permute-start.19 = (bf16[1024,1024]{1,0:T(8,128)(2,1)S(1)}, bf16[1024,1024]{1,0:T(8,128)(2,1)S(1)}, u32[]{:S(2)}, u32[]{:S(2)}) collective-permute-start(bf16[1024,1024]{1,0:T(8,128)(2,1)S(1)} %copy-done.51), channel_id=1, source_target_pairs={{0,2},{1,3},{2,0},{3,1},{4,6},{5,7},{6,4},{7,5},{8,10},{9,11},{10,... | collective-permute-start | bytes 6291464 | tf_op jit(solution)/shard_map/ppermute | solution.py:27
  108.4 22.8 %collective-permute-start.17 = (bf16[256,1024]{1,0:T(8,128)(2,1)S(1)}, bf16[256,1024]{1,0:T(8,128)(2,1)S(1)}, u32[]{:S(2)}, u32[]{:S(2)}) collective-permute-start(bf16[256,1024]{1,0:T(8,128)(2,1)S(1)} %copy-done.13), channel_id=1, source_target_pairs={{0,1},{1,0},{2,3},{3,2},{4,5},{5,4},{6,7},{7,6},{8,9},{9,8},{10,11... | collective-permute-start | bytes 1572872 | tf_op jit(solution)/shard_map/ppermute | solution.py:27
  108.9 47.4 %collective-permute-start.21 = (bf16[256,4096]{1,0:T(8,128)(2,1)S(1)}, bf16[256,4096]{1,0:T(8,128)(2,1)}, u32[]{:S(2)}, u32[]{:S(2)}) collective-permute-start(bf16[256,4096]{1,0:T(8,128)(2,1)S(1)} %copy-done.93), channel_id=1, source_target_pairs={{0,1},{1,0},{2,3},{3,2},{4,5},{5,4},{6,7},{7,6},{8,9},{9,8},{10,11... | collective-permute-start | bytes 6291464 | tf_op jit(solution)/shard_map/ppermute | solution.py:27
  110.8 45.4 %collective-permute-start.23 = (bf16[1024,1024]{1,0:T(8,128)(2,1)S(1)}, bf16[1024,1024]{1,0:T(8,128)(2,1)S(1)}, u32[]{:S(2)}, u32[]{:S(2)}) collective-permute-start(bf16[1024,1024]{1,0:T(8,128)(2,1)S(1)} %copy-done.51), channel_id=1, source_target_pairs={{0,1},{1,0},{2,3},{3,2},{4,5},{5,4},{6,7},{7,6},{8,9},{9,8},{10,11... | collective-permute-start | bytes 6291464 | tf_op jit(solution)/shard_map/ppermute | solution.py:27
  130.7 25.6 %collective-permute-start.22 = (bf16[256,4096]{1,0:T(8,128)(2,1)}, bf16[256,4096]{1,0:T(8,128)(2,1)S(1)}, u32[]{:S(2)}, u32[]{:S(2)}) collective-permute-start(bf16[256,4096]{1,0:T(8,128)(2,1)} %collective-permute-done.18.u2), channel_id=1, source_target_pairs={{0,1},{1,0},{2,3},{3,2},{4,5},{5,4},{6,7},{7,6},{8,9},{9,8},{10,11... | collective-permute-start | bytes 6291464 | tf_op jit(solution)/shard_map/ppermute | solution.py:27
  130.7 25.6 %collective-permute-start.24 = (bf16[1024,1024]{1,0:T(8,128)(2,1)S(1)}, bf16[1024,1024]{1,0:T(8,128)(2,1)S(1)}, u32[]{:S(2)}, u32[]{:S(2)}) collective-permute-start(bf16[1024,1024]{1,0:T(8,128)(2,1)S(1)} %collective-permute-done.19.d2.db), channel_id=1, source_target_pairs={{0,1},{1,0},{2,3},{3,2},{4,5},{5,4},{6,7},{7,6},{8,9},{9,8},{10,11... | collective-permute-start | bytes 6291464 | tf_op jit(solution)/shard_map/ppermute | solution.py:27
  210.6 33.1 %collective-permute-start.28 = (bf16[2,4,256,1024]{3,2,1,0:T(8,128)(2,1)}, bf16[2,4,256,1024]{3,2,1,0:T(8,128)(2,1)S(1)}, u32[]{:S(2)}, u32[]{:S(2)}) collective-permute-start(bf16[2,4,256,1024]{3,2,1,0:T(8,128)(2,1)} %get-tuple-element.219), channel_id=1, source_target_pairs={{0,1},{1,0},{2,3},{3,2},{4,5},{5,4},{6,7},{7,6},{8,9},{9,8},{10,11... | collective-permute-start | bytes 12582920 | tf_op jit(solution)/shard_map/ppermute | solution.py:27
  227.8 34.0 %collective-permute-start.34 = (bf16[2,1024,1024]{2,1,0:T(8,128)(2,1)S(1)}, bf16[2,1024,1024]{2,1,0:T(8,128)(2,1)}, u32[]{:S(2)}, u32[]{:S(2)}) collective-permute-start(bf16[2,1024,1024]{2,1,0:T(8,128)(2,1)S(1)} %get-tuple-element.228), channel_id=1, source_target_pairs={{0,1},{1,0},{2,3},{3,2},{4,5},{5,4},{6,7},{7,6},{8,9},{9,8},{10,11... | collective-permute-start | bytes 12582920 | tf_op jit(solution)/shard_map/ppermute | solution.py:27
  277.6 272.7 %all-gather.2.cloned.1.call-start = ((), (), s32[]{:S(2)}) async-start(), calls=%async_computation.2 | async-start | bytes 5013504 | tf_op jit(solution)/shard_map/all_gather | solution.py:1406
  285.9 63.6 %collective-permute-start.37 = (bf16[2,7,256,256]{3,2,1,0:T(8,128)(2,1)}, bf16[2,7,256,256]{3,2,1,0:T(8,128)(2,1)S(1)}, u32[]{:S(2)}, u32[]{:S(2)}) collective-permute-start(bf16[2,7,256,256]{3,2,1,0:T(8,128)(2,1)} %get-tuple-element.260), channel_id=1, source_target_pairs={{0,124},{1,125},{2,126},{3,127},{4,0},{5,1},{6,2},{7,3},{8,4},{9,5... | collective-permute-start | bytes 5505032 | tf_op jit(solution)/shard_map/ppermute | solution.py:31
  363.5 25.4 %collective-permute-start.40 = (bf16[8,8,4096]{2,1,0:T(8,128)(2,1)}, bf16[8,8,4096]{2,1,0:T(8,128)(2,1)}, u32[]{:S(2)}, u32[]{:S(2)}) collective-permute-start(bf16[8,8,4096]{2,1,0:T(8,128)(2,1)} %join.1.refs_2_), channel_id=1, source_target_pairs={{0,4},{1,5},{2,6},{3,7},{4,0},{5,1},{6,2},{7,3},{8,12},{9,13},{10,... | collective-permute-start | bytes 1572872 | tf_op jit(solution)/shard_map/ppermute | solution.py:27
  363.6 44.8 %collective-permute-start.41 = (bf16[8,8,4096]{2,1,0:T(8,128)(2,1)}, bf16[8,8,4096]{2,1,0:T(8,128)(2,1)}, u32[]{:S(2)}, u32[]{:S(2)}) collective-permute-start(bf16[8,8,4096]{2,1,0:T(8,128)(2,1)} %join.1.refs_2_), channel_id=1, source_target_pairs={{0,8},{1,9},{2,10},{3,11},{4,12},{5,13},{6,14},{7,15},{8,0},{9,1},... | collective-permute-start | bytes 1572872 | tf_op jit(solution)/shard_map/ppermute | solution.py:27
  376.7 32.2 %collective-permute-start.42 = (bf16[8,8,4096]{2,1,0:T(8,128)(2,1)}, bf16[8,8,4096]{2,1,0:T(8,128)(2,1)}, u32[]{:S(2)}, u32[]{:S(2)}) collective-permute-start(bf16[8,8,4096]{2,1,0:T(8,128)(2,1)} %join.1.refs_2_), channel_id=1, source_target_pairs={{0,12},{1,13},{2,14},{3,15},{4,8},{5,9},{6,10},{7,11},{8,4},{9,5},... | collective-permute-start | bytes 1572872 | tf_op jit(solution)/shard_map/ppermute | solution.py:27
  378.0 36.7 %collective-permute-start.39 = (bf16[8,64,1024]{2,1,0:T(8,128)(2,1)}, bf16[8,64,1024]{2,1,0:T(8,128)(2,1)}, u32[]{:S(2)}, u32[]{:S(2)}) collective-permute-start(bf16[8,64,1024]{2,1,0:T(8,128)(2,1)} %fusion), channel_id=1, source_target_pairs={{0,2},{1,3},{2,0},{3,1},{4,6},{5,7},{6,4},{7,5},{8,10},{9,11},{10,... | collective-permute-start | bytes 3145736 | tf_op jit(solution)/shard_map/ppermute | solution.py:27
  410.0 17.8 %collective-permute-start.43 = (bf16[4,64,768]{2,1,0:T(8,128)(2,1)}, bf16[4,64,768]{2,1,0:T(8,128)(2,1)}, u32[]{:S(2)}, u32[]{:S(2)}) collective-permute-start(bf16[4,64,768]{2,1,0:T(8,128)(2,1)} %get-tuple-element.315), channel_id=1, source_target_pairs={{0,4},{1,5},{2,6},{3,7},{4,0},{5,1},{6,2},{7,3},{8,12},{9,13},{10,... | collective-permute-start | bytes 1179656 | tf_op jit(solution)/shard_map/ppermute | solution.py:27
  410.0 31.1 %collective-permute-start.44 = (bf16[4,64,768]{2,1,0:T(8,128)(2,1)}, bf16[4,64,768]{2,1,0:T(8,128)(2,1)}, u32[]{:S(2)}, u32[]{:S(2)}) collective-permute-start(bf16[4,64,768]{2,1,0:T(8,128)(2,1)} %get-tuple-element.314), channel_id=1, source_target_pairs={{0,8},{1,9},{2,10},{3,11},{4,12},{5,13},{6,14},{7,15},{8,0},{9,1},... | collective-permute-start | bytes 1179656 | tf_op jit(solution)/shard_map/ppermute | solution.py:27
  414.0 29.1 %collective-permute-start.45 = (bf16[4,64,768]{2,1,0:T(8,128)(2,1)}, bf16[4,64,768]{2,1,0:T(8,128)(2,1)}, u32[]{:S(2)}, u32[]{:S(2)}) collective-permute-start(bf16[4,64,768]{2,1,0:T(8,128)(2,1)} %get-tuple-element.313), channel_id=1, source_target_pairs={{0,12},{1,13},{2,14},{3,15},{4,8},{5,9},{6,10},{7,11},{8,4},{9,5},... | collective-permute-start | bytes 1179656 | tf_op jit(solution)/shard_map/ppermute | solution.py:27
  421.9 27.5 %collective-permute-start.46 = (f32[8,3584]{1,0:T(8,128)S(1)}, f32[8,3584]{1,0:T(8,128)S(1)}, u32[]{:S(2)}, u32[]{:S(2)}) collective-permute-start(f32[8,3584]{1,0:T(8,128)S(1)} %get-tuple-element.273), channel_id=1, source_target_pairs={{0,1},{1,0},{2,3},{3,2},{4,5},{5,4},{6,7},{7,6},{8,9},{9,8},{10,11... | collective-permute-start | bytes 344072 | tf_op jit(solution)/shard_map/ppermute | solution.py:27
  491.8 16.7 %collective-permute-start.64 = (bf16[4,16,3584]{2,1,0:T(8,128)(2,1)S(1)}, bf16[4,16,3584]{2,1,0:T(8,128)(2,1)S(1)}, u32[]{:S(2)}, u32[]{:S(2)}) collective-permute-start(bf16[4,16,3584]{2,1,0:T(8,128)(2,1)S(1)} %get-tuple-element.296), channel_id=1, source_target_pairs={{0,12},{1,13},{2,14},{3,15},{4,8},{5,9},{6,10},{7,11},{8,4},{9,5},... | collective-permute-start | bytes 1376264 | tf_op jit(solution)/shard_map/ppermute | solution.py:27
  503.4 30.1 %collective-permute-start.67 = (bf16[2,4,16,3072]{3,2,1,0:T(8,128)(2,1)S(1)}, bf16[2,4,16,3072]{3,2,1,0:T(8,128)(2,1)S(1)}, u32[]{:S(2)}, u32[]{:S(2)}) collective-permute-start(bf16[2,4,16,3072]{3,2,1,0:T(8,128)(2,1)S(1)} %pad_maximum_fusion.1.low), channel_id=1, source_target_pairs={{0,12},{1,13},{2,14},{3,15},{4,8},{5,9},{6,10},{7,11},{8,4},{9,5},... | collective-permute-start | bytes 2359304 | tf_op jit(solution)/shard_map/ppermute | solution.py:27
  508.7 32.7 %collective-permute-start.65 = (bf16[2,4,16,3584]{3,2,1,0:T(8,128)(2,1)S(1)}, bf16[2,4,16,3584]{3,2,1,0:T(8,128)(2,1)S(1)}, u32[]{:S(2)}, u32[]{:S(2)}) collective-permute-start(bf16[2,4,16,3584]{3,2,1,0:T(8,128)(2,1)S(1)} %pad_maximum_fusion.refs_0_), channel_id=1, source_target_pairs={{0,4},{1,5},{2,6},{3,7},{4,0},{5,1},{6,2},{7,3},{8,12},{9,13},{10,... | collective-permute-start | bytes 2752520 | tf_op jit(solution)/shard_map/ppermute | solution.py:27
  (135 other events, 2164.2 us)
Sparse Core Ops, SparseCore 0:
  277.0 167.7 reduce-scatter.1
  478.6 64.0 all-gather.1

commit v3 on v2

--- a/solution.py
+++ b/solution.py
@@ -1355,12 +1355,14 @@
         (dk_part, early_parts, ds_part_far, os, far_back)
     )
     back += [far_back[0], swap(far_back[1], CORE)]
-    packed = core_sum((uk, us), (dk_part, ds_part_far), (ok, os))
-    packed, back = lax.optimization_barrier((packed, back))
-    scattered = lax.psum_scatter(packed, ("y", "z"), scatter_dimension=1, tiled=True)
+    dk_part, back = lax.optimization_barrier((dk_part, back))
 
     dq_before, both = attend_back(False, frame_position, q, kp, vp, back, mixed, lse)
     returned = shift(both, -1)
+    uk, dq_before = lax.optimization_barrier((uk, dq_before))
+    packed = core_sum((uk, us), (dk_part, ds_part_far), (ok, os))
+    dq_before, packed = lax.optimization_barrier((dq_before, packed))
+    scattered = lax.psum_scatter(packed, ("y", "z"), scatter_dimension=1, tiled=True)
     dq, dk, dv = attend_back(
         True, frame_position, q, k, v, back, mixed, lse, tables, dq_before
     )

time: 568 us -> 575 us (1.012)
  starting transfers between devices: 85.4 us -> 60.3 us
  waiting for transfers between devices: 192 us -> 213 us
  Pallas kernels: 212 us -> 219 us
    ppermute x3, waiting for transfers between devices: 21.5 us -> 40.3 us  [shift(): lax.ppermute(value, AXES, [(i, (i + 4 * steps) % 128) for i in range(128)])]
    ppermute x3, starting transfers between devices: 20 us -> 1.73 us  [shift(): lax.ppermute(value, AXES, [(i, (i + 4 * steps) % 128) for i in range(128)])]
    pallas_call x2, Pallas kernels: 33.9 us -> 42.8 us  [attend(): pl.pallas_call(attend_own_kernel if own else attend_prev_kernel, out_shap...]
    ppermute x65, starting transfers between devices: 65.4 us -> 58.5 us  [swap(): return lax.ppermute(value, AXES, [(i, i ^ mask) for i in range(128)])]
  transfers between devices with their start and end apart: 70 -> 70, of which waited for: 37 -> 36; matrix products, arithmetic and copies ran while one was open for 2% -> 2% of each run, Pallas kernels for 30% -> 25%
where the time goes in v3:
time: 575 us; the launch traced here: 565 us
  Pallas kernels  219 us (38%)
  waiting for transfers between devices  213 us (37%)
  starting transfers between devices  60.3 us (10%)
  local copies, waits for them, and re-layouts  48.9 us (9%)
  between operations  15.6 us (3%)
  other arithmetic  7.06 us (1%)
    ppermute x65, waiting for transfers between devices, swap(): return lax.ppermute(value, AXES, [(i, i ^ mask) for i in range(128)])  169 us
    ppermute x65, starting transfers between devices, swap(): return lax.ppermute(value, AXES, [(i, i ^ mask) for i in range(128)])  58.5 us
    pallas_call x2, Pallas kernels, attend_back(): pl.pallas_call(lambda *refs: attend_back_kernel(own, *refs), out_shape=[s...  51.6 us
    unnamed x194, local copies, waits for them, and re-layouts  42.8 us
    pallas_call x2, Pallas kernels, attend(): pl.pallas_call(attend_own_kernel if own else attend_prev_kernel, out_shap...  42.8 us
    ppermute x3, waiting for transfers between devices, shift(): lax.ppermute(value, AXES, [(i, (i + 4 * steps) % 128) for i in range(128)])  40.3 us
    pallas_call x1, Pallas kernels, feed(): pl.pallas_call(feed_kernel, out_shape=[shape((TOKENS, FF)), shape((TOKENS...  26.8 us
    pallas_call x2, Pallas kernels, project(): pl.pallas_call(lambda *refs: project_kernel(own, *refs), out_shape=out_sh...  18.3 us
  transfers between devices with their start and end apart: 70, of which 36 were waited for; matrix products, arithmetic and copies ran while one was open for 2% of the time, Pallas kernels for 25%

profile of v3, /device:TPU:6, one launch (start us, length us, event | category | flops | bytes accessed | tf_op | source)
XLA Modules:
  0.0 565.0 jit_solution(11112174459773074678)
XLA Ops:
  19.3 18.3 %collective-permute-done.3 = f32[8,7424]{1,0:T(8,128)S(1)} collective-permute-done((f32[8,7424]{1,0:T(8,128)S(1)}, f32[8,7424]{1,0:T(8,128)S(1)}, u32[]{:S(2)}, u32[]{:S(2)}) %collective-permute-start.3) | collective-permute-done | bytes 237600 | tf_op jit(solution)/shard_map/ppermute | solution.py:27
  37.6 21.5 %collective-permute-done.1.refs_1_ = bf16[7,64,1024]{2,1,0:T(8,128)(2,1)S(1)} collective-permute-done((bf16[7,64,1024]{2,1,0:T(8,128)(2,1)}, bf16[7,64,1024]{2,1,0:T(8,128)(2,1)S(1)}, u32[]{:S(2)}, u32[]{:S(2)}) %collective-permute-start.1) | collective-permute-done | bytes 917536 | tf_op jit(solution)/shard_map/ppermute | solution.py:31
  63.1 11.1 %project_own.1 = (bf16[8,256,1024]{2,1,0:T(8,128)(2,1)S(1)}, bf16[8,256,256]{2,1,0:T(8,128)(2,1)S(1)}, bf16[8,256,256]{2,1,0:T(8,128)(2,1)S(1)}, bf16[8,256,256]{2,1,0:T(8,128)(2,1)S(1)}) custom-call(s32[1]{0:T(128)} %bitcast.row_ref.refs_0_, bf16[8,64,1024]{2,1,0:T(8,128)(2,1)S(1)} %copy-done.3, bf16[8,64,1024]{2,1,0:T(8,128)(2,1)S(1)} %collective-permute-done.7.refs_2_, ...), custom_call_target="tpu_custom_call" | custom-call | flops 3221225472 | bytes 12582912 | tf_op jit(solution)/shard_map/project_own/pallas_call | solution.py:280
  79.0 20.4 %attend_own.1 = (f32[8,256,256]{2,1,0:T(8,128)S(1)}, f32[8,256,128]{2,1,0:T(8,128)S(1)}) custom-call(s32[8]{0:T(128)S(1)} %copy-done.50, bf16[8,256,256]{2,1,0:T(8,128)(2,1)S(1)} %get-tuple-element.183.q.refs_1_, bf16[8,256,256]{2,1,0:T(8,128)(2,1)S(1)} %get-tuple-element.185.k.refs_2_, bf16[8,256,256]{2,1,0:T(8,128)(2,1)S(1)} %get-tuple-element.186.v.refs_3_), custom_call_target="tpu_custom_call" | custom-call | flops 8053063680 | bytes 6291456 | tf_op jit(solution)/shard_map/attend_own/pallas_call | solution.py:436
  102.3 7.2 %project_prev.1 = (bf16[7,256,256]{2,1,0:T(8,128)(2,1)S(1)}, bf16[7,256,256]{2,1,0:T(8,128)(2,1)S(1)}) custom-call(s32[1]{0:T(128)} %bitcast.row_ref.refs_0_, bf16[7,64,1024]{2,1,0:T(8,128)(2,1)S(1)} %copy-done.68, bf16[7,64,1024]{2,1,0:T(8,128)(2,1)S(1)} %collective-permute-done.10.refs_2_, bf16[7,64,1024]{2,1,0:T(8,128)(2,1)S(1)} %collective-permute-done.11.refs_3_, ...), custom_call_target="tpu_custom_call" | custom-call | flops 2818572288 | bytes 11534336 | tf_op jit(solution)/shard_map/project_prev/pallas_call | solution.py:280
  109.6 22.4 %attend_prev.1 = (bf16[8,64,256]{2,1,0:T(8,128)(2,1)S(1)}, bf16[8,64,256]{2,1,0:T(8,128)(2,1)S(1)}, bf16[2,8,64,256]{3,2,1,0:T(8,128)(2,1)S(1)}, f32[8,8,256]{2,1,0:T(8,128)S(1)}) custom-call(s32[8]{0:T(128)S(1)} %copy-done.50, bf16[8,256,256]{2,1,0:T(8,128)(2,1)S(1)} %get-tuple-element.183.q.refs_1_, bf16[7,256,256]{2,1,0:T(8,128)(2,1)S(1)} %get-tuple-element.191.k.refs_2_, ...), custom_call_target="tpu_custom_call" | custom-call | flops 3221225472 | bytes 6291456 | tf_op jit(solution)/shard_map/attend_prev/pallas_call | solution.py:436
  134.6 12.4 %collective-permute-done.15 = bf16[2,8,64,256]{3,2,1,0:T(8,128)(2,1)S(1)} collective-permute-done((bf16[2,8,64,256]{3,2,1,0:T(8,128)(2,1)S(1)}, bf16[2,8,64,256]{3,2,1,0:T(8,128)(2,1)S(1)}, u32[]{:S(2)}, u32[]{:S(2)}) %collective-permute-start.15) | collective-permute-done | bytes 524320 | tf_op jit(solution)/shard_map/ppermute | solution.py:27
  161.0 26.8 %feed.1 = (bf16[512,4096]{1,0:T(8,128)(2,1)}, bf16[512,4096]{1,0:T(8,128)(2,1)}, f32[512,1024]{1,0:T(8,128)}, f32[8,512]{1,0:T(8,128)}) custom-call(s32[1]{0:T(128)} %bitcast.row_ref.refs_0_, bf16[512,1024]{1,0:T(8,128)(2,1)} %bitcast.70, bf16[512,1024]{1,0:T(8,128)(2,1)} %bitcast.67, bf16[256,4096]{1,0:T(8,128)(2,1)} %u0.1, ...), custom_call_target="tpu_custom_call" | custom-call | flops 12884901888 | bytes 31457280 | tf_op jit(solution)/shard_map/feed/pallas_call | solution.py:744
  192.7 3.8 mid_back.1
  201.8 10.8 %up_weight_grad.1 = (bf16[2,4,256,1024]{3,2,1,0:T(8,128)(2,1)}, bf16[2,4,256,1024]{3,2,1,0:T(8,128)(2,1)}) custom-call(s32[1]{0:T(128)} %bitcast.row_ref.refs_0_, bf16[512,1024]{1,0:T(8,128)(2,1)} %bitcast.71, bf16[512,4096]{1,0:T(8,128)(2,1)} %get-tuple-element.216.upg), custom_call_target="tpu_custom_call" | custom-call | flops 4294967296 | bytes 14680064 | tf_op jit(solution)/shard_map/up_weight_grad/pallas_call | solution.py:842
  223.4 6.6 %down_weight_send.1 = (bf16[2,1024,1024]{2,1,0:T(8,128)(2,1)S(1)}, f32[512,1024]{1,0:T(8,128)S(1)}) custom-call(bf16[512,1024]{1,0:T(8,128)(2,1)S(1)} %bitcast.68, bf16[512,4096]{1,0:T(8,128)(2,1)} %get-tuple-element.219.act, bf16[1024,1024]{1,0:T(8,128)(2,1)S(1)} %copy-done.56, bf16[1024,1024]{1,0:T(8,128)(2,1)S(1)} %copy-done.58), custom_call_target="tpu_custom_call" | custom-call | flops 4294967296 | bytes 14680064 | tf_op jit(solution)/shard_map/down_weight_send/pallas_call | solution.py:816
  232.2 5.4 collective-permute-done.30.refs_5_
  237.6 7.5 %collective-permute-done.27 = bf16[8,4096]{1,0:T(8,128)(2,1)S(1)} collective-permute-done((bf16[8,4096]{1,0:T(8,128)(2,1)S(1)}, bf16[8,4096]{1,0:T(8,128)(2,1)S(1)}, u32[]{:S(2)}, u32[]{:S(2)}) %collective-permute-start.27) | collective-permute-done | bytes 65568 | tf_op jit(solution)/shard_map/ppermute | solution.py:27
  249.6 4.6 collective-permute-start.33
  254.2 8.4 %down_weight_keep.1 = (bf16[2,1024,1024]{2,1,0:T(8,128)(2,1)}, bf16[8,64,1024]{2,1,0:T(8,128)(2,1)}, f32[8,1024]{1,0:T(8,128)S(1)}) custom-call(bf16[512,1024]{1,0:T(8,128)(2,1)S(1)} %bitcast.69, bf16[512,4096]{1,0:T(8,128)(2,1)} %get-tuple-element.219.act, bf16[1024,1024]{1,0:T(8,128)(2,1)S(1)} %copy-done.52, bf16[1024,1024]{1,0:T(8,128)(2,1)S(1)} %copy-done.54, ...), custom_call_target="tpu_custom_call" | custom-call | flops 4294967296 | bytes 14680064 | tf_op jit(solution)/shard_map/down_weight_keep/pallas_call | solution.py:816
  266.7 19.5 %attend_back_prev.1 = (f32[8,256,256]{2,1,0:T(8,128)}, bf16[2,7,256,256]{3,2,1,0:T(8,128)(2,1)}) custom-call(s32[8]{0:T(128)} %refs_0_.3, bf16[8,256,256]{2,1,0:T(8,128)(2,1)} %copy-done.17, bf16[7,256,256]{2,1,0:T(8,128)(2,1)} %copy-done.83, bf16[7,256,256]{2,1,0:T(8,128)(2,1)} %copy-done.84, bf16[8,64,256]{2,1,0:T(8,128)(2,1)} %copy-done.34, ...), custom_call_target="tpu_custom_call" | custom-call | flops 8053063680 | bytes 12582912 | tf_op jit(solution)/shard_map/attend_back_prev/pallas_call | solution.py:548
  286.2 12.0 %core_sum.1 = bf16[2,2304,1024]{2,1,0:T(8,128)(2,1)} custom-call(bf16[2,4,256,1024]{3,2,1,0:T(8,128)(2,1)} %get-tuple-element.252.ua, bf16[2,4,256,1024]{3,2,1,0:T(8,128)(2,1)} %copy-done.85, bf16[2,1024,1024]{2,1,0:T(8,128)(2,1)} %get-tuple-element.254.da, bf16[2,1024,1024]{2,1,0:T(8,128)(2,1)} %collective-permute-done.34.db, ...), custom_call_target="tpu_custom_call" | custom-call | flops 1000 | bytes 1000 | tf_op jit(solution)/shard_map/core_sum/pallas_call | solution.py:902
  298.5 32.1 %attend_back_own.1 = (bf16[8,256,256]{2,1,0:T(8,128)(2,1)}, f32[8,256,256]{2,1,0:T(8,128)}, f32[8,256,256]{2,1,0:T(8,128)}) custom-call(s32[8]{0:T(128)} %refs_0_.3, bf16[8,256,256]{2,1,0:T(8,128)(2,1)} %copy-done.17, bf16[8,256,256]{2,1,0:T(8,128)(2,1)} %copy-done.18, bf16[8,256,256]{2,1,0:T(8,128)(2,1)} %copy-done.19, bf16[8,64,256]{2,1,0:T(8,128)(2,1)} %copy-done.34, ...), custom_call_target="tpu_custom_call" | custom-call | flops 1000 | bytes 1000 | tf_op jit(solution)/shard_map/attend_back_own/pallas_call | solution.py:548
  331.4 18.8 %collective-permute-done.37.rk.rv = bf16[2,7,256,256]{3,2,1,0:T(8,128)(2,1)S(1)} collective-permute-done((bf16[2,7,256,256]{3,2,1,0:T(8,128)(2,1)}, bf16[2,7,256,256]{3,2,1,0:T(8,128)(2,1)S(1)}, u32[]{:S(2)}, u32[]{:S(2)}) %collective-permute-start.37) | collective-permute-done | bytes 1835040 | tf_op jit(solution)/shard_map/ppermute | solution.py:31
  354.8 7.5 %project_back.1 = (bf16[8,256,768]{2,1,0:T(8,128)(2,1)S(1)}, bf16[8,64,1024]{2,1,0:T(8,128)(2,1)S(1)}, bf16[8,64,1024]{2,1,0:T(8,128)(2,1)S(1)}, bf16[2,8,64,1024]{3,2,1,0:T(8,128)(2,1)S(1)}, f32[8,512]{1,0:T(8,128)S(1)}) custom-call(s32[1]{0:T(128)} %bitcast.row_ref.refs_0_, bf16[8,256,256]{2,1,0:T(8,128)(2,1)S(1)} %copy-done.66, ...), custom_call_target="tpu_custom_call" | custom-call | flops 3221225472 | bytes 14680064 | tf_op jit(solution)/shard_map/project_back/pallas_call | solution.py:1055
  376.6 4.8 project_weight.1
  381.3 8.5 %collective-permute-done.40.refs_3_ = bf16[8,8,4096]{2,1,0:T(8,128)(2,1)} collective-permute-done((bf16[8,8,4096]{2,1,0:T(8,128)(2,1)}, bf16[8,8,4096]{2,1,0:T(8,128)(2,1)}, u32[]{:S(2)}, u32[]{:S(2)}) %collective-permute-start.40) | collective-permute-done | bytes 524320 | tf_op jit(solution)/shard_map/ppermute | solution.py:27
  389.9 17.4 %collective-permute-done.41.refs_4_ = bf16[8,8,4096]{2,1,0:T(8,128)(2,1)} collective-permute-done((bf16[8,8,4096]{2,1,0:T(8,128)(2,1)}, bf16[8,8,4096]{2,1,0:T(8,128)(2,1)}, u32[]{:S(2)}, u32[]{:S(2)}) %collective-permute-start.41) | collective-permute-done | bytes 524320 | tf_op jit(solution)/shard_map/ppermute | solution.py:27
  416.0 4.2 input_back.1
  420.3 3.9 collective-permute-done.43
  424.1 7.6 %collective-permute-done.44 = bf16[4,64,768]{2,1,0:T(8,128)(2,1)} collective-permute-done((bf16[4,64,768]{2,1,0:T(8,128)(2,1)}, bf16[4,64,768]{2,1,0:T(8,128)(2,1)}, u32[]{:S(2)}, u32[]{:S(2)}) %collective-permute-start.44) | collective-permute-done | bytes 393248 | tf_op jit(solution)/shard_map/ppermute | solution.py:27
  442.5 5.2 collective-permute-done.48
  460.2 4.6 collective-permute-done.58
  469.5 7.1 %collective-permute-done.60.far = bf16[8,3584]{1,0:T(8,128)(2,1)S(1)} collective-permute-done((bf16[8,3584]{1,0:T(8,128)(2,1)S(1)}, bf16[8,3584]{1,0:T(8,128)(2,1)S(1)}, u32[]{:S(2)}, u32[]{:S(2)}) %collective-permute-start.60) | collective-permute-done | bytes 57376 | tf_op jit(solution)/shard_map/ppermute | solution.py:27
  493.3 10.7 %collective-permute-done.66 = bf16[4,16,3072]{2,1,0:T(8,128)(2,1)S(1)} collective-permute-done((bf16[4,16,3072]{2,1,0:T(8,128)(2,1)S(1)}, bf16[4,16,3072]{2,1,0:T(8,128)(2,1)S(1)}, u32[]{:S(2)}, u32[]{:S(2)}) %collective-permute-start.66) | collective-permute-done | bytes 393248 | tf_op jit(solution)/shard_map/ppermute | solution.py:27
  510.5 26.4 %collective-permute-done.67.high = bf16[2,4,16,3072]{3,2,1,0:T(8,128)(2,1)S(1)} collective-permute-done((bf16[2,4,16,3072]{3,2,1,0:T(8,128)(2,1)S(1)}, bf16[2,4,16,3072]{3,2,1,0:T(8,128)(2,1)S(1)}, u32[]{:S(2)}, u32[]{:S(2)}) %collective-permute-start.67) | collective-permute-done | bytes 786464 | tf_op jit(solution)/shard_map/ppermute | solution.py:27
  543.0 7.7 %final_sums.1 = (f32[256,6144]{1,0:T(8,128)}, f32[1,1536]{1,0:T(1,128)S(1)}, f32[1,768]{1,0:T(1,128)S(1)}, f32[1,256]{1,0:T(1,128)}, f32[1,1024]{1,0:T(1,128)}, /*index=5*/f32[1,256]{1,0:T(1,128)}) custom-call(s32[1]{0:T(128)} %bitcast.row_ref.refs_0_, bf16[2,4,16,3584]{3,2,1,0:T(8,128)(2,1)S(1)} %pad_maximum_fusion.refs_0_, ...), custom_call_target="tpu_custom_call" | custom-call | flops 805306368 | bytes 10485760 | tf_op jit(solution)/shard_map/final_sums/pallas_call | solution.py:1204
  (372 shorter events, 164.3 us)
Async XLA Ops:
  7.2 446.7 %reduce-scatter.2.cloned.1.call-start = ((), (), s32[]{:S(2)}) async-start(), calls=%async_computation.1 | async-start | bytes 10027008 | tf_op jit(solution)/shard_map/reduce_scatter | solution.py:1365
  7.2 51.8 %collective-permute-start = (bf16[8,64,1024]{2,1,0:T(8,128)(2,1)}, bf16[8,64,1024]{2,1,0:T(8,128)(2,1)}, u32[]{:S(2)}, u32[]{:S(2)}) collective-permute-start(bf16[8,64,1024]{2,1,0:T(8,128)(2,1)} %x.3), channel_id=1, source_target_pairs={{0,2},{1,3},{2,0},{3,1},{4,6},{5,7},{6,4},{7,5},{8,10},{9,11},{10,... | collective-permute-start | bytes 3145736 | tf_op jit(solution)/shard_map/ppermute | solution.py:27
  10.4 48.7 %collective-permute-start.1 = (bf16[7,64,1024]{2,1,0:T(8,128)(2,1)}, bf16[7,64,1024]{2,1,0:T(8,128)(2,1)S(1)}, u32[]{:S(2)}, u32[]{:S(2)}) collective-permute-start(bf16[7,64,1024]{2,1,0:T(8,128)(2,1)} %slice.63), channel_id=1, source_target_pairs={{0,4},{1,5},{2,6},{3,7},{4,8},{5,9},{6,10},{7,11},{8,12},{9,13},{1... | collective-permute-start | bytes 2752520 | tf_op jit(solution)/shard_map/ppermute | solution.py:31
  12.6 25.0 %collective-permute-start.5 = (bf16[2,256,768]{2,1,0:T(8,128)(2,1)S(1)}, bf16[2,256,768]{2,1,0:T(8,128)(2,1)S(1)}, u32[]{:S(2)}, u32[]{:S(2)}) collective-permute-start(bf16[2,256,768]{2,1,0:T(8,128)(2,1)S(1)} %get-tuple-element.172), channel_id=1, source_target_pairs={{0,66},{1,67},{2,64},{3,65},{4,70},{5,71},{6,68},{7,69},{8,74},{9,... | collective-permute-start | bytes 2359304 | tf_op jit(solution)/shard_map/ppermute | solution.py:27
  16.5 21.1 %collective-permute-start.4 = (bf16[256,768]{1,0:T(8,128)(2,1)S(1)}, bf16[256,768]{1,0:T(8,128)(2,1)S(1)}, u32[]{:S(2)}, u32[]{:S(2)}) collective-permute-start(bf16[256,768]{1,0:T(8,128)(2,1)S(1)} %get-tuple-element.171), channel_id=1, source_target_pairs={{0,1},{1,0},{2,3},{3,2},{4,5},{5,4},{6,7},{7,6},{8,9},{9,8},{10,11... | collective-permute-start | bytes 1179656 | tf_op jit(solution)/shard_map/ppermute | solution.py:27
  18.0 19.5 %collective-permute-start.3 = (f32[8,7424]{1,0:T(8,128)S(1)}, f32[8,7424]{1,0:T(8,128)S(1)}, u32[]{:S(2)}, u32[]{:S(2)}) collective-permute-start(f32[8,7424]{1,0:T(8,128)S(1)} %add.88), channel_id=1, source_target_pairs={{0,2},{1,3},{2,0},{3,1},{4,6},{5,7},{6,4},{7,5},{8,10},{9,11},{10,... | collective-permute-start | bytes 712712 | tf_op jit(solution)/shard_map/ppermute | solution.py:27
  37.5 25.5 %collective-permute-start.7 = (bf16[8,64,1024]{2,1,0:T(8,128)(2,1)S(1)}, bf16[8,64,1024]{2,1,0:T(8,128)(2,1)S(1)}, u32[]{:S(2)}, u32[]{:S(2)}) collective-permute-start(bf16[8,64,1024]{2,1,0:T(8,128)(2,1)S(1)} %copy-done.3), channel_id=1, source_target_pairs={{0,1},{1,0},{2,3},{3,2},{4,5},{5,4},{6,7},{7,6},{8,9},{9,8},{10,11... | collective-permute-start | bytes 3145736 | tf_op jit(solution)/shard_map/ppermute | solution.py:27
  60.0 16.3 %collective-permute-start.6 = (bf16[256,1024]{1,0:T(8,128)(2,1)S(1)}, bf16[256,1024]{1,0:T(8,128)(2,1)S(1)}, u32[]{:S(2)}, u32[]{:S(2)}) collective-permute-start(bf16[256,1024]{1,0:T(8,128)(2,1)S(1)} %copy-done.13), channel_id=1, source_target_pairs={{0,66},{1,67},{2,64},{3,65},{4,70},{5,71},{6,68},{7,69},{8,74},{9,... | collective-permute-start | bytes 1572872 | tf_op jit(solution)/shard_map/ppermute | solution.py:27
  62.8 37.3 %collective-permute-start.10 = (bf16[7,64,1024]{2,1,0:T(8,128)(2,1)}, bf16[7,64,1024]{2,1,0:T(8,128)(2,1)S(1)}, u32[]{:S(2)}, u32[]{:S(2)}) collective-permute-start(bf16[7,64,1024]{2,1,0:T(8,128)(2,1)} %copy-done.67), channel_id=1, source_target_pairs={{0,1},{1,0},{2,3},{3,2},{4,5},{5,4},{6,7},{7,6},{8,9},{9,8},{10,11... | collective-permute-start | bytes 2752520 | tf_op jit(solution)/shard_map/ppermute | solution.py:27
  63.0 36.4 %collective-permute-start.11 = (bf16[7,64,1024]{2,1,0:T(8,128)(2,1)}, bf16[7,64,1024]{2,1,0:T(8,128)(2,1)S(1)}, u32[]{:S(2)}, u32[]{:S(2)}) collective-permute-start(bf16[7,64,1024]{2,1,0:T(8,128)(2,1)} %copy-done.67), channel_id=1, source_target_pairs={{0,2},{1,3},{2,0},{3,1},{4,6},{5,7},{6,4},{7,5},{8,10},{9,11},{10,... | collective-permute-start | bytes 2752520 | tf_op jit(solution)/shard_map/ppermute | solution.py:27
  63.0 36.4 %collective-permute-start.12 = (f32[8,2048]{1,0:T(8,128)S(1)}, f32[8,2048]{1,0:T(8,128)S(1)}, u32[]{:S(2)}, u32[]{:S(2)}) collective-permute-start(f32[8,2048]{1,0:T(8,128)S(1)} %slice.66), channel_id=1, source_target_pairs={{0,4},{1,5},{2,6},{3,7},{4,8},{5,9},{6,10},{7,11},{8,12},{9,13},{1... | collective-permute-start | bytes 196616 | tf_op jit(solution)/shard_map/ppermute | solution.py:31
  76.3 55.7 %collective-permute-start.18 = (bf16[256,4096]{1,0:T(8,128)(2,1)S(1)}, bf16[256,4096]{1,0:T(8,128)(2,1)}, u32[]{:S(2)}, u32[]{:S(2)}) collective-permute-start(bf16[256,4096]{1,0:T(8,128)(2,1)S(1)} %copy-done.93), channel_id=1, source_target_pairs={{0,66},{1,67},{2,64},{3,65},{4,70},{5,71},{6,68},{7,69},{8,74},{9,... | collective-permute-start | bytes 6291464 | tf_op jit(solution)/shard_map/ppermute | solution.py:27
  79.0 53.1 %collective-permute-start.19 = (bf16[1024,1024]{1,0:T(8,128)(2,1)S(1)}, bf16[1024,1024]{1,0:T(8,128)(2,1)S(1)}, u32[]{:S(2)}, u32[]{:S(2)}) collective-permute-start(bf16[1024,1024]{1,0:T(8,128)(2,1)S(1)} %copy-done.51), channel_id=1, source_target_pairs={{0,2},{1,3},{2,0},{3,1},{4,6},{5,7},{6,4},{7,5},{8,10},{9,11},{10,... | collective-permute-start | bytes 6291464 | tf_op jit(solution)/shard_map/ppermute | solution.py:27
  99.5 33.1 %collective-permute-start.17 = (bf16[256,1024]{1,0:T(8,128)(2,1)S(1)}, bf16[256,1024]{1,0:T(8,128)(2,1)S(1)}, u32[]{:S(2)}, u32[]{:S(2)}) collective-permute-start(bf16[256,1024]{1,0:T(8,128)(2,1)S(1)} %copy-done.13), channel_id=1, source_target_pairs={{0,1},{1,0},{2,3},{3,2},{4,5},{5,4},{6,7},{7,6},{8,9},{9,8},{10,11... | collective-permute-start | bytes 1572872 | tf_op jit(solution)/shard_map/ppermute | solution.py:27
  100.0 58.3 %collective-permute-start.21 = (bf16[256,4096]{1,0:T(8,128)(2,1)S(1)}, bf16[256,4096]{1,0:T(8,128)(2,1)}, u32[]{:S(2)}, u32[]{:S(2)}) collective-permute-start(bf16[256,4096]{1,0:T(8,128)(2,1)S(1)} %copy-done.93), channel_id=1, source_target_pairs={{0,1},{1,0},{2,3},{3,2},{4,5},{5,4},{6,7},{7,6},{8,9},{9,8},{10,11... | collective-permute-start | bytes 6291464 | tf_op jit(solution)/shard_map/ppermute | solution.py:27
  102.0 56.3 %collective-permute-start.23 = (bf16[1024,1024]{1,0:T(8,128)(2,1)S(1)}, bf16[1024,1024]{1,0:T(8,128)(2,1)S(1)}, u32[]{:S(2)}, u32[]{:S(2)}) collective-permute-start(bf16[1024,1024]{1,0:T(8,128)(2,1)S(1)} %copy-done.51), channel_id=1, source_target_pairs={{0,1},{1,0},{2,3},{3,2},{4,5},{5,4},{6,7},{7,6},{8,9},{9,8},{10,11... | collective-permute-start | bytes 6291464 | tf_op jit(solution)/shard_map/ppermute | solution.py:27
  132.0 26.3 %collective-permute-start.22 = (bf16[256,4096]{1,0:T(8,128)(2,1)}, bf16[256,4096]{1,0:T(8,128)(2,1)S(1)}, u32[]{:S(2)}, u32[]{:S(2)}) collective-permute-start(bf16[256,4096]{1,0:T(8,128)(2,1)} %collective-permute-done.18.u2), channel_id=1, source_target_pairs={{0,1},{1,0},{2,3},{3,2},{4,5},{5,4},{6,7},{7,6},{8,9},{9,8},{10,11... | collective-permute-start | bytes 6291464 | tf_op jit(solution)/shard_map/ppermute | solution.py:27
  132.5 25.8 %collective-permute-start.24 = (bf16[1024,1024]{1,0:T(8,128)(2,1)S(1)}, bf16[1024,1024]{1,0:T(8,128)(2,1)S(1)}, u32[]{:S(2)}, u32[]{:S(2)}) collective-permute-start(bf16[1024,1024]{1,0:T(8,128)(2,1)S(1)} %collective-permute-done.19.d2.db), channel_id=1, source_target_pairs={{0,1},{1,0},{2,3},{3,2},{4,5},{5,4},{6,7},{7,6},{8,9},{9,8},{10,11... | collective-permute-start | bytes 6291464 | tf_op jit(solution)/shard_map/ppermute | solution.py:27
  212.6 32.5 %collective-permute-start.28 = (bf16[2,4,256,1024]{3,2,1,0:T(8,128)(2,1)}, bf16[2,4,256,1024]{3,2,1,0:T(8,128)(2,1)S(1)}, u32[]{:S(2)}, u32[]{:S(2)}) collective-permute-start(bf16[2,4,256,1024]{3,2,1,0:T(8,128)(2,1)} %get-tuple-element.223), channel_id=1, source_target_pairs={{0,1},{1,0},{2,3},{3,2},{4,5},{5,4},{6,7},{7,6},{8,9},{9,8},{10,11... | collective-permute-start | bytes 12582920 | tf_op jit(solution)/shard_map/ppermute | solution.py:27
  230.0 32.6 %collective-permute-start.34 = (bf16[2,1024,1024]{2,1,0:T(8,128)(2,1)S(1)}, bf16[2,1024,1024]{2,1,0:T(8,128)(2,1)}, u32[]{:S(2)}, u32[]{:S(2)}) collective-permute-start(bf16[2,1024,1024]{2,1,0:T(8,128)(2,1)S(1)} %get-tuple-element.232), channel_id=1, source_target_pairs={{0,1},{1,0},{2,3},{3,2},{4,5},{5,4},{6,7},{7,6},{8,9},{9,8},{10,11... | collective-permute-start | bytes 12582920 | tf_op jit(solution)/shard_map/ppermute | solution.py:27
  298.2 253.6 %all-gather.2.cloned.1.call-start = ((), (), s32[]{:S(2)}) async-start(), calls=%async_computation.2 | async-start | bytes 5013504 | tf_op jit(solution)/shard_map/all_gather | solution.py:1408
  298.4 51.8 %collective-permute-start.37 = (bf16[2,7,256,256]{3,2,1,0:T(8,128)(2,1)}, bf16[2,7,256,256]{3,2,1,0:T(8,128)(2,1)S(1)}, u32[]{:S(2)}, u32[]{:S(2)}) collective-permute-start(bf16[2,7,256,256]{3,2,1,0:T(8,128)(2,1)} %get-tuple-element.268), channel_id=1, source_target_pairs={{0,124},{1,125},{2,126},{3,127},{4,0},{5,1},{6,2},{7,3},{8,4},{9,5... | collective-permute-start | bytes 5505032 | tf_op jit(solution)/shard_map/ppermute | solution.py:31
  364.0 25.9 %collective-permute-start.40 = (bf16[8,8,4096]{2,1,0:T(8,128)(2,1)}, bf16[8,8,4096]{2,1,0:T(8,128)(2,1)}, u32[]{:S(2)}, u32[]{:S(2)}) collective-permute-start(bf16[8,8,4096]{2,1,0:T(8,128)(2,1)} %join.1.refs_2_), channel_id=1, source_target_pairs={{0,4},{1,5},{2,6},{3,7},{4,0},{5,1},{6,2},{7,3},{8,12},{9,13},{10,... | collective-permute-start | bytes 1572872 | tf_op jit(solution)/shard_map/ppermute | solution.py:27
  364.1 43.2 %collective-permute-start.41 = (bf16[8,8,4096]{2,1,0:T(8,128)(2,1)}, bf16[8,8,4096]{2,1,0:T(8,128)(2,1)}, u32[]{:S(2)}, u32[]{:S(2)}) collective-permute-start(bf16[8,8,4096]{2,1,0:T(8,128)(2,1)} %join.1.refs_2_), channel_id=1, source_target_pairs={{0,8},{1,9},{2,10},{3,11},{4,12},{5,13},{6,14},{7,15},{8,0},{9,1},... | collective-permute-start | bytes 1572872 | tf_op jit(solution)/shard_map/ppermute | solution.py:27
  366.9 40.5 %collective-permute-start.42 = (bf16[8,8,4096]{2,1,0:T(8,128)(2,1)}, bf16[8,8,4096]{2,1,0:T(8,128)(2,1)}, u32[]{:S(2)}, u32[]{:S(2)}) collective-permute-start(bf16[8,8,4096]{2,1,0:T(8,128)(2,1)} %join.1.refs_2_), channel_id=1, source_target_pairs={{0,12},{1,13},{2,14},{3,15},{4,8},{5,9},{6,10},{7,11},{8,4},{9,5},... | collective-permute-start | bytes 1572872 | tf_op jit(solution)/shard_map/ppermute | solution.py:27
  370.2 43.0 %collective-permute-start.39 = (bf16[8,64,1024]{2,1,0:T(8,128)(2,1)}, bf16[8,64,1024]{2,1,0:T(8,128)(2,1)}, u32[]{:S(2)}, u32[]{:S(2)}) collective-permute-start(bf16[8,64,1024]{2,1,0:T(8,128)(2,1)} %fusion), channel_id=1, source_target_pairs={{0,2},{1,3},{2,0},{3,1},{4,6},{5,7},{6,4},{7,5},{8,10},{9,11},{10,... | collective-permute-start | bytes 3145736 | tf_op jit(solution)/shard_map/ppermute | solution.py:27
  408.5 15.6 %collective-permute-start.43 = (bf16[4,64,768]{2,1,0:T(8,128)(2,1)}, bf16[4,64,768]{2,1,0:T(8,128)(2,1)}, u32[]{:S(2)}, u32[]{:S(2)}) collective-permute-start(bf16[4,64,768]{2,1,0:T(8,128)(2,1)} %get-tuple-element.323), channel_id=1, source_target_pairs={{0,4},{1,5},{2,6},{3,7},{4,0},{5,1},{6,2},{7,3},{8,12},{9,13},{10,... | collective-permute-start | bytes 1179656 | tf_op jit(solution)/shard_map/ppermute | solution.py:27
  409.6 22.2 %collective-permute-start.44 = (bf16[4,64,768]{2,1,0:T(8,128)(2,1)}, bf16[4,64,768]{2,1,0:T(8,128)(2,1)}, u32[]{:S(2)}, u32[]{:S(2)}) collective-permute-start(bf16[4,64,768]{2,1,0:T(8,128)(2,1)} %get-tuple-element.322), channel_id=1, source_target_pairs={{0,8},{1,9},{2,10},{3,11},{4,12},{5,13},{6,14},{7,15},{8,0},{9,1},... | collective-permute-start | bytes 1179656 | tf_op jit(solution)/shard_map/ppermute | solution.py:27
  410.4 22.6 %collective-permute-start.45 = (bf16[4,64,768]{2,1,0:T(8,128)(2,1)}, bf16[4,64,768]{2,1,0:T(8,128)(2,1)}, u32[]{:S(2)}, u32[]{:S(2)}) collective-permute-start(bf16[4,64,768]{2,1,0:T(8,128)(2,1)} %get-tuple-element.321), channel_id=1, source_target_pairs={{0,12},{1,13},{2,14},{3,15},{4,8},{5,9},{6,10},{7,11},{8,4},{9,5},... | collective-permute-start | bytes 1179656 | tf_op jit(solution)/shard_map/ppermute | solution.py:27
  420.3 19.3 %collective-permute-start.46 = (f32[8,3584]{1,0:T(8,128)S(1)}, f32[8,3584]{1,0:T(8,128)S(1)}, u32[]{:S(2)}, u32[]{:S(2)}) collective-permute-start(f32[8,3584]{1,0:T(8,128)S(1)} %get-tuple-element.281), channel_id=1, source_target_pairs={{0,1},{1,0},{2,3},{3,2},{4,5},{5,4},{6,7},{7,6},{8,9},{9,8},{10,11... | collective-permute-start | bytes 344072 | tf_op jit(solution)/shard_map/ppermute | solution.py:27
  504.1 32.8 %collective-permute-start.67 = (bf16[2,4,16,3072]{3,2,1,0:T(8,128)(2,1)S(1)}, bf16[2,4,16,3072]{3,2,1,0:T(8,128)(2,1)S(1)}, u32[]{:S(2)}, u32[]{:S(2)}) collective-permute-start(bf16[2,4,16,3072]{3,2,1,0:T(8,128)(2,1)S(1)} %pad_maximum_fusion.1.low), channel_id=1, source_target_pairs={{0,12},{1,13},{2,14},{3,15},{4,8},{5,9},{6,10},{7,11},{8,4},{9,5},... | collective-permute-start | bytes 2359304 | tf_op jit(solution)/shard_map/ppermute | solution.py:27
  505.1 37.9 %collective-permute-start.65 = (bf16[2,4,16,3584]{3,2,1,0:T(8,128)(2,1)S(1)}, bf16[2,4,16,3584]{3,2,1,0:T(8,128)(2,1)S(1)}, u32[]{:S(2)}, u32[]{:S(2)}) collective-permute-start(bf16[2,4,16,3584]{3,2,1,0:T(8,128)(2,1)S(1)} %pad_maximum_fusion.refs_0_), channel_id=1, source_target_pairs={{0,4},{1,5},{2,6},{3,7},{4,0},{5,1},{6,2},{7,3},{8,12},{9,13},{10,... | collective-permute-start | bytes 2752520 | tf_op jit(solution)/shard_map/ppermute | solution.py:27
  (135 other events, 2157.7 us)
Sparse Core Ops, SparseCore 0:
  298.4 155.5 reduce-scatter.1
  477.5 67.1 all-gather.1
